TPU v7x, 32 devices: a whole 2x2x4 slice. The times are simulated.
32 devices in a mesh: groups: 2 (over x), row: 16 (over z, y, core).
Axes of the slice: x: 2, y: 2, z: 4, core: 2. Of those that a mesh axis runs over, the one named last changes fastest.
Arguments:
- three_center: bfloat16 [4096, 768], P(('groups', 'row')), parts along dimension 0, may hold values from -4 to 4
- tau_weights: float32 [1536], P('groups'), parts along dimension 0, may hold values from 0.02 to 1
- tile_mask: int32 [16, 6], P('row'), may hold values 0 or 1
- dest: int32 [16, 8], P('row'), may hold values from 0 to 15, all different within a row; in each aligned block of 1 rows (0 to 0, 1 to 1, ...) no two rows name the same one
- metric_half: bfloat16 [2048, 128], P('row'), may hold values from -0.375 to 0.375
Outputs:
- chi_mirror: bfloat16 [32, 8, 128, 128], P(('groups', 'row')), parts along dimension 0
- sandwich: float32 [256, 128], P(('groups', 'row')), parts along dimension 0
There are 2 independent parts, one for each index of `groups`. A program takes and returns all parts, laid end to end along the dimension named above; an argument that names none is the same for every part. Nothing has to cross between parts.
Inputs may be any that keep to these rules, and one draw needn't show every extreme that they name: `dest`: each row names 8 different devices; among the 1 block-rows of one device no device is named twice.
All inputs are finite; a program needn't handle non-finite values. No bound on the sum of `tile_mask` on one device may be relied on, other than what follows from the above.
Results may differ from a plain program's by a relative error of at most 0.0047.
Values may be sent and summed in bfloat16 or wider, within the bound.
No kernel may reach another device: no remote copies, remote signals or barrier semaphores. Data moves between devices by JAX's collectives and lax.ppermute only.
A program may use at most 64 MiB of HBM per device.

v0:
```python
import jax
import jax.numpy as jnp
from jax import lax
from jax.sharding import PartitionSpec as P

BLOCK = 128


def body(three_center, tau_weights, tile_mask, dest, metric_half):
    devices = lax.axis_size("row")
    local_rows, contracted = three_center.shape
    local_blocks = local_rows // BLOCK
    tiles = contracted // BLOCK
    window = metric_half.shape[1]
    fanout = dest.shape[1]
    masked = (
        three_center.reshape(local_blocks, BLOCK, tiles, BLOCK)
        * tile_mask.astype(jnp.bfloat16)[:, None, :, None]
    ).reshape(local_rows, contracted)
    scaled = (masked.astype(jnp.float32) * tau_weights[None, :]).astype(jnp.bfloat16)
    routed = jnp.any(
        dest[:, :, None] == jnp.arange(devices, dtype=jnp.int32)[None, None, :], axis=1
    )
    routed_bf = routed.astype(jnp.bfloat16)
    send_rows = jnp.einsum(
        "bd,brl->drl",
        routed_bf,
        masked.reshape(local_blocks, BLOCK, contracted),
        preferred_element_type=jnp.float32,
    ).astype(jnp.bfloat16)
    source_slot = jnp.sum(
        routed.astype(jnp.int32) * jnp.arange(local_blocks, dtype=jnp.int32)[:, None], axis=0
    )
    got_rows, got_slot = (
        lax.all_to_all(send_rows, "row", split_axis=0, concat_axis=0, tiled=True),
        lax.all_to_all(source_slot, "row", split_axis=0, concat_axis=0, tiled=True),
    )
    whole_metric = lax.all_gather(metric_half, "row", axis=0, tiled=True)
    source_block = jnp.arange(devices, dtype=jnp.int32) * local_blocks + got_slot
    metric_rows = jnp.take(whole_metric.reshape(-1, BLOCK, window), source_block, axis=0)
    strips = jnp.einsum("drl,pl->drp", got_rows, scaled, preferred_element_type=jnp.float32).astype(
        jnp.bfloat16
    )
    product = jnp.einsum(
        "drp,drc->pc", strips, metric_rows, preferred_element_type=jnp.float32
    ).astype(jnp.bfloat16)
    returned = lax.all_to_all(strips, "row", split_axis=0, concat_axis=0, tiled=True)
    chi_mirror = jnp.take(returned, dest.reshape(-1), axis=0).reshape(
        local_blocks, fanout, BLOCK, local_rows
    )
    partial_value = jnp.einsum(
        "rc,rk->ck", metric_half, product, preferred_element_type=jnp.float32
    )
    combined = partial_value + partial_value.T
    sandwich = lax.psum_scatter(combined, "row", scatter_dimension=0, tiled=True)
    return (chi_mirror, sandwich)


def solution(mesh):
    return jax.shard_map(
        body,
        mesh=mesh,
        in_specs=(
            P(("groups", "row"), None),
            P("groups"),
            P("row", None),
            P("row", None),
            P("row", None),
        ),
        out_specs=(P(("groups", "row"), None, None, None), P(("groups", "row"), None)),
        check_vma=False,
    )
```

profile of v0, /device:TPU:0, one launch (start us, length us, event | category | flops | bytes accessed | tf_op | source)
XLA Modules:
  0.0 209.2 jit_solution(8501075301188058694)
XLA Ops:
  7.2 0.7 convert_bitcast_fusion
  7.8 0.1 broadcast_bitcast_fusion
  7.9 0.7 fusion.11
  8.6 1.0 multiply_convert_fusion.2
  9.6 2.4 %multiply_convert_fusion = bf16[16,128,768]{2,1,0:T(8,128)(2,1)} fusion(f32[128,768]{1,0:T(8,128)S(1)} %multiply_convert_fusion.2, f32[16]{0:T(128)S(1)} %convert.6), kind=kLoop, calls=%fused_computation.2 | loop fusion | flops 3145728 | bytes 3539008 | tf_op jit(solution)/shard_map/convert_element_type | solution.py:30
  12.0 0.0 copy-start.3
  12.0 0.0 copy-start.1
  12.0 0.0 copy-start
  12.0 0.0 copy-start.2
  12.0 7.5 %all-to-all-start = ((bf16[16,128,768]{2,1,0:T(8,128)(2,1)}), bf16[16,128,768]{2,1,0:T(8,128)(2,1)S(1)}, u32[]{:S(2)}, u32[]{:S(2)}) async-start(bf16[16,128,768]{2,1,0:T(8,128)(2,1)} %multiply_convert_fusion), calls=%async_computation | async-start | bytes 6291456 | tf_op jit(solution)/shard_map/all_to_all | solution.py:35
  19.6 0.0 copy-done.3
  19.6 0.0 copy-done.1
  19.6 79.9 %all_gather.3 = bf16[2048,128]{1,0:T(8,128)(2,1)} all-gather(bf16[128,128]{1,0:T(8,128)(2,1)S(1)} %copy-done.1), channel_id=1, replica_groups=mesh['groups'=2,'row'=16] {'row'}, dimensions={0}, use_global_device_ids=true | all-gather | bytes 557056 | tf_op jit(solution)/shard_map/all_gather | solution.py:38
  99.5 0.0 copy-start.4
  99.5 0.0 all-to-all-done
  99.5 0.0 copy-done
  99.5 0.0 copy-done.2
  99.5 1.8 convolution_convert_fusion
  101.3 7.6 %all-to-all-start.1 = ((bf16[16,128,128]{2,1,0:T(8,128)(2,1)}), bf16[16,128,128]{2,1,0:T(8,128)(2,1)S(1)}, u32[]{:S(2)}, u32[]{:S(2)}) async-start(bf16[16,128,128]{2,1,0:T(8,128)(2,1)} %convolution_convert_fusion), calls=%async_computation.1 | async-start | bytes 1048576 | tf_op jit(solution)/shard_map/all_to_all | solution.py:47
  108.9 0.0 all-reduce.3.cloned.1.call-start
  109.0 1.7 gather_fusion.1
  110.7 1.6 fusion.1
  112.3 0.1 copy.10
  112.4 0.6 bitcast_add_fusion
  113.1 0.0 all-reduce.3.cloned.1.call-update
  113.1 0.0 copy-done.4
  113.1 0.6 dynamic-slice
  114.4 85.3 %all-reduce.3.cloned.1.call-done = f32[128,128]{1,0:T(8,128)} async-done(((f32[128,128]{1,0:T(8,128)}), f32[128,128]{1,0:T(8,128)}) %all-reduce.3.cloned.1.call-update) | async-done | bytes 65552
  199.7 1.3 constant_dynamic-slice_fusion
  200.9 0.0 all-to-all-done.1
  200.9 0.6 gather_fusion
  201.5 0.8 bitcast_select_fusion
  (7 shorter events, 0.0 us)
Async XLA Ops:
  12.0 7.6 %copy-start.3 = (s32[1,8]{1,0:T(1,128)S(1)}, s32[1,8]{1,0:T(1,128)}, u32[]{:S(2)}) copy-start(s32[1,8]{1,0:T(1,128)} %param.8) | copy-start | bytes 100
  12.0 7.6 %copy-start.1 = (bf16[128,128]{1,0:T(8,128)(2,1)S(1)}, bf16[128,128]{1,0:T(8,128)(2,1)}, u32[]{:S(2)}) copy-start(bf16[128,128]{1,0:T(8,128)(2,1)} %param.9) | copy-start | bytes 98308
  12.0 87.5 %copy-start = (bf16[128,768]{1,0:T(8,128)(2,1)S(1)}, bf16[128,768]{1,0:T(8,128)(2,1)}, u32[]{:S(2)}) copy-start(bf16[128,768]{1,0:T(8,128)(2,1)} %param.5) | copy-start | bytes 589828
  12.0 87.5 %copy-start.2 = (f32[768]{0:T(1024)S(1)}, f32[768]{0:T(1024)}, u32[]{:S(2)}) copy-start(f32[768]{0:T(1024)} %param.6) | copy-start | bytes 9220
  12.0 87.5 %all-to-all-start = ((bf16[16,128,768]{2,1,0:T(8,128)(2,1)}), bf16[16,128,768]{2,1,0:T(8,128)(2,1)S(1)}, u32[]{:S(2)}, u32[]{:S(2)}) async-start(bf16[16,128,768]{2,1,0:T(8,128)(2,1)} %multiply_convert_fusion), calls=%async_computation | async-start | bytes 6291456 | tf_op jit(solution)/shard_map/all_to_all | solution.py:35
  99.5 13.6 %copy-start.4 = (u32[32]{0:T(128)S(1)}, u32[32]{0:T(128)}, u32[]{:S(2)}) copy-start(u32[32]{0:T(128)} %constant.39) | copy-start | bytes 388
  101.3 99.6 %all-to-all-start.1 = ((bf16[16,128,128]{2,1,0:T(8,128)(2,1)}), bf16[16,128,128]{2,1,0:T(8,128)(2,1)S(1)}, u32[]{:S(2)}, u32[]{:S(2)}) async-start(bf16[16,128,128]{2,1,0:T(8,128)(2,1)} %convolution_convert_fusion), calls=%async_computation.1 | async-start | bytes 1048576 | tf_op jit(solution)/shard_map/all_to_all | solution.py:47
  108.9 90.7 %all-reduce.3.cloned.1.call-start = ((), (), s32[]{:S(2)}) async-start(), calls=%async_computation.2 | async-start | bytes 131072
Sparse Core Ops, SparseCore 0:
  113.8 85.8 all-reduce.2
where the time goes:
time: 211 us; the launch traced here: 209 us
  waiting for transfers between devices  85.3 us (40%)
  blocking collectives  79.9 us (38%)
  starting transfers between devices  15.2 us (7%)
  between operations  14.8 us (7%)
  other arithmetic  6.26 us (3%)
  local copies, waits for them, and re-layouts  4.32 us (2%)
  matrix products  3.42 us (2%)
    unnamed x2, waiting for transfers between devices  85.3 us
    all_gather x1, blocking collectives, body(): whole_metric = lax.all_gather(metric_half, 'row', axis=0, tiled=True)  79.9 us
    all_to_all x1, starting transfers between devices, body(): lax.all_to_all(strips, 'row', split_axis=0, concat_axis=0, tiled=True)  7.61 us
    all_to_all x1, starting transfers between devices, body(): lax.all_to_all(send_rows, 'row', split_axis=0, concat_axis=0, tiled=True)  7.53 us
  transfers between devices with their start and end apart: 3, of which 1 were waited for; matrix products, arithmetic and copies ran while one was open for 3% of the time, Pallas kernels for 0%

commit v1 on v0

v1 whole, which is shorter than its diff:
```python
import functools

import jax
import jax.numpy as jnp
from jax import lax
from jax.experimental import pallas as pl
from jax.experimental.pallas import tpu as pltpu
from jax.sharding import PartitionSpec as P

BLOCK = 128
LIST_ROWS = 16
NT_DIMS = (((1,), (1,)), ((), ()))
NN_DIMS = (((1,), (0,)), ((), ()))
TN_DIMS = (((0,), (0,)), ((), ()))


def dot(a, b, dims=NN_DIMS):
    return lax.dot_general(a, b, dims, preferred_element_type=jnp.float32)


def split(x):
    high = x.astype(jnp.bfloat16)
    return high, (x - high.astype(jnp.float32)).astype(jnp.bfloat16)


def pack_kernel(tiles, fanout, mask_ref, dest_ref, rows_ref, tau_ref, metric_ref, out_ref):
    for t in range(tiles):
        cols = slice(t * BLOCK, (t + 1) * BLOCK)
        weight = tau_ref[:, cols] * mask_ref[0, t].astype(jnp.float32)
        out_ref[cols, :] = (rows_ref[:, cols].astype(jnp.float32) * weight).astype(jnp.bfloat16)
    out_ref[tiles * BLOCK : (tiles + 1) * BLOCK, :] = metric_ref[...]
    lane = lax.broadcasted_iota(jnp.int32, (LIST_ROWS, BLOCK), 1)
    listed = jnp.zeros((LIST_ROWS, BLOCK), jnp.float32)
    for j in range(fanout):
        listed += (lane == dest_ref[0, j]).astype(jnp.float32)
    out_ref[(tiles + 1) * BLOCK :, :] = listed.astype(jnp.bfloat16)


def block_kernel(devices, tiles, fanout, *refs):
    me_ref, mask_ref, dest_ref, rows_ref, tau_ref = refs[:5]
    pieces = refs[5 : 5 + devices]
    chi_ref, sand_ref, slot, listed, window = refs[5 + devices :]
    me = me_ref[0]
    window_rows = BLOCK // devices
    depth = tiles * BLOCK

    def init(e, _):
        slot[e] = -1
        return 0

    lax.fori_loop(0, devices, init, 0)
    for j in range(fanout):
        slot[dest_ref[0, j]] = j

    masked = jnp.concatenate(
        [
            rows_ref[:, t * BLOCK : (t + 1) * BLOCK] * mask_ref[0, t].astype(jnp.bfloat16)
            for t in range(tiles)
        ],
        axis=1,
    )

    def scaled_of(ref):
        return jnp.concatenate([ref[t * BLOCK : (t + 1) * BLOCK, :] for t in range(tiles)], axis=1)

    def metric_of(ref):
        return ref[depth : depth + BLOCK, :]

    lane = lax.broadcasted_iota(jnp.int32, (BLOCK, BLOCK), 0)
    column = lax.broadcasted_iota(jnp.int32, (BLOCK, BLOCK), 1)
    pick = (lane == column + me * window_rows).astype(jnp.bfloat16)[:, :window_rows]
    if devices < BLOCK:
        listed[devices:, :] = jnp.zeros((BLOCK - devices, BLOCK), jnp.float32)
    for m in range(devices):
        e = me ^ m
        scaled = scaled_of(pieces[m])
        own = dot(metric_of(pieces[m]), pick).astype(jnp.bfloat16)
        window[m * window_rows : (m + 1) * window_rows, :] = dot(own, scaled, TN_DIMS)
        listed[m : m + 1, :] = pieces[m][depth + BLOCK : depth + BLOCK + 1, :].astype(jnp.float32)
        j = slot[e]

        @pl.when(j >= 0)
        def _(scaled=scaled, j=j):
            chi_ref[0, j] = dot(masked, scaled, NT_DIMS).astype(jnp.bfloat16)

    by_piece = (lane == (column ^ me)).astype(jnp.bfloat16)
    routes = dot(listed[...].astype(jnp.bfloat16), by_piece)
    both = (routes + routes.T).astype(jnp.bfloat16)
    spread = (lane // window_rows == column).astype(jnp.bfloat16)
    pair = dot(dot(spread, both).astype(jnp.bfloat16), spread, NT_DIMS)
    pair = jnp.where(lane % window_rows == column % window_rows, pair, 0.0).astype(jnp.bfloat16)
    high, low = split(window[...])
    mixed = (dot(pair, high) + dot(pair, low)) / tau_ref[...]
    mixed_both = jnp.concatenate(split(mixed), axis=0)
    total = jnp.zeros((BLOCK, BLOCK), jnp.float32)
    for m in range(devices):
        both_parts = dot(scaled_of(pieces[m]), mixed_both, NT_DIMS)
        part = both_parts[:, :BLOCK] + both_parts[:, BLOCK:]
        part = jnp.where(column // window_rows == m, part, 0.0)
        high, low = split(part)
        total += dot(jnp.concatenate([high, low], axis=0), jnp.concatenate([metric_of(pieces[m])] * 2, axis=0), TN_DIMS)
    rows = [total[e * window_rows : (e + 1) * window_rows, :] for e in range(devices)]
    sand_ref[...] = functools.reduce(lambda a, b: a + b, rows)


def body(three_center, tau_weights, tile_mask, dest, metric_half):
    devices = lax.axis_size("row")
    contracted = three_center.shape[1]
    tiles = contracted // BLOCK
    fanout = dest.shape[1]
    window_rows = BLOCK // devices
    piece_rows = (tiles + 1) * BLOCK + LIST_ROWS
    smem = pl.BlockSpec(memory_space=pltpu.SMEM)
    vmem = pl.BlockSpec(memory_space=pltpu.VMEM)
    tau = tau_weights.reshape(1, contracted)
    own = pl.pallas_call(
        functools.partial(pack_kernel, tiles, fanout),
        out_shape=jax.ShapeDtypeStruct((piece_rows, BLOCK), jnp.bfloat16),
        in_specs=[smem, smem, vmem, vmem, vmem],
        out_specs=vmem,
        name="pack",
    )(tile_mask, dest, three_center, tau, metric_half)

    def swap(piece, mask):
        return lax.ppermute(piece, "row", [(i, i ^ mask) for i in range(devices)])

    pieces = {0: own}
    for mask in range(4, devices, 4):
        pieces[mask] = swap(own, mask)
    for mask in range(0, devices, 4):
        pieces[mask + 2] = swap(pieces[mask], 2)
    for mask in range(0, devices, 2):
        pieces[mask + 1] = swap(pieces[mask], 1)
    me = lax.axis_index("row").astype(jnp.int32).reshape(1)
    return pl.pallas_call(
        functools.partial(block_kernel, devices, tiles, fanout),
        out_shape=(
            jax.ShapeDtypeStruct((1, fanout, BLOCK, BLOCK), jnp.bfloat16),
            jax.ShapeDtypeStruct((window_rows, BLOCK), jnp.float32),
        ),
        in_specs=[smem, smem, smem, vmem, vmem] + [vmem] * devices,
        out_specs=(vmem, vmem),
        scratch_shapes=[
            pltpu.SMEM((devices,), jnp.int32),
            pltpu.VMEM((BLOCK, BLOCK), jnp.float32),
            pltpu.VMEM((BLOCK, contracted), jnp.float32),
        ],
        compiler_params=pltpu.CompilerParams(vmem_limit_bytes=40 * 1024 * 1024),
        name="blocks",
    )(me, tile_mask, dest, three_center, tau, *[pieces[m] for m in range(devices)])


def solution(mesh):
    return jax.shard_map(
        body,
        mesh=mesh,
        in_specs=(
            P(("groups", "row"), None),
            P("groups"),
            P("row", None),
            P("row", None),
            P("row", None),
        ),
        out_specs=(P(("groups", "row"), None, None, None), P(("groups", "row"), None)),
        check_vma=False,
    )
```

time: 211 us -> 59.5 us (0.28)
  blocking collectives: 79.9 us -> 0 us
  waiting for transfers between devices: 85.3 us -> 27.4 us
  Pallas kernels: 0 us -> 16.5 us
  between operations: 14.8 us -> 0.7 us
  other arithmetic: 6.26 us -> 0 us
  matrix products: 3.42 us -> 0 us
  starting transfers between devices: 15.2 us -> 12.4 us
    unnamed x2 -> x0, waiting for transfers between devices: 85.3 us -> none
    all_gather x1 -> x0, blocking collectives: 79.9 us -> none  [body(): whole_metric = lax.all_gather(metric_half, 'row', axis=0, tiled=True)]
    ppermute x0 -> x15, waiting for transfers between devices: none -> 27.4 us  [swap(): return lax.ppermute(piece, 'row', [(i, i ^ mask) for i in range(devices)])]
    pallas_call x0 -> x2, Pallas kernels: none -> 16.5 us  [the longest x1 14.8 us: body(): pl.pallas_call(functools.partial(block_kernel, devices, tiles, fanout), o...]
    all_to_all x2 -> x0, starting transfers between devices: 15.1 us -> none  [the longest x1 7.61 us: body(): lax.all_to_all(strips, 'row', split_axis=0, concat_axis=0, tiled=True)]
    ppermute x0 -> x15, starting transfers between devices: none -> 12.4 us  [swap(): return lax.ppermute(piece, 'row', [(i, i ^ mask) for i in range(devices)])]
    dot_general x2 -> x0, matrix products: 3.42 us -> none  [the longest x1 1.79 us: body(): jnp.einsum('drl,pl->drp', got_rows, scaled, preferred_element_type=jnp.fl...]
    convert_element_type x1 -> x0, other arithmetic: 2.43 us -> none  [body(): send_rows = jnp.einsum('bd,brl->drl', routed_bf, masked.reshape(local_blo...]
  transfers between devices with their start and end apart: 3 -> 15, of which waited for: 1 -> 5; matrix products, arithmetic and copies ran while one was open for 3% -> 0% of each run, Pallas kernels for 0% -> 0%
where the time goes in v1:
time: 59.5 us; the launch traced here: 59.3 us
  waiting for transfers between devices  27.4 us (46%)
  Pallas kernels  16.5 us (28%)
  starting transfers between devices  12.4 us (21%)
  local copies, waits for them, and re-layouts  2.22 us (4%)
  between operations  0.7 us (1%)
    ppermute x15, waiting for transfers between devices, swap(): return lax.ppermute(piece, 'row', [(i, i ^ mask) for i in range(devices)])  27.4 us
    pallas_call x1, Pallas kernels, body(): pl.pallas_call(functools.partial(block_kernel, devices, tiles, fanout), o...  14.8 us
    ppermute x15, starting transfers between devices, swap(): return lax.ppermute(piece, 'row', [(i, i ^ mask) for i in range(devices)])  12.4 us
    pallas_call x1, Pallas kernels, body(): pl.pallas_call(functools.partial(pack_kernel, tiles, fanout), out_shape=j...  1.74 us
    reshape x1, local copies, waits for them, and re-layouts, body(): tau = tau_weights.reshape(1, contracted)  1.27 us
  transfers between devices with their start and end apart: 15, of which 5 were waited for; matrix products, arithmetic and copies ran while one was open for 0% of the time, Pallas kernels for 0%

profile of v1, /device:TPU:0, one launch (start us, length us, event | category | flops | bytes accessed | tf_op | source)
XLA Modules:
  0.0 59.3 jit_solution(3492467581323077369)
XLA Ops:
  0.6 1.3 %reshape.11.tau_ref.refs_4_ = f32[1,768]{1,0:T(1,128)} reshape(f32[768]{0:T(1024)} %param.6) | data formatting | bytes 6144 | tf_op jit(solution)/shard_map/reshape | solution.py:115
  1.9 0.0 copy-start.1
  1.9 1.7 %pack.1.refs_5_ = bf16[912,128]{1,0:T(8,128)(2,1)} custom-call(s32[1,6]{1,0:T(1,128)} %refs_1_.1, s32[1,8]{1,0:T(1,128)} %refs_2_.1, bf16[128,768]{1,0:T(8,128)(2,1)} %refs_3_.1, f32[1,768]{1,0:T(1,128)} %reshape.11.tau_ref.refs_4_, bf16[128,128]{1,0:T(8,128)(2,1)} %metric_ref.1), custom_call_target="tpu_custom_call" | custom-call | tf_op jit(solution)/shard_map/pack/pallas_call | solution.py:116
  3.6 5.0 %collective-permute-start.11 = (bf16[912,128]{1,0:T(8,128)(2,1)}, bf16[912,128]{1,0:T(8,128)(2,1)S(1)}, u32[]{:S(2)}, u32[]{:S(2)}) collective-permute-start(bf16[912,128]{1,0:T(8,128)(2,1)} %pack.1.refs_5_), channel_id=1, source_target_pairs={{0,12},{1,13},{2,14},{3,15},{4,8},{5,9},{6,10},{7,11},{8,4},{9,5},... | collective-permute-start | bytes 700424 | tf_op jit(solution)/shard_map/ppermute | solution.py:125
  8.7 0.0 collective-permute-start.7
  8.7 0.6 collective-permute-start.3
  9.3 1.7 %collective-permute-start.1 = (bf16[912,128]{1,0:T(8,128)(2,1)}, bf16[912,128]{1,0:T(8,128)(2,1)S(1)}, u32[]{:S(2)}, u32[]{:S(2)}) collective-permute-start(bf16[912,128]{1,0:T(8,128)(2,1)} %pack.1.refs_5_), channel_id=1, source_target_pairs={{0,2},{1,3},{2,0},{3,1},{4,6},{5,7},{6,4},{7,5},{8,10},{9,11},{10,... | collective-permute-start | bytes 700424 | tf_op jit(solution)/shard_map/ppermute | solution.py:125
  11.0 0.0 collective-permute-start
  11.0 4.6 %collective-permute-done.11.refs_17_ = bf16[912,128]{1,0:T(8,128)(2,1)S(1)} collective-permute-done((bf16[912,128]{1,0:T(8,128)(2,1)}, bf16[912,128]{1,0:T(8,128)(2,1)S(1)}, u32[]{:S(2)}, u32[]{:S(2)}) %collective-permute-start.11) | collective-permute-done | bytes 233504 | tf_op jit(solution)/shard_map/ppermute | solution.py:125
  15.6 1.7 %collective-permute-start.13 = (bf16[912,128]{1,0:T(8,128)(2,1)S(1)}, bf16[912,128]{1,0:T(8,128)(2,1)S(1)}, u32[]{:S(2)}, u32[]{:S(2)}) collective-permute-start(bf16[912,128]{1,0:T(8,128)(2,1)S(1)} %collective-permute-done.11.refs_17_), channel_id=1, source_target_pairs={{0,2},{1,3},{2,0},{3,1},{4,6},{5,7},{6,4},{7,5},{8,10},{9,11},{10,... | collective-permute-start | bytes 700424 | tf_op jit(solution)/shard_map/ppermute | solution.py:125
  17.3 11.5 %collective-permute-done.7.refs_13_ = bf16[912,128]{1,0:T(8,128)(2,1)S(1)} collective-permute-done((bf16[912,128]{1,0:T(8,128)(2,1)}, bf16[912,128]{1,0:T(8,128)(2,1)S(1)}, u32[]{:S(2)}, u32[]{:S(2)}) %collective-permute-start.7) | collective-permute-done | bytes 233504 | tf_op jit(solution)/shard_map/ppermute | solution.py:125
  28.8 0.0 collective-permute-start.12
  28.8 0.0 collective-permute-done.3.refs_9_
  28.8 1.5 %collective-permute-start.9 = (bf16[912,128]{1,0:T(8,128)(2,1)S(1)}, bf16[912,128]{1,0:T(8,128)(2,1)S(1)}, u32[]{:S(2)}, u32[]{:S(2)}) collective-permute-start(bf16[912,128]{1,0:T(8,128)(2,1)S(1)} %collective-permute-done.7.refs_13_), channel_id=1, source_target_pairs={{0,2},{1,3},{2,0},{3,1},{4,6},{5,7},{6,4},{7,5},{8,10},{9,11},{10,... | collective-permute-start | bytes 700424 | tf_op jit(solution)/shard_map/ppermute | solution.py:125
  30.3 0.0 collective-permute-done.1.refs_7_
  30.3 0.2 collective-permute-start.8
  30.5 0.0 collective-permute-done.refs_6_
  30.5 0.5 collective-permute-start.5
  31.0 0.0 collective-permute-done.13.refs_19_
  31.0 0.0 collective-permute-start.4
  31.0 0.0 collective-permute-done.12.refs_18_
  31.0 0.5 collective-permute-start.2
  31.5 5.7 %collective-permute-done.9.refs_15_ = bf16[912,128]{1,0:T(8,128)(2,1)S(1)} collective-permute-done((bf16[912,128]{1,0:T(8,128)(2,1)S(1)}, bf16[912,128]{1,0:T(8,128)(2,1)S(1)}, u32[]{:S(2)}, u32[]{:S(2)}) %collective-permute-start.9) | collective-permute-done | bytes 233504 | tf_op jit(solution)/shard_map/ppermute | solution.py:125
  37.3 0.0 collective-permute-start.14
  37.3 0.0 collective-permute-done.8.refs_14_
  37.3 0.5 collective-permute-start.10
  37.8 4.1 %collective-permute-done.5.refs_11_ = bf16[912,128]{1,0:T(8,128)(2,1)S(1)} collective-permute-done((bf16[912,128]{1,0:T(8,128)(2,1)S(1)}, bf16[912,128]{1,0:T(8,128)(2,1)S(1)}, u32[]{:S(2)}, u32[]{:S(2)}) %collective-permute-start.5) | collective-permute-done | bytes 233504 | tf_op jit(solution)/shard_map/ppermute | solution.py:125
  41.9 0.0 collective-permute-start.6
  41.9 0.0 copy-start.2
  41.9 0.0 copy-start.3
  41.9 0.0 copy-start.4
  41.9 0.0 collective-permute-done.4.refs_10_
  41.9 0.0 collective-permute-done.2.refs_8_
  41.9 0.0 collective-permute-done.14.refs_20_
  41.9 0.0 collective-permute-done.10.refs_16_
  41.9 1.6 %collective-permute-done.6.refs_12_ = bf16[912,128]{1,0:T(8,128)(2,1)} collective-permute-done((bf16[912,128]{1,0:T(8,128)(2,1)S(1)}, bf16[912,128]{1,0:T(8,128)(2,1)}, u32[]{:S(2)}, u32[]{:S(2)}) %collective-permute-start.6) | collective-permute-done | bytes 233504 | tf_op jit(solution)/shard_map/ppermute | solution.py:125
  43.5 0.0 copy-done.1
  43.5 0.0 copy-done.2
  43.5 0.0 copy-done.3
  43.5 0.0 copy-done.4
  43.5 0.0 copy-start
  43.5 0.9 %copy-done = bf16[912,128]{1,0:T(8,128)(2,1)S(1)} copy-done((bf16[912,128]{1,0:T(8,128)(2,1)S(1)}, bf16[912,128]{1,0:T(8,128)(2,1)}, u32[]{:S(2)}) %copy-start) | copy-done | bytes 233496
  44.5 14.8 %blocks.1 = (bf16[1,8,128,128]{3,2,1,0:T(8,128)(2,1)}, f32[8,128]{1,0:T(8,128)}) custom-call(s32[1]{0:T(128)} %bitcast.refs_0_, s32[1,6]{1,0:T(1,128)S(1)} %copy-done.3, s32[1,8]{1,0:T(1,128)S(1)} %copy-done.4, bf16[128,768]{1,0:T(8,128)(2,1)S(1)} %copy-done.1, f32[1,768]{1,0:T(1,128)S(1)} %copy-done.2, bf16[912,128]{1,0:T(8,128)(2,1)S(1)} %copy-done, ...), custom_call_target="tpu_custom_call" | custom-call | tf_op jit(solution)/shard_map/blocks/pallas_call | solution.py:135
Async XLA Ops:
  1.9 41.6 %copy-start.1 = (bf16[128,768]{1,0:T(8,128)(2,1)S(1)}, bf16[128,768]{1,0:T(8,128)(2,1)}, u32[]{:S(2)}) copy-start(bf16[128,768]{1,0:T(8,128)(2,1)} %refs_3_.1) | copy-start | bytes 589828
  3.6 11.9 %collective-permute-start.11 = (bf16[912,128]{1,0:T(8,128)(2,1)}, bf16[912,128]{1,0:T(8,128)(2,1)S(1)}, u32[]{:S(2)}, u32[]{:S(2)}) collective-permute-start(bf16[912,128]{1,0:T(8,128)(2,1)} %pack.1.refs_5_), channel_id=1, source_target_pairs={{0,12},{1,13},{2,14},{3,15},{4,8},{5,9},{6,10},{7,11},{8,4},{9,5},... | collective-permute-start | bytes 700424 | tf_op jit(solution)/shard_map/ppermute | solution.py:125
  8.7 20.1 %collective-permute-start.7 = (bf16[912,128]{1,0:T(8,128)(2,1)}, bf16[912,128]{1,0:T(8,128)(2,1)S(1)}, u32[]{:S(2)}, u32[]{:S(2)}) collective-permute-start(bf16[912,128]{1,0:T(8,128)(2,1)} %pack.1.refs_5_), channel_id=1, source_target_pairs={{0,8},{1,9},{2,10},{3,11},{4,12},{5,13},{6,14},{7,15},{8,0},{9,1},... | collective-permute-start | bytes 700424 | tf_op jit(solution)/shard_map/ppermute | solution.py:125
  8.7 20.1 %collective-permute-start.3 = (bf16[912,128]{1,0:T(8,128)(2,1)}, bf16[912,128]{1,0:T(8,128)(2,1)S(1)}, u32[]{:S(2)}, u32[]{:S(2)}) collective-permute-start(bf16[912,128]{1,0:T(8,128)(2,1)} %pack.1.refs_5_), channel_id=1, source_target_pairs={{0,4},{1,5},{2,6},{3,7},{4,0},{5,1},{6,2},{7,3},{8,12},{9,13},{10,... | collective-permute-start | bytes 700424 | tf_op jit(solution)/shard_map/ppermute | solution.py:125
  9.3 21.0 %collective-permute-start.1 = (bf16[912,128]{1,0:T(8,128)(2,1)}, bf16[912,128]{1,0:T(8,128)(2,1)S(1)}, u32[]{:S(2)}, u32[]{:S(2)}) collective-permute-start(bf16[912,128]{1,0:T(8,128)(2,1)} %pack.1.refs_5_), channel_id=1, source_target_pairs={{0,2},{1,3},{2,0},{3,1},{4,6},{5,7},{6,4},{7,5},{8,10},{9,11},{10,... | collective-permute-start | bytes 700424 | tf_op jit(solution)/shard_map/ppermute | solution.py:125
  11.0 19.5 %collective-permute-start = (bf16[912,128]{1,0:T(8,128)(2,1)}, bf16[912,128]{1,0:T(8,128)(2,1)S(1)}, u32[]{:S(2)}, u32[]{:S(2)}) collective-permute-start(bf16[912,128]{1,0:T(8,128)(2,1)} %pack.1.refs_5_), channel_id=1, source_target_pairs={{0,1},{1,0},{2,3},{3,2},{4,5},{5,4},{6,7},{7,6},{8,9},{9,8},{10,11... | collective-permute-start | bytes 700424 | tf_op jit(solution)/shard_map/ppermute | solution.py:125
  15.6 15.5 %collective-permute-start.13 = (bf16[912,128]{1,0:T(8,128)(2,1)S(1)}, bf16[912,128]{1,0:T(8,128)(2,1)S(1)}, u32[]{:S(2)}, u32[]{:S(2)}) collective-permute-start(bf16[912,128]{1,0:T(8,128)(2,1)S(1)} %collective-permute-done.11.refs_17_), channel_id=1, source_target_pairs={{0,2},{1,3},{2,0},{3,1},{4,6},{5,7},{6,4},{7,5},{8,10},{9,11},{10,... | collective-permute-start | bytes 700424 | tf_op jit(solution)/shard_map/ppermute | solution.py:125
  28.8 2.3 %collective-permute-start.12 = (bf16[912,128]{1,0:T(8,128)(2,1)S(1)}, bf16[912,128]{1,0:T(8,128)(2,1)S(1)}, u32[]{:S(2)}, u32[]{:S(2)}) collective-permute-start(bf16[912,128]{1,0:T(8,128)(2,1)S(1)} %collective-permute-done.11.refs_17_), channel_id=1, source_target_pairs={{0,1},{1,0},{2,3},{3,2},{4,5},{5,4},{6,7},{7,6},{8,9},{9,8},{10,11... | collective-permute-start | bytes 700424 | tf_op jit(solution)/shard_map/ppermute | solution.py:125
  28.8 8.5 %collective-permute-start.9 = (bf16[912,128]{1,0:T(8,128)(2,1)S(1)}, bf16[912,128]{1,0:T(8,128)(2,1)S(1)}, u32[]{:S(2)}, u32[]{:S(2)}) collective-permute-start(bf16[912,128]{1,0:T(8,128)(2,1)S(1)} %collective-permute-done.7.refs_13_), channel_id=1, source_target_pairs={{0,2},{1,3},{2,0},{3,1},{4,6},{5,7},{6,4},{7,5},{8,10},{9,11},{10,... | collective-permute-start | bytes 700424 | tf_op jit(solution)/shard_map/ppermute | solution.py:125
  30.3 7.0 %collective-permute-start.8 = (bf16[912,128]{1,0:T(8,128)(2,1)S(1)}, bf16[912,128]{1,0:T(8,128)(2,1)S(1)}, u32[]{:S(2)}, u32[]{:S(2)}) collective-permute-start(bf16[912,128]{1,0:T(8,128)(2,1)S(1)} %collective-permute-done.7.refs_13_), channel_id=1, source_target_pairs={{0,1},{1,0},{2,3},{3,2},{4,5},{5,4},{6,7},{7,6},{8,9},{9,8},{10,11... | collective-permute-start | bytes 700424 | tf_op jit(solution)/shard_map/ppermute | solution.py:125
  30.5 11.4 %collective-permute-start.5 = (bf16[912,128]{1,0:T(8,128)(2,1)S(1)}, bf16[912,128]{1,0:T(8,128)(2,1)S(1)}, u32[]{:S(2)}, u32[]{:S(2)}) collective-permute-start(bf16[912,128]{1,0:T(8,128)(2,1)S(1)} %collective-permute-done.3.refs_9_), channel_id=1, source_target_pairs={{0,2},{1,3},{2,0},{3,1},{4,6},{5,7},{6,4},{7,5},{8,10},{9,11},{10,... | collective-permute-start | bytes 700424 | tf_op jit(solution)/shard_map/ppermute | solution.py:125
  31.0 10.9 %collective-permute-start.4 = (bf16[912,128]{1,0:T(8,128)(2,1)S(1)}, bf16[912,128]{1,0:T(8,128)(2,1)S(1)}, u32[]{:S(2)}, u32[]{:S(2)}) collective-permute-start(bf16[912,128]{1,0:T(8,128)(2,1)S(1)} %collective-permute-done.3.refs_9_), channel_id=1, source_target_pairs={{0,1},{1,0},{2,3},{3,2},{4,5},{5,4},{6,7},{7,6},{8,9},{9,8},{10,11... | collective-permute-start | bytes 700424 | tf_op jit(solution)/shard_map/ppermute | solution.py:125
  31.0 10.9 %collective-permute-start.2 = (bf16[912,128]{1,0:T(8,128)(2,1)S(1)}, bf16[912,128]{1,0:T(8,128)(2,1)S(1)}, u32[]{:S(2)}, u32[]{:S(2)}) collective-permute-start(bf16[912,128]{1,0:T(8,128)(2,1)S(1)} %collective-permute-done.1.refs_7_), channel_id=1, source_target_pairs={{0,1},{1,0},{2,3},{3,2},{4,5},{5,4},{6,7},{7,6},{8,9},{9,8},{10,11... | collective-permute-start | bytes 700424 | tf_op jit(solution)/shard_map/ppermute | solution.py:125
  37.3 4.7 %collective-permute-start.14 = (bf16[912,128]{1,0:T(8,128)(2,1)S(1)}, bf16[912,128]{1,0:T(8,128)(2,1)S(1)}, u32[]{:S(2)}, u32[]{:S(2)}) collective-permute-start(bf16[912,128]{1,0:T(8,128)(2,1)S(1)} %collective-permute-done.13.refs_19_), channel_id=1, source_target_pairs={{0,1},{1,0},{2,3},{3,2},{4,5},{5,4},{6,7},{7,6},{8,9},{9,8},{10,11... | collective-permute-start | bytes 700424 | tf_op jit(solution)/shard_map/ppermute | solution.py:125
  37.3 4.7 %collective-permute-start.10 = (bf16[912,128]{1,0:T(8,128)(2,1)S(1)}, bf16[912,128]{1,0:T(8,128)(2,1)S(1)}, u32[]{:S(2)}, u32[]{:S(2)}) collective-permute-start(bf16[912,128]{1,0:T(8,128)(2,1)S(1)} %collective-permute-done.9.refs_15_), channel_id=1, source_target_pairs={{0,1},{1,0},{2,3},{3,2},{4,5},{5,4},{6,7},{7,6},{8,9},{9,8},{10,11... | collective-permute-start | bytes 700424 | tf_op jit(solution)/shard_map/ppermute | solution.py:125
  41.9 1.6 %collective-permute-start.6 = (bf16[912,128]{1,0:T(8,128)(2,1)S(1)}, bf16[912,128]{1,0:T(8,128)(2,1)}, u32[]{:S(2)}, u32[]{:S(2)}) collective-permute-start(bf16[912,128]{1,0:T(8,128)(2,1)S(1)} %collective-permute-done.5.refs_11_), channel_id=1, source_target_pairs={{0,1},{1,0},{2,3},{3,2},{4,5},{5,4},{6,7},{7,6},{8,9},{9,8},{10,11... | collective-permute-start | bytes 700424 | tf_op jit(solution)/shard_map/ppermute | solution.py:125
  41.9 1.6 %copy-start.2 = (f32[1,768]{1,0:T(1,128)S(1)}, f32[1,768]{1,0:T(1,128)}, u32[]{:S(2)}) copy-start(f32[1,768]{1,0:T(1,128)} %reshape.11.tau_ref.refs_4_) | copy-start | bytes 9220
  41.9 1.6 %copy-start.3 = (s32[1,6]{1,0:T(1,128)S(1)}, s32[1,6]{1,0:T(1,128)}, u32[]{:S(2)}) copy-start(s32[1,6]{1,0:T(1,128)} %refs_1_.1) | copy-start | bytes 76
  41.9 1.6 %copy-start.4 = (s32[1,8]{1,0:T(1,128)S(1)}, s32[1,8]{1,0:T(1,128)}, u32[]{:S(2)}) copy-start(s32[1,8]{1,0:T(1,128)} %refs_2_.1) | copy-start | bytes 100
  43.5 0.9 %copy-start = (bf16[912,128]{1,0:T(8,128)(2,1)S(1)}, bf16[912,128]{1,0:T(8,128)(2,1)}, u32[]{:S(2)}) copy-start(bf16[912,128]{1,0:T(8,128)(2,1)} %pack.1.refs_5_) | copy-start | bytes 700420

commit v2 on v0

v2 whole, which is shorter than its diff:
```python
import functools

import jax
import jax.numpy as jnp
from jax import lax
from jax.experimental import pallas as pl
from jax.experimental.pallas import tpu as pltpu
from jax.sharding import PartitionSpec as P

BLOCK = 128
LIST_ROWS = 16
LAYER = 4
NT_DIMS = (((1,), (1,)), ((), ()))
NN_DIMS = (((1,), (0,)), ((), ()))


def dot(a, b, dims=NN_DIMS):
    return lax.dot_general(a, b, dims, preferred_element_type=jnp.float32)


def split(x):
    high = x.astype(jnp.bfloat16)
    return high, (x - high.astype(jnp.float32)).astype(jnp.bfloat16)


def pack_kernel(mask_ref, dest_ref, rows_ref, tau_ref, metric_ref, piece_ref, masked_ref, row_ref):
    tiles = mask_ref.shape[1]
    depth = tiles * BLOCK
    row_ref[...] = tau_ref[...].reshape(1, depth)
    for t in range(tiles):
        cols = slice(t * BLOCK, (t + 1) * BLOCK)
        kept = rows_ref[:, cols].astype(jnp.float32) * mask_ref[0, t].astype(jnp.float32)
        masked_ref[:, cols] = kept.astype(jnp.bfloat16)
        piece_ref[cols, :] = (kept * row_ref[:, cols]).astype(jnp.bfloat16)
    piece_ref[depth : depth + BLOCK, :] = metric_ref[...]
    lane = lax.broadcasted_iota(jnp.int32, (LIST_ROWS, BLOCK), 1)
    listed = jnp.zeros((LIST_ROWS, BLOCK), jnp.float32)
    for j in range(dest_ref.shape[1]):
        listed += (lane == dest_ref[0, j]).astype(jnp.float32)
    piece_ref[depth + BLOCK :, :] = listed.astype(jnp.bfloat16)


def scaled_of(piece):
    depth = piece.shape[0] - BLOCK - LIST_ROWS
    return jnp.concatenate([piece[t : t + BLOCK, :] for t in range(0, depth, BLOCK)], axis=1)


def metric_of(piece):
    depth = piece.shape[0] - BLOCK - LIST_ROWS
    return piece[depth : depth + BLOCK, :]


def blocks_of(me, masked, pieces, strips, window):
    rows = window.shape[0] // len(pieces)
    lane = lax.broadcasted_iota(jnp.int32, (rows, BLOCK), 1)
    row = lax.broadcasted_iota(jnp.int32, (rows, BLOCK), 0)
    pick = (lane == row + me * rows).astype(jnp.bfloat16)
    own = [dot(pick, metric_of(piece), NT_DIMS).astype(jnp.bfloat16) for piece in pieces]
    for k, piece in enumerate(pieces):
        scaled = scaled_of(piece)
        window[k * rows : (k + 1) * rows, :] = dot(own[k], scaled)
        strips[k] = dot(masked, scaled, NT_DIMS).astype(jnp.bfloat16)


def early_kernel(me_ref, masked_ref, *refs):
    blocks_of(me_ref[0], masked_ref[...], refs[:-2], refs[-2], refs[-1])


def last_kernel(devices, early, me_ref, dest_ref, masked_ref, tau_ref, *refs):
    pieces = refs[:devices]
    early_strips = refs[devices : devices + early]
    early_windows = refs[devices + early : devices + 2 * early]
    chi_ref, sand_ref, strips, window, listed, sems = refs[devices + 2 * early :]
    me = me_ref[0]
    rows = BLOCK // devices
    fanout = dest_ref.shape[1]
    done = 0
    for k in range(early):
        count = early_strips[k].shape[0]
        strips[done : done + count] = early_strips[k][...]
        window[done * rows : (done + count) * rows, :] = early_windows[k][...]
        done += count
    blocks_of(me, masked_ref[...], pieces[done:], strips.at[done:], window.at[done * rows :])
    copies = [
        pltpu.make_async_copy(strips.at[dest_ref[0, j] ^ me], chi_ref.at[0, j], sems.at[j])
        for j in range(fanout)
    ]
    for copy in copies:
        copy.start()

    for m in range(devices):
        entry = pieces[m][pieces[m].shape[0] - LIST_ROWS :, :].astype(jnp.float32)
        listed[m * rows : (m + 1) * rows, :] = entry[:rows, :]
    row = lax.broadcasted_iota(jnp.int32, (BLOCK, BLOCK), 0)
    column = lax.broadcasted_iota(jnp.int32, (BLOCK, BLOCK), 1)
    by_piece = (row == (column // rows ^ me)).astype(jnp.bfloat16)
    routes = dot(listed[...].astype(jnp.bfloat16), by_piece)
    same = row % rows == column % rows
    pair = jnp.where(same, routes + routes.T, 0.0).astype(jnp.bfloat16)
    mixed = dot(jnp.concatenate([pair, pair], axis=1), jnp.concatenate(split(window[...]), axis=0))
    high, low = split(mixed / tau_ref[...])
    sides = []
    for m in range(devices):
        part = slice(m * rows, (m + 1) * rows)
        side = dot(jnp.concatenate([high[part], low[part]], axis=0), scaled_of(pieces[m]), NT_DIMS)
        sides.append(side[:rows] + side[rows:])
    total = jnp.zeros((2 * rows, BLOCK), jnp.float32)
    for m in range(devices):
        total += dot(jnp.concatenate(split(sides[m]), axis=0), metric_of(pieces[m]))
    sand_ref[...] = total[:rows] + total[rows:]
    for copy in copies:
        copy.wait()


def after(value, *others):
    return lax.optimization_barrier((value, *others))[0]


def gather_pieces(own, devices):
    def swap(piece, mask):
        return lax.ppermute(piece, "row", [(i, i ^ mask) for i in range(devices)])

    far = list(range(LAYER, devices, LAYER))
    got = {0: own, 2: swap(own, 2)}
    for mask in far:
        got[mask] = swap(own, mask)
    for k, mask in enumerate(far):
        got[mask + 2] = swap(after(got[mask], *[got[m] for m in far[:k]]), 2)
    got[1] = swap(after(own, got[2]), 1)
    got[3] = swap(got[2], 1)
    for k, mask in enumerate(far):
        later = got[far[k + 1]] if k + 1 < len(far) else got[mask - 2]
        got[mask + 1] = swap(after(got[mask], got[mask - 2]), 1)
        got[mask + 3] = swap(after(got[mask + 2], later), 1)
    return [got[m] for m in range(devices)]


def body(three_center, tau_weights, tile_mask, dest, metric_half):
    devices = lax.axis_size("row")
    local_rows, contracted = three_center.shape
    fanout = dest.shape[1]
    rows = BLOCK // devices
    piece_rows = contracted + BLOCK + LIST_ROWS
    smem = pl.BlockSpec(memory_space=pltpu.SMEM)
    vmem = pl.BlockSpec(memory_space=pltpu.VMEM)
    own, masked, tau = pl.pallas_call(
        pack_kernel,
        out_shape=(
            jax.ShapeDtypeStruct((piece_rows, BLOCK), jnp.bfloat16),
            jax.ShapeDtypeStruct((local_rows, contracted), jnp.bfloat16),
            jax.ShapeDtypeStruct((1, contracted), jnp.float32),
        ),
        in_specs=[smem, smem, vmem, vmem, vmem],
        out_specs=(vmem, vmem, vmem),
        name="pack",
    )(tile_mask, dest, three_center, tau_weights, metric_half)
    pieces = gather_pieces(own, devices)
    me = lax.axis_index("row").astype(jnp.int32).reshape(1)
    strips, windows = [], []
    for first in range(0, devices - LAYER, LAYER):
        strip, window = pl.pallas_call(
            early_kernel,
            out_shape=(
                jax.ShapeDtypeStruct((LAYER, BLOCK, BLOCK), jnp.bfloat16),
                jax.ShapeDtypeStruct((LAYER * rows, contracted), jnp.float32),
            ),
            in_specs=[smem] + [vmem] * (1 + LAYER),
            out_specs=(vmem, vmem),
            name="early",
        )(me, masked, *pieces[first : first + LAYER])
        strips.append(strip)
        windows.append(window)
    return pl.pallas_call(
        functools.partial(last_kernel, devices, len(strips)),
        out_shape=(
            jax.ShapeDtypeStruct((1, fanout, BLOCK, BLOCK), jnp.bfloat16),
            jax.ShapeDtypeStruct((rows, BLOCK), jnp.float32),
        ),
        in_specs=[smem, smem] + [vmem] * (2 + devices + 2 * len(strips)),
        out_specs=(pl.BlockSpec(memory_space=pl.ANY), vmem),
        scratch_shapes=[
            pltpu.VMEM((devices, BLOCK, BLOCK), jnp.bfloat16),
            pltpu.VMEM((BLOCK, contracted), jnp.float32),
            pltpu.VMEM((BLOCK, BLOCK), jnp.float32),
            pltpu.SemaphoreType.DMA((fanout,)),
        ],
        compiler_params=pltpu.CompilerParams(vmem_limit_bytes=40 * 1024 * 1024),
        name="last",
    )(me, dest, masked, tau, *pieces, *strips, *windows)


def solution(mesh):
    return jax.shard_map(
        body,
        mesh=mesh,
        in_specs=(
            P(("groups", "row"), None),
            P("groups"),
            P("row", None),
            P("row", None),
            P("row", None),
        ),
        out_specs=(P(("groups", "row"), None, None, None), P(("groups", "row"), None)),
        check_vma=False,
    )
```

time: 211 us -> 65.7 us (0.31)
  the two profiles are of different devices: /device:TPU:0 before, /device:TPU:17 now
where the time goes in v2:
time: 65.7 us; the launch traced here: 65.1 us
  waiting for transfers between devices  25.1 us (38%)
  Pallas kernels  13.9 us (21%)
  local copies, waits for them, and re-layouts  12.9 us (20%)
  starting transfers between devices  12.4 us (19%)
  between operations  0.85 us (1%)
    ppermute x15, waiting for transfers between devices, swap(): return lax.ppermute(piece, 'row', [(i, i ^ mask) for i in range(devices)])  25.1 us
    unnamed x64, local copies, waits for them, and re-layouts  12.9 us
    ppermute x15, starting transfers between devices, swap(): return lax.ppermute(piece, 'row', [(i, i ^ mask) for i in range(devices)])  12.4 us
    pallas_call x3, Pallas kernels, body(): pl.pallas_call(early_kernel, out_shape=(jax.ShapeDtypeStruct((LAYER, BLOC...  7.83 us
    pallas_call x1, Pallas kernels, body(): pl.pallas_call(functools.partial(last_kernel, devices, len(strips)), out_...  4.32 us
    pallas_call x1, Pallas kernels, body(): pl.pallas_call(pack_kernel, out_shape=(jax.ShapeDtypeStruct((piece_rows,...  1.77 us
  transfers between devices with their start and end apart: 15, of which 5 were waited for; matrix products, arithmetic and copies ran while one was open for 0% of the time, Pallas kernels for 12%

profile of v2, /device:TPU:17, one launch (start us, length us, event | category | flops | bytes accessed | tf_op | source)
XLA Modules:
  0.0 65.1 jit_solution(13687164533604935089)
XLA Ops:
  0.6 1.8 %pack.1 = (bf16[912,128]{1,0:T(8,128)(2,1)}, bf16[128,768]{1,0:T(8,128)(2,1)}, f32[1,768]{1,0:T(1,128)}) custom-call(s32[1,6]{1,0:T(1,128)} %mask_ref.1, s32[1,8]{1,0:T(1,128)} %dest_ref.3, bf16[128,768]{1,0:T(8,128)(2,1)} %rows_ref.1, f32[768]{0:T(1024)} %tau_ref.1, bf16[128,128]{1,0:T(8,128)(2,1)} %metric_ref.1), custom_call_target="tpu_custom_call" | custom-call | tf_op jit(solution)/shard_map/pack/pallas_call | solution.py:146
  2.4 1.3 %collective-permute-start.3 = (bf16[912,128]{1,0:T(8,128)(2,1)}, bf16[912,128]{1,0:T(8,128)(2,1)S(1)}, u32[]{:S(2)}, u32[]{:S(2)}) collective-permute-start(bf16[912,128]{1,0:T(8,128)(2,1)} %get-tuple-element.23.refs_0_), channel_id=1, source_target_pairs={{0,4},{1,5},{2,6},{3,7},{4,0},{5,1},{6,2},{7,3},{8,12},{9,13},{10,... | collective-permute-start | bytes 700424 | tf_op jit(solution)/shard_map/ppermute | solution.py:121
  3.8 1.3 %collective-permute-start.10 = (bf16[912,128]{1,0:T(8,128)(2,1)}, bf16[912,128]{1,0:T(8,128)(2,1)S(1)}, u32[]{:S(2)}, u32[]{:S(2)}) collective-permute-start(bf16[912,128]{1,0:T(8,128)(2,1)} %get-tuple-element.23.refs_0_), channel_id=1, source_target_pairs={{0,12},{1,13},{2,14},{3,15},{4,8},{5,9},{6,10},{7,11},{8,4},{9,5},... | collective-permute-start | bytes 700424 | tf_op jit(solution)/shard_map/ppermute | solution.py:121
  5.0 1.2 %collective-permute-start = (bf16[912,128]{1,0:T(8,128)(2,1)}, bf16[912,128]{1,0:T(8,128)(2,1)S(1)}, u32[]{:S(2)}, u32[]{:S(2)}) collective-permute-start(bf16[912,128]{1,0:T(8,128)(2,1)} %get-tuple-element.23.refs_0_), channel_id=1, source_target_pairs={{0,2},{1,3},{2,0},{3,1},{4,6},{5,7},{6,4},{7,5},{8,10},{9,11},{10,... | collective-permute-start | bytes 700424 | tf_op jit(solution)/shard_map/ppermute | solution.py:121
  6.3 6.2 %collective-permute-done.6.refs_0_.refs_8_ = bf16[912,128]{1,0:T(8,128)(2,1)S(1)} collective-permute-done((bf16[912,128]{1,0:T(8,128)(2,1)}, bf16[912,128]{1,0:T(8,128)(2,1)S(1)}, u32[]{:S(2)}, u32[]{:S(2)}) %collective-permute-start.6) | collective-permute-done | bytes 233504 | tf_op jit(solution)/shard_map/ppermute | solution.py:121
  12.4 1.7 %collective-permute-done.3.refs_0_.refs_4_ = bf16[912,128]{1,0:T(8,128)(2,1)S(1)} collective-permute-done((bf16[912,128]{1,0:T(8,128)(2,1)}, bf16[912,128]{1,0:T(8,128)(2,1)S(1)}, u32[]{:S(2)}, u32[]{:S(2)}) %collective-permute-start.3) | collective-permute-done | bytes 233504 | tf_op jit(solution)/shard_map/ppermute | solution.py:121
  14.2 1.2 %collective-permute-start.9 = (bf16[912,128]{1,0:T(8,128)(2,1)S(1)}, bf16[912,128]{1,0:T(8,128)(2,1)S(1)}, u32[]{:S(2)}, u32[]{:S(2)}) collective-permute-start(bf16[912,128]{1,0:T(8,128)(2,1)S(1)} %collective-permute-done.6.refs_0_.refs_8_), channel_id=1, source_target_pairs={{0,2},{1,3},{2,0},{3,1},{4,6},{5,7},{6,4},{7,5},{8,10},{9,11},{10,... | collective-permute-start | bytes 700424 | tf_op jit(solution)/shard_map/ppermute | solution.py:121
  15.4 10.7 %collective-permute-done.10.refs_12_ = bf16[912,128]{1,0:T(8,128)(2,1)S(1)} collective-permute-done((bf16[912,128]{1,0:T(8,128)(2,1)}, bf16[912,128]{1,0:T(8,128)(2,1)S(1)}, u32[]{:S(2)}, u32[]{:S(2)}) %collective-permute-start.10) | collective-permute-done | bytes 233504 | tf_op jit(solution)/shard_map/ppermute | solution.py:121
  26.1 1.2 %collective-permute-start.13 = (bf16[912,128]{1,0:T(8,128)(2,1)S(1)}, bf16[912,128]{1,0:T(8,128)(2,1)S(1)}, u32[]{:S(2)}, u32[]{:S(2)}) collective-permute-start(bf16[912,128]{1,0:T(8,128)(2,1)S(1)} %collective-permute-done.10.refs_12_), channel_id=1, source_target_pairs={{0,2},{1,3},{2,0},{3,1},{4,6},{5,7},{6,4},{7,5},{8,10},{9,11},{10,... | collective-permute-start | bytes 700424 | tf_op jit(solution)/shard_map/ppermute | solution.py:121
  27.4 0.2 collective-permute-start.5
  27.6 1.1 %collective-permute-start.1 = (bf16[912,128]{1,0:T(8,128)(2,1)}, bf16[912,128]{1,0:T(8,128)(2,1)S(1)}, u32[]{:S(2)}, u32[]{:S(2)}) collective-permute-start(bf16[912,128]{1,0:T(8,128)(2,1)} %get-tuple-element.23.refs_0_), channel_id=1, source_target_pairs={{0,1},{1,0},{2,3},{3,2},{4,5},{5,4},{6,7},{7,6},{8,9},{9,8},{10,11... | collective-permute-start | bytes 700424 | tf_op jit(solution)/shard_map/ppermute | solution.py:121
  28.7 0.1 collective-permute-start.2
  28.7 0.4 collective-permute-start.11
  29.2 3.7 %collective-permute-done.13.refs_14_ = bf16[912,128]{1,0:T(8,128)(2,1)S(1)} collective-permute-done((bf16[912,128]{1,0:T(8,128)(2,1)S(1)}, bf16[912,128]{1,0:T(8,128)(2,1)S(1)}, u32[]{:S(2)}, u32[]{:S(2)}) %collective-permute-start.13) | collective-permute-done | bytes 233504 | tf_op jit(solution)/shard_map/ppermute | solution.py:121
  32.9 2.3 %collective-permute-start.4 = (bf16[912,128]{1,0:T(8,128)(2,1)S(1)}, bf16[912,128]{1,0:T(8,128)(2,1)S(1)}, u32[]{:S(2)}, u32[]{:S(2)}) collective-permute-start(bf16[912,128]{1,0:T(8,128)(2,1)S(1)} %collective-permute-done.3.refs_0_.refs_4_), channel_id=1, source_target_pairs={{0,1},{1,0},{2,3},{3,2},{4,5},{5,4},{6,7},{7,6},{8,9},{9,8},{10,11... | collective-permute-start | bytes 700424 | tf_op jit(solution)/shard_map/ppermute | solution.py:121
  35.2 2.7 %collective-permute-done.5.refs_2_.refs_6_ = bf16[912,128]{1,0:T(8,128)(2,1)S(1)} collective-permute-done((bf16[912,128]{1,0:T(8,128)(2,1)S(1)}, bf16[912,128]{1,0:T(8,128)(2,1)S(1)}, u32[]{:S(2)}, u32[]{:S(2)}) %collective-permute-start.5) | collective-permute-done | bytes 233504 | tf_op jit(solution)/shard_map/ppermute | solution.py:121
  37.9 1.3 %collective-permute-start.12 = (bf16[912,128]{1,0:T(8,128)(2,1)S(1)}, bf16[912,128]{1,0:T(8,128)(2,1)}, u32[]{:S(2)}, u32[]{:S(2)}) collective-permute-start(bf16[912,128]{1,0:T(8,128)(2,1)S(1)} %collective-permute-done.10.refs_12_), channel_id=1, source_target_pairs={{0,1},{1,0},{2,3},{3,2},{4,5},{5,4},{6,7},{7,6},{8,9},{9,8},{10,11... | collective-permute-start | bytes 700424 | tf_op jit(solution)/shard_map/ppermute | solution.py:121
  39.2 0.0 collective-permute-done.1.refs_1_
  39.3 0.1 collective-permute-start.8
  39.3 0.4 collective-permute-start.7
  39.8 0.1 collective-permute-start.14
  39.9 0.1 copy-done.12
  39.9 0.1 copy-done.14
  40.0 2.6 %early.3 = (bf16[4,128,128]{2,1,0:T(8,128)(2,1)}, f32[32,768]{1,0:T(8,128)}) custom-call(s32[1]{0:T(128)} %bitcast.me_ref, bf16[128,768]{1,0:T(8,128)(2,1)} %get-tuple-element.20.masked_ref, bf16[912,128]{1,0:T(8,128)(2,1)} %get-tuple-element.23.refs_0_, bf16[912,128]{1,0:T(8,128)(2,1)} %copy-done.12, bf16[912,128]{1,0:T(8,128)(2,1)} %copy-done.6, ...), custom_call_target="tpu_custom_call" | custom-call | tf_op jit(solution)/shard_map/early/pallas_call | solution.py:161
  42.6 0.0 collective-permute-done.8.refs_1_.refs_9_
  42.7 0.7 %copy-done.20 = bf16[912,128]{1,0:T(8,128)(2,1)} copy-done((bf16[912,128]{1,0:T(8,128)(2,1)}, bf16[912,128]{1,0:T(8,128)(2,1)S(1)}, u32[]{:S(2)}) %copy-start.20) | copy-done | bytes 233496
  43.3 2.6 %early.5 = (bf16[4,128,128]{2,1,0:T(8,128)(2,1)}, f32[32,768]{1,0:T(8,128)}) custom-call(s32[1]{0:T(128)} %bitcast.me_ref, bf16[128,768]{1,0:T(8,128)(2,1)} %get-tuple-element.20.masked_ref, bf16[912,128]{1,0:T(8,128)(2,1)} %copy-done.2, bf16[912,128]{1,0:T(8,128)(2,1)} %copy-done.20, bf16[912,128]{1,0:T(8,128)(2,1)} %copy-done.8, bf16[912,128]{1,0:T(8,128)(2,1)} %copy-done.16), custom_call_target="tpu_custom_call" | custom-call | tf_op jit(solution)/shard_map/early/pallas_call | solution.py:161
  46.0 0.0 copy-start.1
  46.1 0.7 %copy-done.18 = bf16[912,128]{1,0:T(8,128)(2,1)} copy-done((bf16[912,128]{1,0:T(8,128)(2,1)}, bf16[912,128]{1,0:T(8,128)(2,1)S(1)}, u32[]{:S(2)}) %copy-start.18) | copy-done | bytes 233496
  46.7 0.7 %copy-done.22 = bf16[912,128]{1,0:T(8,128)(2,1)} copy-done((bf16[912,128]{1,0:T(8,128)(2,1)}, bf16[912,128]{1,0:T(8,128)(2,1)S(1)}, u32[]{:S(2)}) %copy-start.22) | copy-done | bytes 233496
  47.4 2.6 %early.4 = (bf16[4,128,128]{2,1,0:T(8,128)(2,1)}, f32[32,768]{1,0:T(8,128)}) custom-call(s32[1]{0:T(128)} %bitcast.me_ref, bf16[128,768]{1,0:T(8,128)(2,1)} %get-tuple-element.20.masked_ref, bf16[912,128]{1,0:T(8,128)(2,1)} %copy-done.4, bf16[912,128]{1,0:T(8,128)(2,1)} %copy-done.18, bf16[912,128]{1,0:T(8,128)(2,1)} %copy-done.10, bf16[912,128]{1,0:T(8,128)(2,1)} %copy-done.22), custom_call_target="tpu_custom_call" | custom-call | tf_op jit(solution)/shard_map/early/pallas_call | solution.py:161
  50.0 0.0 collective-permute-done.12.refs_13_
  50.0 0.0 collective-permute-done.14.refs_15_
  50.0 0.0 copy-start.30
  50.0 0.0 copy-start.31
  50.1 0.6 copy-done.30
  50.7 0.9 %copy-done.11 = bf16[912,128]{1,0:T(8,128)(2,1)S(1)} copy-done((bf16[912,128]{1,0:T(8,128)(2,1)S(1)}, bf16[912,128]{1,0:T(8,128)(2,1)}, u32[]{:S(2)}) %copy-start.11) | copy-done | bytes 233496
  51.6 0.9 %copy-done.17 = bf16[912,128]{1,0:T(8,128)(2,1)S(1)} copy-done((bf16[912,128]{1,0:T(8,128)(2,1)S(1)}, bf16[912,128]{1,0:T(8,128)(2,1)}, u32[]{:S(2)}) %copy-start.17) | copy-done | bytes 233496
  52.6 0.9 %copy-done.19 = bf16[912,128]{1,0:T(8,128)(2,1)S(1)} copy-done((bf16[912,128]{1,0:T(8,128)(2,1)S(1)}, bf16[912,128]{1,0:T(8,128)(2,1)}, u32[]{:S(2)}) %copy-start.19) | copy-done | bytes 233496
  53.5 0.9 %copy-done.21 = bf16[912,128]{1,0:T(8,128)(2,1)S(1)} copy-done((bf16[912,128]{1,0:T(8,128)(2,1)S(1)}, bf16[912,128]{1,0:T(8,128)(2,1)}, u32[]{:S(2)}) %copy-start.21) | copy-done | bytes 233496
  54.5 0.9 %copy-done.23 = bf16[912,128]{1,0:T(8,128)(2,1)S(1)} copy-done((bf16[912,128]{1,0:T(8,128)(2,1)S(1)}, bf16[912,128]{1,0:T(8,128)(2,1)}, u32[]{:S(2)}) %copy-start.23) | copy-done | bytes 233496
  55.4 0.9 %copy-done.24 = bf16[4,128,128]{2,1,0:T(8,128)(2,1)S(1)} copy-done((bf16[4,128,128]{2,1,0:T(8,128)(2,1)S(1)}, bf16[4,128,128]{2,1,0:T(8,128)(2,1)}, u32[]{:S(2)}) %copy-start.24) | copy-done | bytes 131096
  56.3 0.9 %copy-done.25 = bf16[4,128,128]{2,1,0:T(8,128)(2,1)S(1)} copy-done((bf16[4,128,128]{2,1,0:T(8,128)(2,1)S(1)}, bf16[4,128,128]{2,1,0:T(8,128)(2,1)}, u32[]{:S(2)}) %copy-start.25) | copy-done | bytes 131096
  57.2 0.9 %copy-done.26 = bf16[4,128,128]{2,1,0:T(8,128)(2,1)S(1)} copy-done((bf16[4,128,128]{2,1,0:T(8,128)(2,1)S(1)}, bf16[4,128,128]{2,1,0:T(8,128)(2,1)}, u32[]{:S(2)}) %copy-start.26) | copy-done | bytes 131096
  58.1 0.9 %copy-done.27 = f32[32,768]{1,0:T(8,128)S(1)} copy-done((f32[32,768]{1,0:T(8,128)S(1)}, f32[32,768]{1,0:T(8,128)}, u32[]{:S(2)}) %copy-start.27) | copy-done | bytes 98328
  59.0 0.9 %copy-done.28 = f32[32,768]{1,0:T(8,128)S(1)} copy-done((f32[32,768]{1,0:T(8,128)S(1)}, f32[32,768]{1,0:T(8,128)}, u32[]{:S(2)}) %copy-start.28) | copy-done | bytes 98328
  59.9 0.9 %copy-done.29 = f32[32,768]{1,0:T(8,128)S(1)} copy-done((f32[32,768]{1,0:T(8,128)S(1)}, f32[32,768]{1,0:T(8,128)}, u32[]{:S(2)}) %copy-start.29) | copy-done | bytes 98328
  60.8 4.3 %last.1 = (bf16[1,8,128,128]{3,2,1,0:T(8,128)(2,1)}, f32[8,128]{1,0:T(8,128)}) custom-call(s32[1]{0:T(128)} %bitcast.me_ref, s32[1,8]{1,0:T(1,128)S(1)} %copy-done.31, bf16[128,768]{1,0:T(8,128)(2,1)S(1)} %copy-done, f32[1,768]{1,0:T(1,128)S(1)} %copy-done.30, bf16[912,128]{1,0:T(8,128)(2,1)S(1)} %copy-done.1, bf16[912,128]{1,0:T(8,128)(2,1)S(1)} %copy-done.13, ...), custom_call_target="tpu_custom_call" | custom-call | tf_op jit(solution)/shard_map/last/pallas_call | solution.py:173
  (51 shorter events, 0.1 us)
Async XLA Ops:
  2.4 10.0 %collective-permute-start.6 = (bf16[912,128]{1,0:T(8,128)(2,1)}, bf16[912,128]{1,0:T(8,128)(2,1)S(1)}, u32[]{:S(2)}, u32[]{:S(2)}) collective-permute-start(bf16[912,128]{1,0:T(8,128)(2,1)} %get-tuple-element.23.refs_0_), channel_id=1, source_target_pairs={{0,8},{1,9},{2,10},{3,11},{4,12},{5,13},{6,14},{7,15},{8,0},{9,1},... | collective-permute-start | bytes 700424 | tf_op jit(solution)/shard_map/ppermute | solution.py:121
  2.4 11.7 %collective-permute-start.3 = (bf16[912,128]{1,0:T(8,128)(2,1)}, bf16[912,128]{1,0:T(8,128)(2,1)S(1)}, u32[]{:S(2)}, u32[]{:S(2)}) collective-permute-start(bf16[912,128]{1,0:T(8,128)(2,1)} %get-tuple-element.23.refs_0_), channel_id=1, source_target_pairs={{0,4},{1,5},{2,6},{3,7},{4,0},{5,1},{6,2},{7,3},{8,12},{9,13},{10,... | collective-permute-start | bytes 700424 | tf_op jit(solution)/shard_map/ppermute | solution.py:121
  3.8 22.4 %collective-permute-start.10 = (bf16[912,128]{1,0:T(8,128)(2,1)}, bf16[912,128]{1,0:T(8,128)(2,1)S(1)}, u32[]{:S(2)}, u32[]{:S(2)}) collective-permute-start(bf16[912,128]{1,0:T(8,128)(2,1)} %get-tuple-element.23.refs_0_), channel_id=1, source_target_pairs={{0,12},{1,13},{2,14},{3,15},{4,8},{5,9},{6,10},{7,11},{8,4},{9,5},... | collective-permute-start | bytes 700424 | tf_op jit(solution)/shard_map/ppermute | solution.py:121
  5.0 22.6 %collective-permute-start = (bf16[912,128]{1,0:T(8,128)(2,1)}, bf16[912,128]{1,0:T(8,128)(2,1)S(1)}, u32[]{:S(2)}, u32[]{:S(2)}) collective-permute-start(bf16[912,128]{1,0:T(8,128)(2,1)} %get-tuple-element.23.refs_0_), channel_id=1, source_target_pairs={{0,2},{1,3},{2,0},{3,1},{4,6},{5,7},{6,4},{7,5},{8,10},{9,11},{10,... | collective-permute-start | bytes 700424 | tf_op jit(solution)/shard_map/ppermute | solution.py:121
  12.4 30.2 %copy-start.2 = (bf16[912,128]{1,0:T(8,128)(2,1)}, bf16[912,128]{1,0:T(8,128)(2,1)S(1)}, u32[]{:S(2)}) copy-start(bf16[912,128]{1,0:T(8,128)(2,1)S(1)} %collective-permute-done.6.refs_0_.refs_8_) | copy-start | bytes 700420
  14.2 31.8 %copy-start.4 = (bf16[912,128]{1,0:T(8,128)(2,1)}, bf16[912,128]{1,0:T(8,128)(2,1)S(1)}, u32[]{:S(2)}) copy-start(bf16[912,128]{1,0:T(8,128)(2,1)S(1)} %collective-permute-done.3.refs_0_.refs_4_) | copy-start | bytes 700420
  14.2 14.6 %collective-permute-start.9 = (bf16[912,128]{1,0:T(8,128)(2,1)S(1)}, bf16[912,128]{1,0:T(8,128)(2,1)S(1)}, u32[]{:S(2)}, u32[]{:S(2)}) collective-permute-start(bf16[912,128]{1,0:T(8,128)(2,1)S(1)} %collective-permute-done.6.refs_0_.refs_8_), channel_id=1, source_target_pairs={{0,2},{1,3},{2,0},{3,1},{4,6},{5,7},{6,4},{7,5},{8,10},{9,11},{10,... | collective-permute-start | bytes 700424 | tf_op jit(solution)/shard_map/ppermute | solution.py:121
  26.1 6.8 %collective-permute-start.13 = (bf16[912,128]{1,0:T(8,128)(2,1)S(1)}, bf16[912,128]{1,0:T(8,128)(2,1)S(1)}, u32[]{:S(2)}, u32[]{:S(2)}) collective-permute-start(bf16[912,128]{1,0:T(8,128)(2,1)S(1)} %collective-permute-done.10.refs_12_), channel_id=1, source_target_pairs={{0,2},{1,3},{2,0},{3,1},{4,6},{5,7},{6,4},{7,5},{8,10},{9,11},{10,... | collective-permute-start | bytes 700424 | tf_op jit(solution)/shard_map/ppermute | solution.py:121
  27.4 10.5 %collective-permute-start.5 = (bf16[912,128]{1,0:T(8,128)(2,1)S(1)}, bf16[912,128]{1,0:T(8,128)(2,1)S(1)}, u32[]{:S(2)}, u32[]{:S(2)}) collective-permute-start(bf16[912,128]{1,0:T(8,128)(2,1)S(1)} %collective-permute-done.3.refs_0_.refs_4_), channel_id=1, source_target_pairs={{0,2},{1,3},{2,0},{3,1},{4,6},{5,7},{6,4},{7,5},{8,10},{9,11},{10,... | collective-permute-start | bytes 700424 | tf_op jit(solution)/shard_map/ppermute | solution.py:121
  27.6 12.3 %copy-start.6 = (bf16[912,128]{1,0:T(8,128)(2,1)}, bf16[912,128]{1,0:T(8,128)(2,1)S(1)}, u32[]{:S(2)}) copy-start(bf16[912,128]{1,0:T(8,128)(2,1)S(1)} %collective-permute-done.refs_2_) | copy-start | bytes 700420
  27.6 11.6 %collective-permute-start.1 = (bf16[912,128]{1,0:T(8,128)(2,1)}, bf16[912,128]{1,0:T(8,128)(2,1)S(1)}, u32[]{:S(2)}, u32[]{:S(2)}) collective-permute-start(bf16[912,128]{1,0:T(8,128)(2,1)} %get-tuple-element.23.refs_0_), channel_id=1, source_target_pairs={{0,1},{1,0},{2,3},{3,2},{4,5},{5,4},{6,7},{7,6},{8,9},{9,8},{10,11... | collective-permute-start | bytes 700424 | tf_op jit(solution)/shard_map/ppermute | solution.py:121
  28.7 10.7 %collective-permute-start.2 = (bf16[912,128]{1,0:T(8,128)(2,1)S(1)}, bf16[912,128]{1,0:T(8,128)(2,1)S(1)}, u32[]{:S(2)}, u32[]{:S(2)}) collective-permute-start(bf16[912,128]{1,0:T(8,128)(2,1)S(1)} %collective-permute-done.refs_2_), channel_id=1, source_target_pairs={{0,1},{1,0},{2,3},{3,2},{4,5},{5,4},{6,7},{7,6},{8,9},{9,8},{10,11... | collective-permute-start | bytes 700424 | tf_op jit(solution)/shard_map/ppermute | solution.py:121
  28.7 13.9 %copy-start.8 = (bf16[912,128]{1,0:T(8,128)(2,1)}, bf16[912,128]{1,0:T(8,128)(2,1)S(1)}, u32[]{:S(2)}) copy-start(bf16[912,128]{1,0:T(8,128)(2,1)S(1)} %collective-permute-done.9.refs_2_.refs_10_) | copy-start | bytes 700420
  28.7 11.0 %collective-permute-start.11 = (bf16[912,128]{1,0:T(8,128)(2,1)S(1)}, bf16[912,128]{1,0:T(8,128)(2,1)S(1)}, u32[]{:S(2)}, u32[]{:S(2)}) collective-permute-start(bf16[912,128]{1,0:T(8,128)(2,1)S(1)} %collective-permute-done.9.refs_2_.refs_10_), channel_id=1, source_target_pairs={{0,1},{1,0},{2,3},{3,2},{4,5},{5,4},{6,7},{7,6},{8,9},{9,8},{10,11... | collective-permute-start | bytes 700424 | tf_op jit(solution)/shard_map/ppermute | solution.py:121
  32.9 13.1 %collective-permute-start.4 = (bf16[912,128]{1,0:T(8,128)(2,1)S(1)}, bf16[912,128]{1,0:T(8,128)(2,1)S(1)}, u32[]{:S(2)}, u32[]{:S(2)}) collective-permute-start(bf16[912,128]{1,0:T(8,128)(2,1)S(1)} %collective-permute-done.3.refs_0_.refs_4_), channel_id=1, source_target_pairs={{0,1},{1,0},{2,3},{3,2},{4,5},{5,4},{6,7},{7,6},{8,9},{9,8},{10,11... | collective-permute-start | bytes 700424 | tf_op jit(solution)/shard_map/ppermute | solution.py:121
  37.9 8.1 %copy-start.10 = (bf16[912,128]{1,0:T(8,128)(2,1)}, bf16[912,128]{1,0:T(8,128)(2,1)S(1)}, u32[]{:S(2)}) copy-start(bf16[912,128]{1,0:T(8,128)(2,1)S(1)} %collective-permute-done.5.refs_2_.refs_6_) | copy-start | bytes 700420
  37.9 12.1 %collective-permute-start.12 = (bf16[912,128]{1,0:T(8,128)(2,1)S(1)}, bf16[912,128]{1,0:T(8,128)(2,1)}, u32[]{:S(2)}, u32[]{:S(2)}) collective-permute-start(bf16[912,128]{1,0:T(8,128)(2,1)S(1)} %collective-permute-done.10.refs_12_), channel_id=1, source_target_pairs={{0,1},{1,0},{2,3},{3,2},{4,5},{5,4},{6,7},{7,6},{8,9},{9,8},{10,11... | collective-permute-start | bytes 700424 | tf_op jit(solution)/shard_map/ppermute | solution.py:121
  39.2 0.7 %copy-start.12 = (bf16[912,128]{1,0:T(8,128)(2,1)}, bf16[912,128]{1,0:T(8,128)(2,1)S(1)}, u32[]{:S(2)}) copy-start(bf16[912,128]{1,0:T(8,128)(2,1)S(1)} %collective-permute-done.1.refs_1_) | copy-start | bytes 700420
  39.3 3.4 %collective-permute-start.8 = (bf16[912,128]{1,0:T(8,128)(2,1)S(1)}, bf16[912,128]{1,0:T(8,128)(2,1)S(1)}, u32[]{:S(2)}, u32[]{:S(2)}) collective-permute-start(bf16[912,128]{1,0:T(8,128)(2,1)S(1)} %collective-permute-done.6.refs_0_.refs_8_), channel_id=1, source_target_pairs={{0,1},{1,0},{2,3},{3,2},{4,5},{5,4},{6,7},{7,6},{8,9},{9,8},{10,11... | collective-permute-start | bytes 700424 | tf_op jit(solution)/shard_map/ppermute | solution.py:121
  39.3 0.7 %copy-start.14 = (bf16[912,128]{1,0:T(8,128)(2,1)}, bf16[912,128]{1,0:T(8,128)(2,1)S(1)}, u32[]{:S(2)}) copy-start(bf16[912,128]{1,0:T(8,128)(2,1)S(1)} %collective-permute-done.2.refs_3_) | copy-start | bytes 700420
  39.3 6.7 %collective-permute-start.7 = (bf16[912,128]{1,0:T(8,128)(2,1)S(1)}, bf16[912,128]{1,0:T(8,128)(2,1)S(1)}, u32[]{:S(2)}, u32[]{:S(2)}) collective-permute-start(bf16[912,128]{1,0:T(8,128)(2,1)S(1)} %collective-permute-done.5.refs_2_.refs_6_), channel_id=1, source_target_pairs={{0,1},{1,0},{2,3},{3,2},{4,5},{5,4},{6,7},{7,6},{8,9},{9,8},{10,11... | collective-permute-start | bytes 700424 | tf_op jit(solution)/shard_map/ppermute | solution.py:121
  39.8 2.9 %copy-start.16 = (bf16[912,128]{1,0:T(8,128)(2,1)}, bf16[912,128]{1,0:T(8,128)(2,1)S(1)}, u32[]{:S(2)}) copy-start(bf16[912,128]{1,0:T(8,128)(2,1)S(1)} %collective-permute-done.11.refs_3_.refs_11_) | copy-start | bytes 700420
  39.8 10.2 %collective-permute-start.14 = (bf16[912,128]{1,0:T(8,128)(2,1)S(1)}, bf16[912,128]{1,0:T(8,128)(2,1)}, u32[]{:S(2)}, u32[]{:S(2)}) collective-permute-start(bf16[912,128]{1,0:T(8,128)(2,1)S(1)} %collective-permute-done.13.refs_14_), channel_id=1, source_target_pairs={{0,1},{1,0},{2,3},{3,2},{4,5},{5,4},{6,7},{7,6},{8,9},{9,8},{10,11... | collective-permute-start | bytes 700424 | tf_op jit(solution)/shard_map/ppermute | solution.py:121
  42.6 0.7 %copy-start.20 = (bf16[912,128]{1,0:T(8,128)(2,1)}, bf16[912,128]{1,0:T(8,128)(2,1)S(1)}, u32[]{:S(2)}) copy-start(bf16[912,128]{1,0:T(8,128)(2,1)S(1)} %collective-permute-done.8.refs_1_.refs_9_) | copy-start | bytes 700420
  43.3 6.7 %copy-start.9 = (bf16[912,128]{1,0:T(8,128)(2,1)S(1)}, bf16[912,128]{1,0:T(8,128)(2,1)}, u32[]{:S(2)}) copy-start(bf16[912,128]{1,0:T(8,128)(2,1)} %copy-done.8) | copy-start | bytes 700420
  43.3 6.7 %copy-start.13 = (bf16[912,128]{1,0:T(8,128)(2,1)S(1)}, bf16[912,128]{1,0:T(8,128)(2,1)}, u32[]{:S(2)}) copy-start(bf16[912,128]{1,0:T(8,128)(2,1)} %copy-done.12) | copy-start | bytes 700420
  43.3 6.7 %copy-start.15 = (bf16[912,128]{1,0:T(8,128)(2,1)S(1)}, bf16[912,128]{1,0:T(8,128)(2,1)}, u32[]{:S(2)}) copy-start(bf16[912,128]{1,0:T(8,128)(2,1)} %copy-done.14) | copy-start | bytes 700420
  46.0 4.1 %copy-start = (bf16[128,768]{1,0:T(8,128)(2,1)S(1)}, bf16[128,768]{1,0:T(8,128)(2,1)}, u32[]{:S(2)}) copy-start(bf16[128,768]{1,0:T(8,128)(2,1)} %get-tuple-element.20.masked_ref) | copy-start | bytes 589828
  46.0 4.1 %copy-start.1 = (bf16[912,128]{1,0:T(8,128)(2,1)S(1)}, bf16[912,128]{1,0:T(8,128)(2,1)}, u32[]{:S(2)}) copy-start(bf16[912,128]{1,0:T(8,128)(2,1)} %get-tuple-element.23.refs_0_) | copy-start | bytes 700420
  46.0 4.1 %copy-start.3 = (bf16[912,128]{1,0:T(8,128)(2,1)S(1)}, bf16[912,128]{1,0:T(8,128)(2,1)}, u32[]{:S(2)}) copy-start(bf16[912,128]{1,0:T(8,128)(2,1)} %copy-done.2) | copy-start | bytes 700420
  46.0 4.1 %copy-start.7 = (bf16[912,128]{1,0:T(8,128)(2,1)S(1)}, bf16[912,128]{1,0:T(8,128)(2,1)}, u32[]{:S(2)}) copy-start(bf16[912,128]{1,0:T(8,128)(2,1)} %copy-done.6) | copy-start | bytes 700420
  46.0 0.7 %copy-start.18 = (bf16[912,128]{1,0:T(8,128)(2,1)}, bf16[912,128]{1,0:T(8,128)(2,1)S(1)}, u32[]{:S(2)}) copy-start(bf16[912,128]{1,0:T(8,128)(2,1)S(1)} %collective-permute-done.4.refs_1_.refs_5_) | copy-start | bytes 700420
  46.0 4.1 %copy-start.5 = (bf16[912,128]{1,0:T(8,128)(2,1)S(1)}, bf16[912,128]{1,0:T(8,128)(2,1)}, u32[]{:S(2)}) copy-start(bf16[912,128]{1,0:T(8,128)(2,1)} %copy-done.4) | copy-start | bytes 700420
  46.7 0.7 %copy-start.22 = (bf16[912,128]{1,0:T(8,128)(2,1)}, bf16[912,128]{1,0:T(8,128)(2,1)S(1)}, u32[]{:S(2)}) copy-start(bf16[912,128]{1,0:T(8,128)(2,1)S(1)} %collective-permute-done.7.refs_3_.refs_7_) | copy-start | bytes 700420
  50.0 0.7 %copy-start.30 = (f32[1,768]{1,0:T(1,128)S(1)}, f32[1,768]{1,0:T(1,128)}, u32[]{:S(2)}) copy-start(f32[1,768]{1,0:T(1,128)} %get-tuple-element.21.tau_ref) | copy-start | bytes 9220
  50.0 0.7 %copy-start.31 = (s32[1,8]{1,0:T(1,128)S(1)}, s32[1,8]{1,0:T(1,128)}, u32[]{:S(2)}) copy-start(s32[1,8]{1,0:T(1,128)} %dest_ref.3) | copy-start | bytes 100
  50.7 0.9 %copy-start.11 = (bf16[912,128]{1,0:T(8,128)(2,1)S(1)}, bf16[912,128]{1,0:T(8,128)(2,1)}, u32[]{:S(2)}) copy-start(bf16[912,128]{1,0:T(8,128)(2,1)} %copy-done.10) | copy-start | bytes 700420
  51.6 0.9 %copy-start.17 = (bf16[912,128]{1,0:T(8,128)(2,1)S(1)}, bf16[912,128]{1,0:T(8,128)(2,1)}, u32[]{:S(2)}) copy-start(bf16[912,128]{1,0:T(8,128)(2,1)} %copy-done.16) | copy-start | bytes 700420
  52.6 0.9 %copy-start.19 = (bf16[912,128]{1,0:T(8,128)(2,1)S(1)}, bf16[912,128]{1,0:T(8,128)(2,1)}, u32[]{:S(2)}) copy-start(bf16[912,128]{1,0:T(8,128)(2,1)} %copy-done.18) | copy-start | bytes 700420
  53.5 0.9 %copy-start.21 = (bf16[912,128]{1,0:T(8,128)(2,1)S(1)}, bf16[912,128]{1,0:T(8,128)(2,1)}, u32[]{:S(2)}) copy-start(bf16[912,128]{1,0:T(8,128)(2,1)} %copy-done.20) | copy-start | bytes 700420
  54.5 0.9 %copy-start.23 = (bf16[912,128]{1,0:T(8,128)(2,1)S(1)}, bf16[912,128]{1,0:T(8,128)(2,1)}, u32[]{:S(2)}) copy-start(bf16[912,128]{1,0:T(8,128)(2,1)} %copy-done.22) | copy-start | bytes 700420
  55.4 0.9 %copy-start.24 = (bf16[4,128,128]{2,1,0:T(8,128)(2,1)S(1)}, bf16[4,128,128]{2,1,0:T(8,128)(2,1)}, u32[]{:S(2)}) copy-start(bf16[4,128,128]{2,1,0:T(8,128)(2,1)} %get-tuple-element.32.refs_16_) | copy-start | bytes 393220
  56.3 0.9 %copy-start.25 = (bf16[4,128,128]{2,1,0:T(8,128)(2,1)S(1)}, bf16[4,128,128]{2,1,0:T(8,128)(2,1)}, u32[]{:S(2)}) copy-start(bf16[4,128,128]{2,1,0:T(8,128)(2,1)} %get-tuple-element.34.refs_18_) | copy-start | bytes 393220
  57.2 0.9 %copy-start.26 = (bf16[4,128,128]{2,1,0:T(8,128)(2,1)S(1)}, bf16[4,128,128]{2,1,0:T(8,128)(2,1)}, u32[]{:S(2)}) copy-start(bf16[4,128,128]{2,1,0:T(8,128)(2,1)} %get-tuple-element.33.refs_17_) | copy-start | bytes 393220
  58.1 0.9 %copy-start.27 = (f32[32,768]{1,0:T(8,128)S(1)}, f32[32,768]{1,0:T(8,128)}, u32[]{:S(2)}) copy-start(f32[32,768]{1,0:T(8,128)} %get-tuple-element.35.refs_19_) | copy-start | bytes 294916
  59.0 0.9 %copy-start.28 = (f32[32,768]{1,0:T(8,128)S(1)}, f32[32,768]{1,0:T(8,128)}, u32[]{:S(2)}) copy-start(f32[32,768]{1,0:T(8,128)} %get-tuple-element.37.refs_21_) | copy-start | bytes 294916
  59.9 0.9 %copy-start.29 = (f32[32,768]{1,0:T(8,128)S(1)}, f32[32,768]{1,0:T(8,128)}, u32[]{:S(2)}) copy-start(f32[32,768]{1,0:T(8,128)} %get-tuple-element.36.refs_20_) | copy-start | bytes 294916

commit v3 on v2

v3 whole, which is shorter than its diff:
```python
import functools

import jax
import jax.numpy as jnp
from jax import lax
from jax.experimental import pallas as pl
from jax.experimental.pallas import tpu as pltpu
from jax.sharding import PartitionSpec as P

BLOCK = 128
LIST_ROWS = 16
LAYER = 4
MIB = 1 << 20
NT_DIMS = (((1,), (1,)), ((), ()))
NN_DIMS = (((1,), (0,)), ((), ()))


def dot(a, b, dims=NN_DIMS):
    return lax.dot_general(a, b, dims, preferred_element_type=jnp.float32)


def split(x):
    high = x.astype(jnp.bfloat16)
    return high, (x - high.astype(jnp.float32)).astype(jnp.bfloat16)


def pack_kernel(
    mask_hbm, dest_hbm, rows_hbm, tau_hbm, metric_hbm, piece_ref, mask_ref, dest_ref, rows_ref, tau_ref, sems
):
    tiles = mask_ref.shape[1]
    depth = tiles * BLOCK
    moves = [
        (rows_hbm, rows_ref),
        (tau_hbm, tau_ref),
        (mask_hbm, mask_ref),
        (dest_hbm, dest_ref),
        (metric_hbm, piece_ref.at[depth : depth + BLOCK]),
    ]
    copies = [pltpu.make_async_copy(source, target, sems.at[k]) for k, (source, target) in enumerate(moves)]
    for copy in copies:
        copy.start()
    for copy in copies:
        copy.wait()
    tau = tau_ref[...].reshape(1, depth)
    for t in range(tiles):
        cols = slice(t * BLOCK, (t + 1) * BLOCK)
        weight = tau[:, cols] * mask_ref[0, t].astype(jnp.float32)
        piece_ref[cols, :] = (rows_ref[:, cols].astype(jnp.float32) * weight).astype(jnp.bfloat16)
    lane = lax.broadcasted_iota(jnp.int32, (LIST_ROWS, BLOCK), 1)
    listed = jnp.zeros((LIST_ROWS, BLOCK), jnp.float32)
    for j in range(dest_ref.shape[1]):
        listed += (lane == dest_ref[0, j]).astype(jnp.float32)
    piece_ref[depth + BLOCK :, :] = listed.astype(jnp.bfloat16)


def local_kernel(mask_ref, rows_ref, tau_ref, masked_ref, row_ref):
    row_ref[...] = tau_ref[...].reshape(row_ref.shape)
    for t in range(mask_ref.shape[1]):
        cols = slice(t * BLOCK, (t + 1) * BLOCK)
        masked_ref[:, cols] = rows_ref[:, cols] * mask_ref[0, t].astype(jnp.bfloat16)


def scaled_of(piece):
    depth = piece.shape[0] - BLOCK - LIST_ROWS
    return jnp.concatenate([piece[t : t + BLOCK, :] for t in range(0, depth, BLOCK)], axis=1)


def metric_of(piece):
    depth = piece.shape[0] - BLOCK - LIST_ROWS
    return piece[depth : depth + BLOCK, :]


def blocks_of(me, masked, pieces, strips, windows):
    rows = windows[0].shape[0]
    lane = lax.broadcasted_iota(jnp.int32, (rows, BLOCK), 1)
    row = lax.broadcasted_iota(jnp.int32, (rows, BLOCK), 0)
    pick = (lane == row + me * rows).astype(jnp.bfloat16)
    own = [dot(pick, metric_of(piece), NT_DIMS).astype(jnp.bfloat16) for piece in pieces]
    for k, piece in enumerate(pieces):
        scaled = scaled_of(piece)
        windows[k][...] = dot(own[k], scaled)
        strips[k][...] = dot(masked, scaled, NT_DIMS).astype(jnp.bfloat16)


def early_kernel(me_ref, masked_ref, *refs):
    strips, windows = refs[-2:]
    count = strips.shape[0]
    blocks_of(
        me_ref[0],
        masked_ref[...],
        refs[:-2],
        [strips.at[k] for k in range(count)],
        [windows.at[k] for k in range(count)],
    )


def last_kernel(devices, groups, me_ref, dest_hbm, masked_ref, tau_ref, *refs):
    pieces = refs[:devices]
    early = refs[devices : devices + 2 * len(groups)]
    chi_ref, sand_ref, strips, window, listed, dest_ref, sems, dest_sem = refs[devices + 2 * len(groups) :]
    fetch = pltpu.make_async_copy(dest_hbm, dest_ref, dest_sem)
    fetch.start()
    me = me_ref[0]
    rows = BLOCK // devices
    fanout = dest_ref.shape[1]
    late = [m for m in range(devices) if all(m not in group for group in groups)]
    blocks_of(
        me,
        masked_ref[...],
        [pieces[m] for m in late],
        [strips.at[m] for m in late],
        [window.at[m * rows : (m + 1) * rows] for m in late],
    )
    for group, strip, part in zip(groups, early[::2], early[1::2]):
        for k, m in enumerate(group):
            strips[m] = strip[k]
            window[m * rows : (m + 1) * rows, :] = part[k]
    fetch.wait()
    copies = [
        pltpu.make_async_copy(strips.at[dest_ref[0, j] ^ me], chi_ref.at[0, j], sems.at[j])
        for j in range(fanout)
    ]
    for copy in copies:
        copy.start()

    for m in range(devices):
        entry = pieces[m][pieces[m].shape[0] - LIST_ROWS :, :].astype(jnp.float32)
        listed[m * rows : (m + 1) * rows, :] = entry[:rows, :]
    row = lax.broadcasted_iota(jnp.int32, (BLOCK, BLOCK), 0)
    column = lax.broadcasted_iota(jnp.int32, (BLOCK, BLOCK), 1)
    by_piece = (row == (column // rows ^ me)).astype(jnp.bfloat16)
    routes = dot(listed[...].astype(jnp.bfloat16), by_piece)
    same = row % rows == column % rows
    pair = jnp.where(same, routes + routes.T, 0.0).astype(jnp.bfloat16)
    mixed = dot(jnp.concatenate([pair, pair], axis=1), jnp.concatenate(split(window[...]), axis=0))
    high, low = split(mixed / tau_ref[...])
    sides = []
    for m in range(devices):
        part = slice(m * rows, (m + 1) * rows)
        side = dot(jnp.concatenate([high[part], low[part]], axis=0), scaled_of(pieces[m]), NT_DIMS)
        sides.append(side[:rows] + side[rows:])
    total = jnp.zeros((2 * rows, BLOCK), jnp.float32)
    for m in range(devices):
        total += dot(jnp.concatenate(split(sides[m]), axis=0), metric_of(pieces[m]))
    sand_ref[...] = total[:rows] + total[rows:]
    for copy in copies:
        copy.wait()


def after(value, *others):
    return lax.optimization_barrier((value, others))[0]


def body(three_center, tau_weights, tile_mask, dest, metric_half):
    devices = lax.axis_size("row")
    local_rows, contracted = three_center.shape
    fanout = dest.shape[1]
    rows = BLOCK // devices
    piece_rows = contracted + BLOCK + LIST_ROWS
    smem = pl.BlockSpec(memory_space=pltpu.SMEM)
    vmem = pl.BlockSpec(memory_space=pltpu.VMEM)
    hbm = pl.BlockSpec(memory_space=pltpu.HBM)
    own = pl.pallas_call(
        pack_kernel,
        out_shape=jax.ShapeDtypeStruct((piece_rows, BLOCK), jnp.bfloat16),
        in_specs=[hbm] * 5,
        out_specs=vmem,
        scratch_shapes=[
            pltpu.SMEM(tile_mask.shape, jnp.int32),
            pltpu.SMEM(dest.shape, jnp.int32),
            pltpu.VMEM(three_center.shape, jnp.bfloat16),
            pltpu.VMEM(tau_weights.shape, jnp.float32),
            pltpu.SemaphoreType.DMA((5,)),
        ],
        compiler_params=pltpu.CompilerParams(vmem_limit_bytes=56 * MIB),
        cost_estimate=pl.CostEstimate(flops=0, bytes_accessed=MIB, transcendentals=0),
        name="pack",
    )(tile_mask, dest, three_center, tau_weights, metric_half)
    masked, tau = pl.pallas_call(
        local_kernel,
        out_shape=(
            jax.ShapeDtypeStruct((local_rows, contracted), jnp.bfloat16),
            jax.ShapeDtypeStruct((1, contracted), jnp.float32),
        ),
        in_specs=[smem, vmem, vmem],
        out_specs=(vmem, vmem),
        compiler_params=pltpu.CompilerParams(vmem_limit_bytes=4 * MIB),
        cost_estimate=pl.CostEstimate(flops=0, bytes_accessed=MIB, transcendentals=0),
        name="local",
    )(*after((tile_mask, three_center, tau_weights), own))
    me = lax.axis_index("row").astype(jnp.int32).reshape(1)

    def early(group):
        return pl.pallas_call(
            early_kernel,
            out_shape=(
                jax.ShapeDtypeStruct((len(group), BLOCK, BLOCK), jnp.bfloat16),
                jax.ShapeDtypeStruct((len(group), rows, contracted), jnp.float32),
            ),
            in_specs=[smem] + [vmem] * (1 + len(group)),
            out_specs=(vmem, vmem),
            compiler_params=pltpu.CompilerParams(vmem_limit_bytes=8 * MIB),
            cost_estimate=pl.CostEstimate(flops=0, bytes_accessed=MIB, transcendentals=0),
            name="early",
        )(me, masked, *[got[m] for m in group])

    def swap(piece, mask):
        return lax.ppermute(piece, "row", [(i, i ^ mask) for i in range(devices)])

    far = list(range(LAYER, devices, LAYER))
    near, last = far[0], far[-1]
    got = {0: own}
    for mask in far[1:-1] + [near]:
        got[mask] = swap(own, mask)
    got[2], got[near + 2], got[1] = swap(own, 2), swap(own, near + 2), swap(own, 1)
    got[last] = swap(after(own, got[near], got[1]), last)
    for mask in far[1:-1]:
        got[mask + 2] = swap(after(got[mask], got[near]), 2)
    got[last + 2] = swap(after(got[last], got[near + 2], [got[m + 2] for m in far[1:-1]]), 2)
    got[3] = swap(after(got[2], got[near]), 1)
    for mask in far[:-1]:
        got[mask + 1] = swap(after(got[mask], got[far[1]]), 1)
    got[near + 3] = swap(after(got[near + 2], got[far[1]]), 1)
    for mask in far[1:-1]:
        got[mask + 3] = swap(after(got[mask + 2], got[last]), 1)
    got[last + 1] = swap(after(got[last], [got[m + 2] for m in far[1:-1]]), 1)
    forwarded = [mask + 2 for mask in far[1:-1]]
    first = [m for m in range(last) if m not in forwarded and m - 1 not in forwarded]
    second = [m for m in range(last + 2) if m not in first]
    groups = [first, second]
    masked, tau = after((masked, tau), got[last])
    results = [early(first), early(second)]
    got[last + 3] = swap(after(got[last + 2], results), 1)
    pieces = [got[m] for m in range(devices)]
    return pl.pallas_call(
        functools.partial(last_kernel, devices, groups),
        out_shape=(
            jax.ShapeDtypeStruct((1, fanout, BLOCK, BLOCK), jnp.bfloat16),
            jax.ShapeDtypeStruct((rows, BLOCK), jnp.float32),
        ),
        in_specs=[smem, hbm] + [vmem] * (2 + devices + 2 * len(groups)),
        out_specs=(hbm, vmem),
        scratch_shapes=[
            pltpu.VMEM((devices, BLOCK, BLOCK), jnp.bfloat16),
            pltpu.VMEM((BLOCK, contracted), jnp.float32),
            pltpu.VMEM((BLOCK, BLOCK), jnp.float32),
            pltpu.SMEM(dest.shape, jnp.int32),
            pltpu.SemaphoreType.DMA((fanout,)),
            pltpu.SemaphoreType.DMA,
        ],
        compiler_params=pltpu.CompilerParams(vmem_limit_bytes=24 * MIB),
        cost_estimate=pl.CostEstimate(flops=0, bytes_accessed=MIB, transcendentals=0),
        name="last",
    )(me, dest, masked, tau, *pieces, *[part for result in results for part in result])


def solution(mesh):
    return jax.shard_map(
        body,
        mesh=mesh,
        in_specs=(
            P(("groups", "row"), None),
            P("groups"),
            P("row", None),
            P("row", None),
            P("row", None),
        ),
        out_specs=(P(("groups", "row"), None, None, None), P(("groups", "row"), None)),
        check_vma=False,
    )
```

time: 65.7 us -> 43.1 us (0.66)
  the two profiles are of different devices: /device:TPU:17 before, /device:TPU:0 now
where the time goes in v3:
time: 43.1 us; the launch traced here: 42.9 us
  waiting for transfers between devices  18.5 us (43%)
  starting transfers between devices  14.7 us (34%)
  Pallas kernels  7.37 us (17%)
  local copies, waits for them, and re-layouts  1.61 us (4%)
  between operations  0.74 us (2%)
    ppermute x15, waiting for transfers between devices, swap(): return lax.ppermute(piece, 'row', [(i, i ^ mask) for i in range(devices)])  18.5 us
    ppermute x15, starting transfers between devices, swap(): return lax.ppermute(piece, 'row', [(i, i ^ mask) for i in range(devices)])  14.7 us
    pallas_call x1, Pallas kernels, body(): pl.pallas_call(functools.partial(last_kernel, devices, groups), out_shape...  3.24 us
    pallas_call x1, Pallas kernels, body(): pl.pallas_call(pack_kernel, out_shape=jax.ShapeDtypeStruct((piece_rows, B...  1.79 us
    pallas_call x2, Pallas kernels, early(): pl.pallas_call(early_kernel, out_shape=(jax.ShapeDtypeStruct((len(group),...  1.76 us
    unnamed x12, local copies, waits for them, and re-layouts  1.61 us
  transfers between devices with their start and end apart: 15, of which 5 were waited for; matrix products, arithmetic and copies ran while one was open for 0% of the time, Pallas kernels for 5%

profile of v3, /device:TPU:0, one launch (start us, length us, event | category | flops | bytes accessed | tf_op | source)
XLA Modules:
  0.0 42.9 jit_solution(4964239622313284895)
XLA Ops:
  0.6 0.0 copy-start.2
  0.6 1.8 %pack.1.refs_0_ = bf16[912,128]{1,0:T(8,128)(2,1)} custom-call(s32[1,6]{1,0:T(1,128)} %mask_ref, s32[1,8]{1,0:T(1,128)} %dest_hbm.3, bf16[128,768]{1,0:T(8,128)(2,1)} %rows_ref, f32[768]{0:T(1024)} %tau_ref, bf16[128,128]{1,0:T(8,128)(2,1)} %metric_hbm.1), custom_call_target="tpu_custom_call" | custom-call | bytes 1048576 | tf_op jit(solution)/shard_map/pack/pallas_call | solution.py:163
  2.4 0.0 copy-start.3
  2.4 0.5 %collective-permute-start.1 = (bf16[912,128]{1,0:T(8,128)(2,1)}, bf16[912,128]{1,0:T(8,128)(2,1)S(1)}, u32[]{:S(2)}, u32[]{:S(2)}) collective-permute-start(bf16[912,128]{1,0:T(8,128)(2,1)} %pack.1.refs_0_), channel_id=1, source_target_pairs={{0,1},{1,0},{2,3},{3,2},{4,5},{5,4},{6,7},{7,6},{8,9},{9,8},{10,11... | collective-permute-start | bytes 700424 | tf_op jit(solution)/shard_map/ppermute | solution.py:208
  3.0 2.6 %collective-permute-start = (bf16[912,128]{1,0:T(8,128)(2,1)}, bf16[912,128]{1,0:T(8,128)(2,1)S(1)}, u32[]{:S(2)}, u32[]{:S(2)}) collective-permute-start(bf16[912,128]{1,0:T(8,128)(2,1)} %pack.1.refs_0_), channel_id=1, source_target_pairs={{0,4},{1,5},{2,6},{3,7},{4,0},{5,1},{6,2},{7,3},{8,12},{9,13},{10,... | collective-permute-start | bytes 700424 | tf_op jit(solution)/shard_map/ppermute | solution.py:208
  5.6 2.6 %collective-permute-start.5 = (bf16[912,128]{1,0:T(8,128)(2,1)}, bf16[912,128]{1,0:T(8,128)(2,1)S(1)}, u32[]{:S(2)}, u32[]{:S(2)}) collective-permute-start(bf16[912,128]{1,0:T(8,128)(2,1)} %pack.1.refs_0_), channel_id=1, source_target_pairs={{0,8},{1,9},{2,10},{3,11},{4,12},{5,13},{6,14},{7,15},{8,0},{9,1},... | collective-permute-start | bytes 700424 | tf_op jit(solution)/shard_map/ppermute | solution.py:208
  8.2 1.4 %collective-permute-start.7 = (bf16[912,128]{1,0:T(8,128)(2,1)}, bf16[912,128]{1,0:T(8,128)(2,1)S(1)}, u32[]{:S(2)}, u32[]{:S(2)}) collective-permute-start(bf16[912,128]{1,0:T(8,128)(2,1)} %pack.1.refs_0_), channel_id=1, source_target_pairs={{0,6},{1,7},{2,4},{3,5},{4,2},{5,3},{6,0},{7,1},{8,14},{9,15},{10,... | collective-permute-start | bytes 700424 | tf_op jit(solution)/shard_map/ppermute | solution.py:208
  9.6 0.5 %collective-permute-start.3 = (bf16[912,128]{1,0:T(8,128)(2,1)}, bf16[912,128]{1,0:T(8,128)(2,1)S(1)}, u32[]{:S(2)}, u32[]{:S(2)}) collective-permute-start(bf16[912,128]{1,0:T(8,128)(2,1)} %pack.1.refs_0_), channel_id=1, source_target_pairs={{0,2},{1,3},{2,0},{3,1},{4,6},{5,7},{6,4},{7,5},{8,10},{9,11},{10,... | collective-permute-start | bytes 700424 | tf_op jit(solution)/shard_map/ppermute | solution.py:208
  10.1 0.0 collective-permute-done.1.refs_1_
  10.1 7.1 %collective-permute-done.refs_4_ = bf16[912,128]{1,0:T(8,128)(2,1)S(1)} collective-permute-done((bf16[912,128]{1,0:T(8,128)(2,1)}, bf16[912,128]{1,0:T(8,128)(2,1)S(1)}, u32[]{:S(2)}, u32[]{:S(2)}) %collective-permute-start) | collective-permute-done | bytes 233504 | tf_op jit(solution)/shard_map/ppermute | solution.py:208
  17.2 2.9 %collective-permute-start.2 = (bf16[912,128]{1,0:T(8,128)(2,1)}, bf16[912,128]{1,0:T(8,128)(2,1)S(1)}, u32[]{:S(2)}, u32[]{:S(2)}) collective-permute-start(bf16[912,128]{1,0:T(8,128)(2,1)} %pack.1.refs_0_), channel_id=1, source_target_pairs={{0,12},{1,13},{2,14},{3,15},{4,8},{5,9},{6,10},{7,11},{8,4},{9,5},... | collective-permute-start | bytes 700424 | tf_op jit(solution)/shard_map/ppermute | solution.py:208
  20.1 0.0 collective-permute-done.5.refs_8_
  20.1 1.5 %collective-permute-start.10 = (bf16[912,128]{1,0:T(8,128)(2,1)S(1)}, bf16[912,128]{1,0:T(8,128)(2,1)S(1)}, u32[]{:S(2)}, u32[]{:S(2)}) collective-permute-start(bf16[912,128]{1,0:T(8,128)(2,1)S(1)} %collective-permute-done.5.refs_8_), channel_id=1, source_target_pairs={{0,2},{1,3},{2,0},{3,1},{4,6},{5,7},{6,4},{7,5},{8,10},{9,11},{10,... | collective-permute-start | bytes 700424 | tf_op jit(solution)/shard_map/ppermute | solution.py:208
  21.6 1.7 %collective-permute-done.7.refs_6_ = bf16[912,128]{1,0:T(8,128)(2,1)S(1)} collective-permute-done((bf16[912,128]{1,0:T(8,128)(2,1)}, bf16[912,128]{1,0:T(8,128)(2,1)S(1)}, u32[]{:S(2)}, u32[]{:S(2)}) %collective-permute-start.7) | collective-permute-done | bytes 233504 | tf_op jit(solution)/shard_map/ppermute | solution.py:208
  23.4 0.0 collective-permute-start.8
  23.4 0.5 %collective-permute-start.9 = (bf16[912,128]{1,0:T(8,128)(2,1)S(1)}, bf16[912,128]{1,0:T(8,128)(2,1)S(1)}, u32[]{:S(2)}, u32[]{:S(2)}) collective-permute-start(bf16[912,128]{1,0:T(8,128)(2,1)S(1)} %collective-permute-done.5.refs_8_), channel_id=1, source_target_pairs={{0,1},{1,0},{2,3},{3,2},{4,5},{5,4},{6,7},{7,6},{8,9},{9,8},{10,11... | collective-permute-start | bytes 700424 | tf_op jit(solution)/shard_map/ppermute | solution.py:208
  23.9 0.0 collective-permute-done.3.refs_2_
  23.9 0.0 collective-permute-start.4
  23.9 5.6 %collective-permute-done.2.refs_2_.refs_12_ = bf16[912,128]{1,0:T(8,128)(2,1)S(1)} collective-permute-done((bf16[912,128]{1,0:T(8,128)(2,1)}, bf16[912,128]{1,0:T(8,128)(2,1)S(1)}, u32[]{:S(2)}, u32[]{:S(2)}) %collective-permute-start.2) | collective-permute-done | bytes 233504 | tf_op jit(solution)/shard_map/ppermute | solution.py:208
  29.5 0.0 collective-permute-start.6
  29.5 0.0 collective-permute-done.10.refs_0_.refs_10_
  29.5 0.5 %collective-permute-start.11 = (bf16[912,128]{1,0:T(8,128)(2,1)S(1)}, bf16[912,128]{1,0:T(8,128)(2,1)S(1)}, u32[]{:S(2)}, u32[]{:S(2)}) collective-permute-start(bf16[912,128]{1,0:T(8,128)(2,1)S(1)} %collective-permute-done.10.refs_0_.refs_10_), channel_id=1, source_target_pairs={{0,1},{1,0},{2,3},{3,2},{4,5},{5,4},{6,7},{7,6},{8,9},{9,8},{10,11... | collective-permute-start | bytes 700424 | tf_op jit(solution)/shard_map/ppermute | solution.py:208
  30.0 0.0 collective-permute-done.8.refs_7_
  30.0 0.1 collective-permute-start.12
  30.1 0.0 collective-permute-done.9.refs_9_
  30.1 1.5 %collective-permute-start.13 = (bf16[912,128]{1,0:T(8,128)(2,1)S(1)}, bf16[912,128]{1,0:T(8,128)(2,1)S(1)}, u32[]{:S(2)}, u32[]{:S(2)}) collective-permute-start(bf16[912,128]{1,0:T(8,128)(2,1)S(1)} %collective-permute-done.2.refs_2_.refs_12_), channel_id=1, source_target_pairs={{0,2},{1,3},{2,0},{3,1},{4,6},{5,7},{6,4},{7,5},{8,10},{9,11},{10,... | collective-permute-start | bytes 700424 | tf_op jit(solution)/shard_map/ppermute | solution.py:208
  31.6 0.0 copy-start.4
  31.6 0.0 copy-done.2
  31.6 0.0 copy-done.3
  31.6 0.6 %copy-done.4 = s32[1,6]{1,0:T(1,128)S(1)} copy-done((s32[1,6]{1,0:T(1,128)S(1)}, s32[1,6]{1,0:T(1,128)}, u32[]{:S(2)}) %copy-start.4) | copy-done | bytes 48
  32.3 0.6 %local.1 = (bf16[128,768]{1,0:T(8,128)(2,1)S(1)}, f32[1,768]{1,0:T(1,128)S(1)}) custom-call(s32[1,6]{1,0:T(1,128)S(1)} %copy-done.4, bf16[128,768]{1,0:T(8,128)(2,1)S(1)} %copy-done.2, f32[768]{0:T(1024)S(1)} %copy-done.3), custom_call_target="tpu_custom_call" | custom-call | bytes 1048576 | tf_op jit(solution)/shard_map/local/pallas_call | solution.py:179
  32.9 0.0 collective-permute-done.4.refs_3_
  32.9 0.0 collective-permute-done.6.refs_5_
  32.9 0.0 copy-start
  32.9 0.9 %copy-done = bf16[912,128]{1,0:T(8,128)(2,1)S(1)} copy-done((bf16[912,128]{1,0:T(8,128)(2,1)S(1)}, bf16[912,128]{1,0:T(8,128)(2,1)}, u32[]{:S(2)}) %copy-start) | copy-done | bytes 233496
  33.8 1.2 %early.2 = (bf16[10,128,128]{2,1,0:T(8,128)(2,1)S(1)}, f32[10,8,768]{2,1,0:T(8,128)S(1)}) custom-call(s32[1]{0:T(128)} %bitcast.me_ref, bf16[128,768]{1,0:T(8,128)(2,1)S(1)} %get-tuple-element.29.masked_ref, bf16[912,128]{1,0:T(8,128)(2,1)S(1)} %copy-done, bf16[912,128]{1,0:T(8,128)(2,1)S(1)} %collective-permute-done.1.refs_1_, ...), custom_call_target="tpu_custom_call" | custom-call | bytes 1048576 | tf_op jit(solution)/shard_map/early/pallas_call | solution.py:194
  35.0 0.0 copy-start.1
  35.0 0.0 collective-permute-done.11.refs_1_.refs_11_
  35.0 0.0 collective-permute-done.12.refs_3_.refs_13_
  35.0 0.6 %early.3 = (bf16[4,128,128]{2,1,0:T(8,128)(2,1)S(1)}, f32[4,8,768]{2,1,0:T(8,128)S(1)}) custom-call(s32[1]{0:T(128)} %bitcast.me_ref, bf16[128,768]{1,0:T(8,128)(2,1)S(1)} %get-tuple-element.29.masked_ref, bf16[912,128]{1,0:T(8,128)(2,1)S(1)} %collective-permute-done.10.refs_0_.refs_10_, bf16[912,128]{1,0:T(8,128)(2,1)S(1)} %collective-permute-done.11.refs_1_.refs_11_, ...), custom_call_target="tpu_custom_call" | custom-call | bytes 1048576 | tf_op jit(solution)/shard_map/early/pallas_call | solution.py:194
  35.7 2.5 %collective-permute-done.13.refs_14_ = bf16[912,128]{1,0:T(8,128)(2,1)S(1)} collective-permute-done((bf16[912,128]{1,0:T(8,128)(2,1)S(1)}, bf16[912,128]{1,0:T(8,128)(2,1)S(1)}, u32[]{:S(2)}, u32[]{:S(2)}) %collective-permute-start.13) | collective-permute-done | bytes 233504 | tf_op jit(solution)/shard_map/ppermute | solution.py:208
  38.2 0.0 copy-start.5
  38.2 0.0 collective-permute-start.14
  38.2 1.5 %collective-permute-done.14.refs_15_ = bf16[912,128]{1,0:T(8,128)(2,1)S(1)} collective-permute-done((bf16[912,128]{1,0:T(8,128)(2,1)S(1)}, bf16[912,128]{1,0:T(8,128)(2,1)S(1)}, u32[]{:S(2)}, u32[]{:S(2)}) %collective-permute-start.14) | collective-permute-done | bytes 233504 | tf_op jit(solution)/shard_map/ppermute | solution.py:208
  39.7 0.0 copy-done.1
  39.7 0.0 copy-done.5
  39.7 3.2 %last.1 = (bf16[1,8,128,128]{3,2,1,0:T(8,128)(2,1)}, f32[8,128]{1,0:T(8,128)}) custom-call(s32[1]{0:T(128)} %bitcast.me_ref, s32[1,8]{1,0:T(1,128)S(1)} %copy-done.5, bf16[128,768]{1,0:T(8,128)(2,1)S(1)} %get-tuple-element.29.masked_ref, f32[1,768]{1,0:T(1,128)S(1)} %get-tuple-element.30.tau_ref, bf16[912,128]{1,0:T(8,128)(2,1)S(1)} %copy-done.1, ...), custom_call_target="tpu_custom_call" | custom-call | bytes 1048576 | tf_op jit(solution)/shard_map/last/pallas_call | solution.py:235
Async XLA Ops:
  0.6 31.0 %copy-start.2 = (bf16[128,768]{1,0:T(8,128)(2,1)S(1)}, bf16[128,768]{1,0:T(8,128)(2,1)}, u32[]{:S(2)}) copy-start(bf16[128,768]{1,0:T(8,128)(2,1)} %rows_ref) | copy-start | bytes 589828
  2.4 29.2 %copy-start.3 = (f32[768]{0:T(1024)S(1)}, f32[768]{0:T(1024)}, u32[]{:S(2)}) copy-start(f32[768]{0:T(1024)} %tau_ref) | copy-start | bytes 9220
  2.4 7.7 %collective-permute-start.1 = (bf16[912,128]{1,0:T(8,128)(2,1)}, bf16[912,128]{1,0:T(8,128)(2,1)S(1)}, u32[]{:S(2)}, u32[]{:S(2)}) collective-permute-start(bf16[912,128]{1,0:T(8,128)(2,1)} %pack.1.refs_0_), channel_id=1, source_target_pairs={{0,1},{1,0},{2,3},{3,2},{4,5},{5,4},{6,7},{7,6},{8,9},{9,8},{10,11... | collective-permute-start | bytes 700424 | tf_op jit(solution)/shard_map/ppermute | solution.py:208
  3.0 14.3 %collective-permute-start = (bf16[912,128]{1,0:T(8,128)(2,1)}, bf16[912,128]{1,0:T(8,128)(2,1)S(1)}, u32[]{:S(2)}, u32[]{:S(2)}) collective-permute-start(bf16[912,128]{1,0:T(8,128)(2,1)} %pack.1.refs_0_), channel_id=1, source_target_pairs={{0,4},{1,5},{2,6},{3,7},{4,0},{5,1},{6,2},{7,3},{8,12},{9,13},{10,... | collective-permute-start | bytes 700424 | tf_op jit(solution)/shard_map/ppermute | solution.py:208
  5.6 14.5 %collective-permute-start.5 = (bf16[912,128]{1,0:T(8,128)(2,1)}, bf16[912,128]{1,0:T(8,128)(2,1)S(1)}, u32[]{:S(2)}, u32[]{:S(2)}) collective-permute-start(bf16[912,128]{1,0:T(8,128)(2,1)} %pack.1.refs_0_), channel_id=1, source_target_pairs={{0,8},{1,9},{2,10},{3,11},{4,12},{5,13},{6,14},{7,15},{8,0},{9,1},... | collective-permute-start | bytes 700424 | tf_op jit(solution)/shard_map/ppermute | solution.py:208
  8.2 15.2 %collective-permute-start.7 = (bf16[912,128]{1,0:T(8,128)(2,1)}, bf16[912,128]{1,0:T(8,128)(2,1)S(1)}, u32[]{:S(2)}, u32[]{:S(2)}) collective-permute-start(bf16[912,128]{1,0:T(8,128)(2,1)} %pack.1.refs_0_), channel_id=1, source_target_pairs={{0,6},{1,7},{2,4},{3,5},{4,2},{5,3},{6,0},{7,1},{8,14},{9,15},{10,... | collective-permute-start | bytes 700424 | tf_op jit(solution)/shard_map/ppermute | solution.py:208
  9.6 14.3 %collective-permute-start.3 = (bf16[912,128]{1,0:T(8,128)(2,1)}, bf16[912,128]{1,0:T(8,128)(2,1)S(1)}, u32[]{:S(2)}, u32[]{:S(2)}) collective-permute-start(bf16[912,128]{1,0:T(8,128)(2,1)} %pack.1.refs_0_), channel_id=1, source_target_pairs={{0,2},{1,3},{2,0},{3,1},{4,6},{5,7},{6,4},{7,5},{8,10},{9,11},{10,... | collective-permute-start | bytes 700424 | tf_op jit(solution)/shard_map/ppermute | solution.py:208
  17.2 12.3 %collective-permute-start.2 = (bf16[912,128]{1,0:T(8,128)(2,1)}, bf16[912,128]{1,0:T(8,128)(2,1)S(1)}, u32[]{:S(2)}, u32[]{:S(2)}) collective-permute-start(bf16[912,128]{1,0:T(8,128)(2,1)} %pack.1.refs_0_), channel_id=1, source_target_pairs={{0,12},{1,13},{2,14},{3,15},{4,8},{5,9},{6,10},{7,11},{8,4},{9,5},... | collective-permute-start | bytes 700424 | tf_op jit(solution)/shard_map/ppermute | solution.py:208
  20.1 9.4 %collective-permute-start.10 = (bf16[912,128]{1,0:T(8,128)(2,1)S(1)}, bf16[912,128]{1,0:T(8,128)(2,1)S(1)}, u32[]{:S(2)}, u32[]{:S(2)}) collective-permute-start(bf16[912,128]{1,0:T(8,128)(2,1)S(1)} %collective-permute-done.5.refs_8_), channel_id=1, source_target_pairs={{0,2},{1,3},{2,0},{3,1},{4,6},{5,7},{6,4},{7,5},{8,10},{9,11},{10,... | collective-permute-start | bytes 700424 | tf_op jit(solution)/shard_map/ppermute | solution.py:208
  23.4 6.7 %collective-permute-start.8 = (bf16[912,128]{1,0:T(8,128)(2,1)S(1)}, bf16[912,128]{1,0:T(8,128)(2,1)S(1)}, u32[]{:S(2)}, u32[]{:S(2)}) collective-permute-start(bf16[912,128]{1,0:T(8,128)(2,1)S(1)} %collective-permute-done.7.refs_6_), channel_id=1, source_target_pairs={{0,1},{1,0},{2,3},{3,2},{4,5},{5,4},{6,7},{7,6},{8,9},{9,8},{10,11... | collective-permute-start | bytes 700424 | tf_op jit(solution)/shard_map/ppermute | solution.py:208
  23.4 6.8 %collective-permute-start.9 = (bf16[912,128]{1,0:T(8,128)(2,1)S(1)}, bf16[912,128]{1,0:T(8,128)(2,1)S(1)}, u32[]{:S(2)}, u32[]{:S(2)}) collective-permute-start(bf16[912,128]{1,0:T(8,128)(2,1)S(1)} %collective-permute-done.5.refs_8_), channel_id=1, source_target_pairs={{0,1},{1,0},{2,3},{3,2},{4,5},{5,4},{6,7},{7,6},{8,9},{9,8},{10,11... | collective-permute-start | bytes 700424 | tf_op jit(solution)/shard_map/ppermute | solution.py:208
  23.9 9.0 %collective-permute-start.4 = (bf16[912,128]{1,0:T(8,128)(2,1)S(1)}, bf16[912,128]{1,0:T(8,128)(2,1)S(1)}, u32[]{:S(2)}, u32[]{:S(2)}) collective-permute-start(bf16[912,128]{1,0:T(8,128)(2,1)S(1)} %collective-permute-done.3.refs_2_), channel_id=1, source_target_pairs={{0,1},{1,0},{2,3},{3,2},{4,5},{5,4},{6,7},{7,6},{8,9},{9,8},{10,11... | collective-permute-start | bytes 700424 | tf_op jit(solution)/shard_map/ppermute | solution.py:208
  29.5 3.4 %collective-permute-start.6 = (bf16[912,128]{1,0:T(8,128)(2,1)S(1)}, bf16[912,128]{1,0:T(8,128)(2,1)S(1)}, u32[]{:S(2)}, u32[]{:S(2)}) collective-permute-start(bf16[912,128]{1,0:T(8,128)(2,1)S(1)} %collective-permute-done.refs_4_), channel_id=1, source_target_pairs={{0,1},{1,0},{2,3},{3,2},{4,5},{5,4},{6,7},{7,6},{8,9},{9,8},{10,11... | collective-permute-start | bytes 700424 | tf_op jit(solution)/shard_map/ppermute | solution.py:208
  29.5 5.5 %collective-permute-start.11 = (bf16[912,128]{1,0:T(8,128)(2,1)S(1)}, bf16[912,128]{1,0:T(8,128)(2,1)S(1)}, u32[]{:S(2)}, u32[]{:S(2)}) collective-permute-start(bf16[912,128]{1,0:T(8,128)(2,1)S(1)} %collective-permute-done.10.refs_0_.refs_10_), channel_id=1, source_target_pairs={{0,1},{1,0},{2,3},{3,2},{4,5},{5,4},{6,7},{7,6},{8,9},{9,8},{10,11... | collective-permute-start | bytes 700424 | tf_op jit(solution)/shard_map/ppermute | solution.py:208
  30.0 5.0 %collective-permute-start.12 = (bf16[912,128]{1,0:T(8,128)(2,1)S(1)}, bf16[912,128]{1,0:T(8,128)(2,1)S(1)}, u32[]{:S(2)}, u32[]{:S(2)}) collective-permute-start(bf16[912,128]{1,0:T(8,128)(2,1)S(1)} %collective-permute-done.2.refs_2_.refs_12_), channel_id=1, source_target_pairs={{0,1},{1,0},{2,3},{3,2},{4,5},{5,4},{6,7},{7,6},{8,9},{9,8},{10,11... | collective-permute-start | bytes 700424 | tf_op jit(solution)/shard_map/ppermute | solution.py:208
  30.1 8.0 %collective-permute-start.13 = (bf16[912,128]{1,0:T(8,128)(2,1)S(1)}, bf16[912,128]{1,0:T(8,128)(2,1)S(1)}, u32[]{:S(2)}, u32[]{:S(2)}) collective-permute-start(bf16[912,128]{1,0:T(8,128)(2,1)S(1)} %collective-permute-done.2.refs_2_.refs_12_), channel_id=1, source_target_pairs={{0,2},{1,3},{2,0},{3,1},{4,6},{5,7},{6,4},{7,5},{8,10},{9,11},{10,... | collective-permute-start | bytes 700424 | tf_op jit(solution)/shard_map/ppermute | solution.py:208
  31.6 0.7 %copy-start.4 = (s32[1,6]{1,0:T(1,128)S(1)}, s32[1,6]{1,0:T(1,128)}, u32[]{:S(2)}) copy-start(s32[1,6]{1,0:T(1,128)} %mask_ref) | copy-start | bytes 76
  32.9 0.9 %copy-start = (bf16[912,128]{1,0:T(8,128)(2,1)S(1)}, bf16[912,128]{1,0:T(8,128)(2,1)}, u32[]{:S(2)}) copy-start(bf16[912,128]{1,0:T(8,128)(2,1)} %pack.1.refs_0_) | copy-start | bytes 700420
  35.0 4.6 %copy-start.1 = (bf16[912,128]{1,0:T(8,128)(2,1)S(1)}, bf16[912,128]{1,0:T(8,128)(2,1)}, u32[]{:S(2)}) copy-start(bf16[912,128]{1,0:T(8,128)(2,1)} %pack.1.refs_0_) | copy-start | bytes 700420
  38.2 1.5 %copy-start.5 = (s32[1,8]{1,0:T(1,128)S(1)}, s32[1,8]{1,0:T(1,128)}, u32[]{:S(2)}) copy-start(s32[1,8]{1,0:T(1,128)} %dest_hbm.3) | copy-start | bytes 100
  38.2 1.5 %collective-permute-start.14 = (bf16[912,128]{1,0:T(8,128)(2,1)S(1)}, bf16[912,128]{1,0:T(8,128)(2,1)S(1)}, u32[]{:S(2)}, u32[]{:S(2)}) collective-permute-start(bf16[912,128]{1,0:T(8,128)(2,1)S(1)} %collective-permute-done.13.refs_14_), channel_id=1, source_target_pairs={{0,1},{1,0},{2,3},{3,2},{4,5},{5,4},{6,7},{7,6},{8,9},{9,8},{10,11... | collective-permute-start | bytes 700424 | tf_op jit(solution)/shard_map/ppermute | solution.py:208

commit v4 on v3

--- a/solution.py
+++ b/solution.py
@@ -213,23 +213,29 @@
     for mask in far[1:-1] + [near]:
         got[mask] = swap(own, mask)
     got[2], got[near + 2], got[1] = swap(own, 2), swap(own, near + 2), swap(own, 1)
-    got[last] = swap(after(own, got[near], got[1]), last)
+    if len(far) == 3:
+        layer = me[0] // LAYER
+        middle = (layer == 1) | (layer == 2)
+        onward = (2, 0, 3, 1)
+        got[last] = lax.ppermute(
+            jnp.where(middle, got[2 * LAYER], got[near]),
+            "row",
+            [(i, onward[i // LAYER] * LAYER + i % LAYER) for i in range(devices)],
+        )
+    else:
+        got[last] = swap(own, last)
     for mask in far[1:-1]:
         got[mask + 2] = swap(after(got[mask], got[near]), 2)
-    got[last + 2] = swap(after(got[last], got[near + 2], [got[m + 2] for m in far[1:-1]]), 2)
     got[3] = swap(after(got[2], got[near]), 1)
-    for mask in far[:-1]:
-        got[mask + 1] = swap(after(got[mask], got[far[1]]), 1)
-    got[near + 3] = swap(after(got[near + 2], got[far[1]]), 1)
+    first = [0, 1, 2, 3] + far[:-1] + [near + 2]
+    groups = [first]
+    results = [early(first)]
+    got[last + 2] = swap(after(got[last], results[0]), 2)
+    got[near + 3] = swap(after(got[near + 2], results[0]), 1)
     for mask in far[1:-1]:
-        got[mask + 3] = swap(after(got[mask + 2], got[last]), 1)
-    got[last + 1] = swap(after(got[last], [got[m + 2] for m in far[1:-1]]), 1)
-    forwarded = [mask + 2 for mask in far[1:-1]]
-    first = [m for m in range(last) if m not in forwarded and m - 1 not in forwarded]
-    second = [m for m in range(last + 2) if m not in first]
-    groups = [first, second]
-    masked, tau = after((masked, tau), got[last])
-    results = [early(first), early(second)]
+        got[mask + 3] = swap(after(got[mask + 2], results[0]), 1)
+    for mask in far:
+        got[mask + 1] = swap(after(got[mask], results[0]), 1)
     got[last + 3] = swap(after(got[last + 2], results), 1)
     pieces = [got[m] for m in range(devices)]
     return pl.pallas_call(

time: 43.1 us -> 38.8 us (0.900)
  starting transfers between devices: 14.7 us -> 12.5 us
  local copies, waits for them, and re-layouts: 1.61 us -> 0.02 us
    ppermute x15 -> x14, starting transfers between devices: 14.7 us -> 12.4 us  [swap(): return lax.ppermute(piece, 'row', [(i, i ^ mask) for i in range(devices)])]
    ppermute x15 -> x14, waiting for transfers between devices: 18.5 us -> 16.4 us  [swap(): return lax.ppermute(piece, 'row', [(i, i ^ mask) for i in range(devices)])]
    ppermute x0 -> x1, waiting for transfers between devices: none -> 2 us  [body(): lax.ppermute(jnp.where(middle, got[2 * LAYER], got[near]), 'row', [(i, on...]
    unnamed x12 -> x10, local copies, waits for them, and re-layouts: 1.61 us -> 0.02 us
    pallas_call x2 -> x1, Pallas kernels: 1.76 us -> 0.92 us  [early(): pl.pallas_call(early_kernel, out_shape=(jax.ShapeDtypeStruct((len(group),...]
    pallas_call x1, Pallas kernels: 3.24 us -> 3.77 us  [body(): pl.pallas_call(functools.partial(last_kernel, devices, groups), out_shape...]
  transfers between devices with their start and end apart: 15 -> 15, of which waited for: 5 -> 7; matrix products, arithmetic and copies ran while one was open for 0% -> 0% of each run, Pallas kernels for 5% -> 4%
where the time goes in v4:
time: 38.8 us; the launch traced here: 38.7 us
  waiting for transfers between devices  18.4 us (47%)
  starting transfers between devices  12.5 us (32%)
  Pallas kernels  7 us (18%)
  between operations  0.68 us (2%)
    ppermute x14, waiting for transfers between devices, swap(): return lax.ppermute(piece, 'row', [(i, i ^ mask) for i in range(devices)])  16.4 us
    ppermute x14, starting transfers between devices, swap(): return lax.ppermute(piece, 'row', [(i, i ^ mask) for i in range(devices)])  12.4 us
    pallas_call x1, Pallas kernels, body(): pl.pallas_call(functools.partial(last_kernel, devices, groups), out_shape...  3.77 us
    ppermute x1, waiting for transfers between devices, body(): lax.ppermute(jnp.where(middle, got[2 * LAYER], got[near]), 'row', [(i, on...  2 us
    pallas_call x1, Pallas kernels, body(): pl.pallas_call(pack_kernel, out_shape=jax.ShapeDtypeStruct((piece_rows, B...  1.73 us
    pallas_call x1, Pallas kernels, early(): pl.pallas_call(early_kernel, out_shape=(jax.ShapeDtypeStruct((len(group),...  0.92 us
  transfers between devices with their start and end apart: 15, of which 7 were waited for; matrix products, arithmetic and copies ran while one was open for 0% of the time, Pallas kernels for 4%

profile of v4, /device:TPU:0, one launch (start us, length us, event | category | flops | bytes accessed | tf_op | source)
XLA Modules:
  0.0 38.7 jit_solution(11405451970979508157)
XLA Ops:
  0.6 1.7 %pack.1.refs_0_ = bf16[912,128]{1,0:T(8,128)(2,1)} custom-call(s32[1,6]{1,0:T(1,128)} %mask_ref, s32[1,8]{1,0:T(1,128)} %dest_hbm.3, bf16[128,768]{1,0:T(8,128)(2,1)} %rows_ref, f32[768]{0:T(1024)} %tau_ref, bf16[128,128]{1,0:T(8,128)(2,1)} %metric_hbm.1), custom_call_target="tpu_custom_call" | custom-call | bytes 1048576 | tf_op jit(solution)/shard_map/pack/pallas_call | solution.py:163
  2.4 3.1 %collective-permute-start.2 = (bf16[912,128]{1,0:T(8,128)(2,1)}, bf16[912,128]{1,0:T(8,128)(2,1)S(1)}, u32[]{:S(2)}, u32[]{:S(2)}) collective-permute-start(bf16[912,128]{1,0:T(8,128)(2,1)} %pack.1.refs_0_), channel_id=1, source_target_pairs={{0,4},{1,5},{2,6},{3,7},{4,0},{5,1},{6,2},{7,3},{8,12},{9,13},{10,... | collective-permute-start | bytes 700424 | tf_op jit(solution)/shard_map/ppermute | solution.py:208
  5.5 1.5 %collective-permute-start.1 = (bf16[912,128]{1,0:T(8,128)(2,1)}, bf16[912,128]{1,0:T(8,128)(2,1)S(1)}, u32[]{:S(2)}, u32[]{:S(2)}) collective-permute-start(bf16[912,128]{1,0:T(8,128)(2,1)} %pack.1.refs_0_), channel_id=1, source_target_pairs={{0,2},{1,3},{2,0},{3,1},{4,6},{5,7},{6,4},{7,5},{8,10},{9,11},{10,... | collective-permute-start | bytes 700424 | tf_op jit(solution)/shard_map/ppermute | solution.py:208
  7.0 2.6 %collective-permute-start.4 = (bf16[912,128]{1,0:T(8,128)(2,1)}, bf16[912,128]{1,0:T(8,128)(2,1)S(1)}, u32[]{:S(2)}, u32[]{:S(2)}) collective-permute-start(bf16[912,128]{1,0:T(8,128)(2,1)} %pack.1.refs_0_), channel_id=1, source_target_pairs={{0,8},{1,9},{2,10},{3,11},{4,12},{5,13},{6,14},{7,15},{8,0},{9,1},... | collective-permute-start | bytes 700424 | tf_op jit(solution)/shard_map/ppermute | solution.py:208
  9.6 0.4 %collective-permute-start.5 = (bf16[912,128]{1,0:T(8,128)(2,1)}, bf16[912,128]{1,0:T(8,128)(2,1)S(1)}, u32[]{:S(2)}, u32[]{:S(2)}) collective-permute-start(bf16[912,128]{1,0:T(8,128)(2,1)} %pack.1.refs_0_), channel_id=1, source_target_pairs={{0,6},{1,7},{2,4},{3,5},{4,2},{5,3},{6,0},{7,1},{8,14},{9,15},{10,... | collective-permute-start | bytes 700424 | tf_op jit(solution)/shard_map/ppermute | solution.py:208
  10.0 0.0 collective-permute-start
  10.0 0.0 copy-start.1
  10.0 0.0 copy-start.2
  10.0 0.0 copy-start.3
  10.0 5.8 %collective-permute-done.2.refs_4_ = bf16[912,128]{1,0:T(8,128)(2,1)S(1)} collective-permute-done((bf16[912,128]{1,0:T(8,128)(2,1)}, bf16[912,128]{1,0:T(8,128)(2,1)S(1)}, u32[]{:S(2)}, u32[]{:S(2)}) %collective-permute-start.2) | collective-permute-done | bytes 233504 | tf_op jit(solution)/shard_map/ppermute | solution.py:208
  15.8 0.0 collective-permute-done.1.refs_2_
  15.8 0.0 collective-permute-start.3
  15.8 4.3 %collective-permute-done.4.refs_5_.refs_8_ = bf16[912,128]{1,0:T(8,128)(2,1)S(1)} collective-permute-done((bf16[912,128]{1,0:T(8,128)(2,1)}, bf16[912,128]{1,0:T(8,128)(2,1)S(1)}, u32[]{:S(2)}, u32[]{:S(2)}) %collective-permute-start.4) | collective-permute-done | bytes 233504 | tf_op jit(solution)/shard_map/ppermute | solution.py:208
  20.1 0.0 copy-start
  20.2 0.1 collective-permute-start.11
  20.3 0.0 copy-done.1
  20.3 0.0 copy-done.2
  20.3 0.0 copy-done.3
  20.3 0.6 %local.1 = (bf16[128,768]{1,0:T(8,128)(2,1)S(1)}, f32[1,768]{1,0:T(1,128)S(1)}) custom-call(s32[1,6]{1,0:T(1,128)S(1)} %copy-done.3, bf16[128,768]{1,0:T(8,128)(2,1)S(1)} %copy-done.1, f32[768]{0:T(1024)S(1)} %copy-done.2), custom_call_target="tpu_custom_call" | custom-call | bytes 1048576 | tf_op jit(solution)/shard_map/local/pallas_call | solution.py:179
  20.9 1.6 %collective-permute-start.9 = (bf16[912,128]{1,0:T(8,128)(2,1)S(1)}, bf16[912,128]{1,0:T(8,128)(2,1)S(1)}, u32[]{:S(2)}, u32[]{:S(2)}) collective-permute-start(bf16[912,128]{1,0:T(8,128)(2,1)S(1)} %collective-permute-done.4.refs_5_.refs_8_), channel_id=1, source_target_pairs={{0,2},{1,3},{2,0},{3,1},{4,6},{5,7},{6,4},{7,5},{8,10},{9,11},{10,... | collective-permute-start | bytes 700424 | tf_op jit(solution)/shard_map/ppermute | solution.py:208
  22.5 1.0 %collective-permute-done.5.refs_6_ = bf16[912,128]{1,0:T(8,128)(2,1)S(1)} collective-permute-done((bf16[912,128]{1,0:T(8,128)(2,1)}, bf16[912,128]{1,0:T(8,128)(2,1)S(1)}, u32[]{:S(2)}, u32[]{:S(2)}) %collective-permute-start.5) | collective-permute-done | bytes 233504 | tf_op jit(solution)/shard_map/ppermute | solution.py:208
  23.4 0.0 collective-permute-done.refs_1_
  23.4 0.0 collective-permute-done.3.refs_3_
  23.4 0.0 copy-done
  23.4 0.9 %early.1 = (bf16[7,128,128]{2,1,0:T(8,128)(2,1)S(1)}, f32[7,8,768]{2,1,0:T(8,128)S(1)}) custom-call(s32[1]{0:T(128)} %bitcast.me_ref, bf16[128,768]{1,0:T(8,128)(2,1)S(1)} %get-tuple-element.20.masked_ref, bf16[912,128]{1,0:T(8,128)(2,1)S(1)} %copy-done, bf16[912,128]{1,0:T(8,128)(2,1)S(1)} %collective-permute-done.refs_1_, ...), custom_call_target="tpu_custom_call" | custom-call | bytes 1048576 | tf_op jit(solution)/shard_map/early/pallas_call | solution.py:194
  24.4 2.0 %collective-permute-done.11.refs_12_ = bf16[912,128]{1,0:T(8,128)(2,1)S(1)} collective-permute-done((bf16[912,128]{1,0:T(8,128)(2,1)S(1)}, bf16[912,128]{1,0:T(8,128)(2,1)S(1)}, u32[]{:S(2)}, u32[]{:S(2)}) %collective-permute-start.11) | collective-permute-done | bytes 233504 | tf_op jit(solution)/shard_map/ppermute | solution.py:220
  26.4 0.0 copy-start.4
  26.4 1.7 %collective-permute-start.13 = (bf16[912,128]{1,0:T(8,128)(2,1)S(1)}, bf16[912,128]{1,0:T(8,128)(2,1)S(1)}, u32[]{:S(2)}, u32[]{:S(2)}) collective-permute-start(bf16[912,128]{1,0:T(8,128)(2,1)S(1)} %collective-permute-done.11.refs_12_), channel_id=1, source_target_pairs={{0,2},{1,3},{2,0},{3,1},{4,6},{5,7},{6,4},{7,5},{8,10},{9,11},{10,... | collective-permute-start | bytes 700424 | tf_op jit(solution)/shard_map/ppermute | solution.py:208
  28.1 0.0 collective-permute-start.6
  28.1 0.5 %collective-permute-start.12 = (bf16[912,128]{1,0:T(8,128)(2,1)S(1)}, bf16[912,128]{1,0:T(8,128)(2,1)S(1)}, u32[]{:S(2)}, u32[]{:S(2)}) collective-permute-start(bf16[912,128]{1,0:T(8,128)(2,1)S(1)} %collective-permute-done.11.refs_12_), channel_id=1, source_target_pairs={{0,1},{1,0},{2,3},{3,2},{4,5},{5,4},{6,7},{7,6},{8,9},{9,8},{10,11... | collective-permute-start | bytes 700424 | tf_op jit(solution)/shard_map/ppermute | solution.py:208
  28.6 0.0 collective-permute-done.9.refs_10_
  28.6 0.0 collective-permute-start.7
  28.6 0.5 %collective-permute-start.8 = (bf16[912,128]{1,0:T(8,128)(2,1)S(1)}, bf16[912,128]{1,0:T(8,128)(2,1)S(1)}, u32[]{:S(2)}, u32[]{:S(2)}) collective-permute-start(bf16[912,128]{1,0:T(8,128)(2,1)S(1)} %collective-permute-done.4.refs_5_.refs_8_), channel_id=1, source_target_pairs={{0,1},{1,0},{2,3},{3,2},{4,5},{5,4},{6,7},{7,6},{8,9},{9,8},{10,11... | collective-permute-start | bytes 700424 | tf_op jit(solution)/shard_map/ppermute | solution.py:208
  29.1 4.0 %collective-permute-done.13.refs_14_ = bf16[912,128]{1,0:T(8,128)(2,1)S(1)} collective-permute-done((bf16[912,128]{1,0:T(8,128)(2,1)S(1)}, bf16[912,128]{1,0:T(8,128)(2,1)S(1)}, u32[]{:S(2)}, u32[]{:S(2)}) %collective-permute-start.13) | collective-permute-done | bytes 233504 | tf_op jit(solution)/shard_map/ppermute | solution.py:208
  33.1 0.0 collective-permute-start.10
  33.1 0.0 collective-permute-done.6.refs_5_
  33.1 0.5 %collective-permute-start.14 = (bf16[912,128]{1,0:T(8,128)(2,1)S(1)}, bf16[912,128]{1,0:T(8,128)(2,1)S(1)}, u32[]{:S(2)}, u32[]{:S(2)}) collective-permute-start(bf16[912,128]{1,0:T(8,128)(2,1)S(1)} %collective-permute-done.13.refs_14_), channel_id=1, source_target_pairs={{0,1},{1,0},{2,3},{3,2},{4,5},{5,4},{6,7},{7,6},{8,9},{9,8},{10,11... | collective-permute-start | bytes 700424 | tf_op jit(solution)/shard_map/ppermute | solution.py:208
  33.6 0.0 collective-permute-done.7.refs_7_
  33.6 0.0 collective-permute-done.8.refs_9_
  33.6 1.0 %collective-permute-done.10.refs_11_ = bf16[912,128]{1,0:T(8,128)(2,1)S(1)} collective-permute-done((bf16[912,128]{1,0:T(8,128)(2,1)S(1)}, bf16[912,128]{1,0:T(8,128)(2,1)S(1)}, u32[]{:S(2)}, u32[]{:S(2)}) %collective-permute-start.10) | collective-permute-done | bytes 233504 | tf_op jit(solution)/shard_map/ppermute | solution.py:208
  34.6 0.0 collective-permute-done.12.refs_13_
  34.6 0.3 collective-permute-done.14.refs_15_
  34.9 0.0 copy-done.4
  34.9 3.8 %last.1 = (bf16[1,8,128,128]{3,2,1,0:T(8,128)(2,1)}, f32[8,128]{1,0:T(8,128)}) custom-call(s32[1]{0:T(128)} %bitcast.me_ref, s32[1,8]{1,0:T(1,128)S(1)} %copy-done.4, bf16[128,768]{1,0:T(8,128)(2,1)S(1)} %get-tuple-element.20.masked_ref, f32[1,768]{1,0:T(1,128)S(1)} %get-tuple-element.21.tau_ref, bf16[912,128]{1,0:T(8,128)(2,1)S(1)} %copy-done, ...), custom_call_target="tpu_custom_call" | custom-call | bytes 1048576 | tf_op jit(solution)/shard_map/last/pallas_call | solution.py:241
  (1 shorter events, 0.0 us)
Async XLA Ops:
  2.4 13.5 %collective-permute-start.2 = (bf16[912,128]{1,0:T(8,128)(2,1)}, bf16[912,128]{1,0:T(8,128)(2,1)S(1)}, u32[]{:S(2)}, u32[]{:S(2)}) collective-permute-start(bf16[912,128]{1,0:T(8,128)(2,1)} %pack.1.refs_0_), channel_id=1, source_target_pairs={{0,4},{1,5},{2,6},{3,7},{4,0},{5,1},{6,2},{7,3},{8,12},{9,13},{10,... | collective-permute-start | bytes 700424 | tf_op jit(solution)/shard_map/ppermute | solution.py:208
  5.5 10.4 %collective-permute-start.1 = (bf16[912,128]{1,0:T(8,128)(2,1)}, bf16[912,128]{1,0:T(8,128)(2,1)S(1)}, u32[]{:S(2)}, u32[]{:S(2)}) collective-permute-start(bf16[912,128]{1,0:T(8,128)(2,1)} %pack.1.refs_0_), channel_id=1, source_target_pairs={{0,2},{1,3},{2,0},{3,1},{4,6},{5,7},{6,4},{7,5},{8,10},{9,11},{10,... | collective-permute-start | bytes 700424 | tf_op jit(solution)/shard_map/ppermute | solution.py:208
  7.0 13.1 %collective-permute-start.4 = (bf16[912,128]{1,0:T(8,128)(2,1)}, bf16[912,128]{1,0:T(8,128)(2,1)S(1)}, u32[]{:S(2)}, u32[]{:S(2)}) collective-permute-start(bf16[912,128]{1,0:T(8,128)(2,1)} %pack.1.refs_0_), channel_id=1, source_target_pairs={{0,8},{1,9},{2,10},{3,11},{4,12},{5,13},{6,14},{7,15},{8,0},{9,1},... | collective-permute-start | bytes 700424 | tf_op jit(solution)/shard_map/ppermute | solution.py:208
  9.6 13.9 %collective-permute-start.5 = (bf16[912,128]{1,0:T(8,128)(2,1)}, bf16[912,128]{1,0:T(8,128)(2,1)S(1)}, u32[]{:S(2)}, u32[]{:S(2)}) collective-permute-start(bf16[912,128]{1,0:T(8,128)(2,1)} %pack.1.refs_0_), channel_id=1, source_target_pairs={{0,6},{1,7},{2,4},{3,5},{4,2},{5,3},{6,0},{7,1},{8,14},{9,15},{10,... | collective-permute-start | bytes 700424 | tf_op jit(solution)/shard_map/ppermute | solution.py:208
  10.0 13.5 %collective-permute-start = (bf16[912,128]{1,0:T(8,128)(2,1)}, bf16[912,128]{1,0:T(8,128)(2,1)S(1)}, u32[]{:S(2)}, u32[]{:S(2)}) collective-permute-start(bf16[912,128]{1,0:T(8,128)(2,1)} %pack.1.refs_0_), channel_id=1, source_target_pairs={{0,1},{1,0},{2,3},{3,2},{4,5},{5,4},{6,7},{7,6},{8,9},{9,8},{10,11... | collective-permute-start | bytes 700424 | tf_op jit(solution)/shard_map/ppermute | solution.py:208
  10.0 10.3 %copy-start.1 = (bf16[128,768]{1,0:T(8,128)(2,1)S(1)}, bf16[128,768]{1,0:T(8,128)(2,1)}, u32[]{:S(2)}) copy-start(bf16[128,768]{1,0:T(8,128)(2,1)} %rows_ref) | copy-start | bytes 589828
  10.0 10.3 %copy-start.2 = (f32[768]{0:T(1024)S(1)}, f32[768]{0:T(1024)}, u32[]{:S(2)}) copy-start(f32[768]{0:T(1024)} %tau_ref) | copy-start | bytes 9220
  10.0 10.3 %copy-start.3 = (s32[1,6]{1,0:T(1,128)S(1)}, s32[1,6]{1,0:T(1,128)}, u32[]{:S(2)}) copy-start(s32[1,6]{1,0:T(1,128)} %mask_ref) | copy-start | bytes 76
  15.8 7.6 %collective-permute-start.3 = (bf16[912,128]{1,0:T(8,128)(2,1)S(1)}, bf16[912,128]{1,0:T(8,128)(2,1)S(1)}, u32[]{:S(2)}, u32[]{:S(2)}) collective-permute-start(bf16[912,128]{1,0:T(8,128)(2,1)S(1)} %collective-permute-done.1.refs_2_), channel_id=1, source_target_pairs={{0,1},{1,0},{2,3},{3,2},{4,5},{5,4},{6,7},{7,6},{8,9},{9,8},{10,11... | collective-permute-start | bytes 700424 | tf_op jit(solution)/shard_map/ppermute | solution.py:208
  20.1 3.3 %copy-start = (bf16[912,128]{1,0:T(8,128)(2,1)S(1)}, bf16[912,128]{1,0:T(8,128)(2,1)}, u32[]{:S(2)}) copy-start(bf16[912,128]{1,0:T(8,128)(2,1)} %pack.1.refs_0_) | copy-start | bytes 700420
  20.2 6.2 %collective-permute-start.11 = (bf16[912,128]{1,0:T(8,128)(2,1)S(1)}, bf16[912,128]{1,0:T(8,128)(2,1)S(1)}, u32[]{:S(2)}, u32[]{:S(2)}) collective-permute-start(bf16[912,128]{1,0:T(8,128)(2,1)S(1)} %broadcast_select_fusion), channel_id=1, source_target_pairs={{0,8},{1,9},{2,10},{3,11},{4,0},{5,1},{6,2},{7,3},{8,12},{9,13},{1... | collective-permute-start | bytes 700424 | tf_op jit(solution)/shard_map/ppermute | solution.py:220
  20.9 7.7 %collective-permute-start.9 = (bf16[912,128]{1,0:T(8,128)(2,1)S(1)}, bf16[912,128]{1,0:T(8,128)(2,1)S(1)}, u32[]{:S(2)}, u32[]{:S(2)}) collective-permute-start(bf16[912,128]{1,0:T(8,128)(2,1)S(1)} %collective-permute-done.4.refs_5_.refs_8_), channel_id=1, source_target_pairs={{0,2},{1,3},{2,0},{3,1},{4,6},{5,7},{6,4},{7,5},{8,10},{9,11},{10,... | collective-permute-start | bytes 700424 | tf_op jit(solution)/shard_map/ppermute | solution.py:208
  26.4 8.5 %copy-start.4 = (s32[1,8]{1,0:T(1,128)S(1)}, s32[1,8]{1,0:T(1,128)}, u32[]{:S(2)}) copy-start(s32[1,8]{1,0:T(1,128)} %dest_hbm.3) | copy-start | bytes 100
  26.4 6.7 %collective-permute-start.13 = (bf16[912,128]{1,0:T(8,128)(2,1)S(1)}, bf16[912,128]{1,0:T(8,128)(2,1)S(1)}, u32[]{:S(2)}, u32[]{:S(2)}) collective-permute-start(bf16[912,128]{1,0:T(8,128)(2,1)S(1)} %collective-permute-done.11.refs_12_), channel_id=1, source_target_pairs={{0,2},{1,3},{2,0},{3,1},{4,6},{5,7},{6,4},{7,5},{8,10},{9,11},{10,... | collective-permute-start | bytes 700424 | tf_op jit(solution)/shard_map/ppermute | solution.py:208
  28.1 5.0 %collective-permute-start.6 = (bf16[912,128]{1,0:T(8,128)(2,1)S(1)}, bf16[912,128]{1,0:T(8,128)(2,1)S(1)}, u32[]{:S(2)}, u32[]{:S(2)}) collective-permute-start(bf16[912,128]{1,0:T(8,128)(2,1)S(1)} %collective-permute-done.2.refs_4_), channel_id=1, source_target_pairs={{0,1},{1,0},{2,3},{3,2},{4,5},{5,4},{6,7},{7,6},{8,9},{9,8},{10,11... | collective-permute-start | bytes 700424 | tf_op jit(solution)/shard_map/ppermute | solution.py:208
  28.1 6.5 %collective-permute-start.12 = (bf16[912,128]{1,0:T(8,128)(2,1)S(1)}, bf16[912,128]{1,0:T(8,128)(2,1)S(1)}, u32[]{:S(2)}, u32[]{:S(2)}) collective-permute-start(bf16[912,128]{1,0:T(8,128)(2,1)S(1)} %collective-permute-done.11.refs_12_), channel_id=1, source_target_pairs={{0,1},{1,0},{2,3},{3,2},{4,5},{5,4},{6,7},{7,6},{8,9},{9,8},{10,11... | collective-permute-start | bytes 700424 | tf_op jit(solution)/shard_map/ppermute | solution.py:208
  28.6 5.0 %collective-permute-start.7 = (bf16[912,128]{1,0:T(8,128)(2,1)S(1)}, bf16[912,128]{1,0:T(8,128)(2,1)S(1)}, u32[]{:S(2)}, u32[]{:S(2)}) collective-permute-start(bf16[912,128]{1,0:T(8,128)(2,1)S(1)} %collective-permute-done.5.refs_6_), channel_id=1, source_target_pairs={{0,1},{1,0},{2,3},{3,2},{4,5},{5,4},{6,7},{7,6},{8,9},{9,8},{10,11... | collective-permute-start | bytes 700424 | tf_op jit(solution)/shard_map/ppermute | solution.py:208
  28.6 5.0 %collective-permute-start.8 = (bf16[912,128]{1,0:T(8,128)(2,1)S(1)}, bf16[912,128]{1,0:T(8,128)(2,1)S(1)}, u32[]{:S(2)}, u32[]{:S(2)}) collective-permute-start(bf16[912,128]{1,0:T(8,128)(2,1)S(1)} %collective-permute-done.4.refs_5_.refs_8_), channel_id=1, source_target_pairs={{0,1},{1,0},{2,3},{3,2},{4,5},{5,4},{6,7},{7,6},{8,9},{9,8},{10,11... | collective-permute-start | bytes 700424 | tf_op jit(solution)/shard_map/ppermute | solution.py:208
  33.1 1.5 %collective-permute-start.10 = (bf16[912,128]{1,0:T(8,128)(2,1)S(1)}, bf16[912,128]{1,0:T(8,128)(2,1)S(1)}, u32[]{:S(2)}, u32[]{:S(2)}) collective-permute-start(bf16[912,128]{1,0:T(8,128)(2,1)S(1)} %collective-permute-done.9.refs_10_), channel_id=1, source_target_pairs={{0,1},{1,0},{2,3},{3,2},{4,5},{5,4},{6,7},{7,6},{8,9},{9,8},{10,11... | collective-permute-start | bytes 700424 | tf_op jit(solution)/shard_map/ppermute | solution.py:208
  33.1 1.8 %collective-permute-start.14 = (bf16[912,128]{1,0:T(8,128)(2,1)S(1)}, bf16[912,128]{1,0:T(8,128)(2,1)S(1)}, u32[]{:S(2)}, u32[]{:S(2)}) collective-permute-start(bf16[912,128]{1,0:T(8,128)(2,1)S(1)} %collective-permute-done.13.refs_14_), channel_id=1, source_target_pairs={{0,1},{1,0},{2,3},{3,2},{4,5},{5,4},{6,7},{7,6},{8,9},{9,8},{10,11... | collective-permute-start | bytes 700424 | tf_op jit(solution)/shard_map/ppermute | solution.py:208

commit v5 on v4

v5 whole, which is shorter than its diff:
```python
import functools

import jax
import jax.numpy as jnp
from jax import lax
from jax.experimental import pallas as pl
from jax.experimental.pallas import tpu as pltpu
from jax.sharding import PartitionSpec as P

BLOCK = 128
LIST_ROWS = 16
LAYER = 4
CUT = 4 * BLOCK
MIB = 1 << 20
NT_DIMS = (((1,), (1,)), ((), ()))
NN_DIMS = (((1,), (0,)), ((), ()))
TN_DIMS = (((0,), (0,)), ((), ()))


def dot(a, b, dims=NN_DIMS):
    return lax.dot_general(a, b, dims, preferred_element_type=jnp.float32)


def split(x):
    high = x.astype(jnp.bfloat16)
    return high, (x - high.astype(jnp.float32)).astype(jnp.bfloat16)


def pack_kernel(
    mask_hbm, dest_hbm, rows_hbm, tau_hbm, metric_hbm, piece_ref, mask_ref, dest_ref, rows_ref, tau_ref, sems
):
    tiles = mask_ref.shape[1]
    depth = tiles * BLOCK
    moves = [
        (rows_hbm, rows_ref),
        (tau_hbm, tau_ref),
        (mask_hbm, mask_ref),
        (dest_hbm, dest_ref),
        (metric_hbm, piece_ref.at[depth : depth + BLOCK]),
    ]
    copies = [pltpu.make_async_copy(source, target, sems.at[k]) for k, (source, target) in enumerate(moves)]
    for copy in copies:
        copy.start()
    for copy in copies:
        copy.wait()
    tau = tau_ref[...].reshape(1, depth)
    for t in range(tiles):
        cols = slice(t * BLOCK, (t + 1) * BLOCK)
        weight = tau[:, cols] * mask_ref[0, t].astype(jnp.float32)
        piece_ref[cols, :] = (rows_ref[:, cols].astype(jnp.float32) * weight).astype(jnp.bfloat16)
    lane = lax.broadcasted_iota(jnp.int32, (LIST_ROWS, BLOCK), 1)
    listed = jnp.zeros((LIST_ROWS, BLOCK), jnp.float32)
    for j in range(dest_ref.shape[1]):
        listed += (lane == dest_ref[0, j]).astype(jnp.float32)
    piece_ref[depth + BLOCK :, :] = listed.astype(jnp.bfloat16)


def local_kernel(mask_ref, rows_ref, tau_ref, masked_ref, row_ref):
    row_ref[...] = tau_ref[...].reshape(row_ref.shape)
    for t in range(mask_ref.shape[1]):
        cols = slice(t * BLOCK, (t + 1) * BLOCK)
        masked_ref[:, cols] = rows_ref[:, cols] * mask_ref[0, t].astype(jnp.bfloat16)


def rows_of(piece, first, count):
    for part in piece:
        if first < part.shape[0]:
            return part[first : first + count, :]
        first -= part.shape[0]


def scaled_of(piece):
    depth = sum(part.shape[0] for part in piece) - BLOCK - LIST_ROWS
    return jnp.concatenate([rows_of(piece, t, BLOCK) for t in range(0, depth, BLOCK)], axis=1)


def metric_of(piece):
    depth = sum(part.shape[0] for part in piece) - BLOCK - LIST_ROWS
    return rows_of(piece, depth, BLOCK)


def listed_of(piece):
    part = piece[-1]
    return part[part.shape[0] - LIST_ROWS :, :]


def grouped(refs, parts):
    pieces = []
    for count in parts:
        pieces.append(tuple(refs[:count]))
        refs = refs[count:]
    return pieces


def strips_of(masked, pieces, strips):
    for k, piece in enumerate(pieces):
        strips[k][...] = dot(masked, scaled_of(piece), NT_DIMS).astype(jnp.bfloat16)


def window_of(me, pieces, windows, grams):
    rows = windows[0].shape[0]
    lane = lax.broadcasted_iota(jnp.int32, (rows, BLOCK), 1)
    row = lax.broadcasted_iota(jnp.int32, (rows, BLOCK), 0)
    pick = (lane == row + me * rows).astype(jnp.bfloat16)
    own = [dot(pick, metric_of(piece), NT_DIMS).astype(jnp.bfloat16) for piece in pieces]
    for k, piece in enumerate(pieces):
        windows[k][...] = dot(own[k], scaled_of(piece))
    for k, piece in enumerate(pieces):
        grams[k][...] = dot(scaled_of(piece), metric_of(piece), TN_DIMS).astype(jnp.bfloat16)


def early_kernel(parts, masked_ref, *refs):
    strips, windows, grams = refs[-3:]
    pieces = grouped(refs[:-3], parts)
    each = range(len(pieces))
    strips_of(masked_ref[...], pieces, [strips.at[k] for k in each])
    window_of(lax.axis_index("row"), pieces, [windows.at[k] for k in each], [grams.at[k] for k in each])


def last_kernel(devices, groups, parts, dest_hbm, masked_ref, tau_ref, *refs):
    pieces = grouped(refs, parts)
    early = refs[sum(parts) : sum(parts) + 3 * len(groups)]
    chi_ref, sand_ref, strips, window, late_grams, listed, dest_ref, sems, dest_sem = refs[
        sum(parts) + 3 * len(groups) :
    ]
    fetch = pltpu.make_async_copy(dest_hbm, dest_ref, dest_sem)
    fetch.start()
    me = lax.axis_index("row")
    rows = BLOCK // devices
    fanout = dest_ref.shape[1]
    late = [m for m in range(devices) if all(m not in group for group in groups)]
    strips_of(masked_ref[...], [pieces[m] for m in late], [strips.at[m] for m in late])
    grams = {m: late_grams.at[k] for k, m in enumerate(late)}
    for group, strip, part, gram in zip(groups, early[::3], early[1::3], early[2::3]):
        for k, m in enumerate(group):
            strips[m] = strip[k]
            window[m * rows : (m + 1) * rows, :] = part[k]
            grams[m] = gram.at[k]
    fetch.wait()
    copies = [
        pltpu.make_async_copy(strips.at[dest_ref[0, j] ^ me], chi_ref.at[0, j], sems.at[j])
        for j in range(fanout)
    ]
    for copy in copies:
        copy.start()
    window_of(
        me,
        [pieces[m] for m in late],
        [window.at[m * rows : (m + 1) * rows] for m in late],
        [grams[m] for m in late],
    )

    for m in range(devices):
        entry = listed_of(pieces[m]).astype(jnp.float32)
        listed[m * rows : (m + 1) * rows, :] = entry[:rows, :]
    row = lax.broadcasted_iota(jnp.int32, (BLOCK, BLOCK), 0)
    column = lax.broadcasted_iota(jnp.int32, (BLOCK, BLOCK), 1)
    by_piece = (row == (column // rows ^ me)).astype(jnp.bfloat16)
    routes = dot(listed[...].astype(jnp.bfloat16), by_piece)
    same = row % rows == column % rows
    pair = jnp.where(same, routes + routes.T, 0.0).astype(jnp.bfloat16)
    mixed = dot(jnp.concatenate([pair, pair], axis=1), jnp.concatenate(split(window[...]), axis=0))
    high, low = split(mixed / tau_ref[...])
    total = jnp.zeros((2 * rows, BLOCK), jnp.float32)
    for m in range(devices):
        part = slice(m * rows, (m + 1) * rows)
        total += dot(jnp.concatenate([high[part], low[part]], axis=0), grams[m][...])
    sand_ref[...] = total[:rows] + total[rows:]
    for copy in copies:
        copy.wait()


def after(value, *others):
    return lax.optimization_barrier((value, others))[0]


def body(three_center, tau_weights, tile_mask, dest, metric_half):
    devices = lax.axis_size("row")
    local_rows, contracted = three_center.shape
    fanout = dest.shape[1]
    rows = BLOCK // devices
    piece_rows = contracted + BLOCK + LIST_ROWS
    smem = pl.BlockSpec(memory_space=pltpu.SMEM)
    vmem = pl.BlockSpec(memory_space=pltpu.VMEM)
    hbm = pl.BlockSpec(memory_space=pltpu.HBM)
    own = pl.pallas_call(
        pack_kernel,
        out_shape=jax.ShapeDtypeStruct((piece_rows, BLOCK), jnp.bfloat16),
        in_specs=[hbm] * 5,
        out_specs=vmem,
        scratch_shapes=[
            pltpu.SMEM(tile_mask.shape, jnp.int32),
            pltpu.SMEM(dest.shape, jnp.int32),
            pltpu.VMEM(three_center.shape, jnp.bfloat16),
            pltpu.VMEM(tau_weights.shape, jnp.float32),
            pltpu.SemaphoreType.DMA((5,)),
        ],
        compiler_params=pltpu.CompilerParams(vmem_limit_bytes=56 * MIB),
        name="pack",
    )(tile_mask, dest, three_center, tau_weights, metric_half)
    masked, tau = pl.pallas_call(
        local_kernel,
        out_shape=(
            jax.ShapeDtypeStruct((local_rows, contracted), jnp.bfloat16),
            jax.ShapeDtypeStruct((1, contracted), jnp.float32),
        ),
        in_specs=[smem, vmem, vmem],
        out_specs=(vmem, vmem),
        compiler_params=pltpu.CompilerParams(vmem_limit_bytes=4 * MIB),
        name="local",
    )(*after((tile_mask, three_center, tau_weights), own))
    layer = lax.axis_index("row") // LAYER

    def early(group, masked):
        used = [got[m] for m in group]
        return pl.pallas_call(
            functools.partial(early_kernel, [len(piece) for piece in used]),
            out_shape=(
                jax.ShapeDtypeStruct((len(group), BLOCK, BLOCK), jnp.bfloat16),
                jax.ShapeDtypeStruct((len(group), rows, contracted), jnp.float32),
                jax.ShapeDtypeStruct((len(group), contracted, BLOCK), jnp.bfloat16),
            ),
            in_specs=[vmem] * (1 + sum(len(piece) for piece in used)),
            out_specs=(vmem, vmem, vmem),
            compiler_params=pltpu.CompilerParams(vmem_limit_bytes=8 * MIB),
            name="early",
        )(masked, *[part for piece in used for part in piece])

    def swap(piece, mask):
        return tuple(lax.ppermute(part, "row", [(i, i ^ mask) for i in range(devices)]) for part in piece)

    far = list(range(LAYER, devices, LAYER))
    near, inner, last = far[0], far[1:-1], far[-1]
    got = {0: (own,)}
    for mask in inner:
        got[mask] = swap(got[0], mask)
    got[near], got[2] = swap(got[0], near), swap(got[0], 2)
    got[near + 2], got[1] = swap(got[near], 2), swap(got[0], 1)
    got[3], got[near + 1] = swap(got[2], 1), swap(got[near], 1)
    first = [0, 1, 3, *inner, near + 2, near + 1]
    results = [early(first, after(masked, got[2]))]
    got[near + 3] = swap(after(got[near + 2], results[0]), 1)
    for mask in inner:
        got[mask + 1] = swap(after(got[mask], results[0]), 1)
    for mask in inner:
        got[mask + 2] = swap(after(got[mask], got[near], got[2], got[near + 1]), 2)
    for mask in inner:
        got[mask + 3] = swap(after(got[mask + 2], results[0], got[1], got[near]), 1)
    if len(far) == 3:
        middle = (layer == 1) | (layer == 2)
        onward = (2, 0, 3, 1)
        got[last] = (
            lax.ppermute(
                jnp.where(middle, got[2 * LAYER][0], got[near][0]),
                "row",
                [(i, onward[i // LAYER] * LAYER + i % LAYER) for i in range(devices)],
            ),
        )
    else:
        got[last] = swap(got[0], last)
    got[last + 1] = swap(after(got[last], results[0]), 1)
    got[last + 2] = swap(after(got[last], results[0]), 2)
    got[last + 3] = swap(after(got[last + 2], [got[mask] for mask in inner]), 1)
    second = [2, near] + [mask + 3 for mask in inner]
    groups = [first, second]
    results.append(early(second, masked))
    parts = [len(got[m]) for m in range(devices)]
    pieces = [part for m in range(devices) for part in got[m]]
    return pl.pallas_call(
        functools.partial(last_kernel, devices, groups, parts),
        out_shape=(
            jax.ShapeDtypeStruct((1, fanout, BLOCK, BLOCK), jnp.bfloat16),
            jax.ShapeDtypeStruct((rows, BLOCK), jnp.float32),
        ),
        in_specs=[hbm] + [vmem] * (2 + len(pieces) + 3 * len(groups)),
        out_specs=(hbm, vmem),
        scratch_shapes=[
            pltpu.VMEM((devices, BLOCK, BLOCK), jnp.bfloat16),
            pltpu.VMEM((BLOCK, contracted), jnp.float32),
            pltpu.VMEM((devices - sum(len(group) for group in groups), contracted, BLOCK), jnp.bfloat16),
            pltpu.VMEM((BLOCK, BLOCK), jnp.float32),
            pltpu.SMEM(dest.shape, jnp.int32),
            pltpu.SemaphoreType.DMA((fanout,)),
            pltpu.SemaphoreType.DMA,
        ],
        compiler_params=pltpu.CompilerParams(vmem_limit_bytes=24 * MIB),
        name="last",
    )(dest, masked, tau, *pieces, *[part for result in results for part in result])


def solution(mesh):
    return jax.shard_map(
        body,
        mesh=mesh,
        in_specs=(
            P(("groups", "row"), None),
            P("groups"),
            P("row", None),
            P("row", None),
            P("row", None),
        ),
        out_specs=(P(("groups", "row"), None, None, None), P(("groups", "row"), None)),
        check_vma=False,
    )
```

time: 38.8 us -> 37.7 us (0.972)
  waiting for transfers between devices: 18.4 us -> 14.8 us
  local copies, waits for them, and re-layouts: 0.02 us -> 0.96 us
  starting transfers between devices: 12.5 us -> 13.4 us
  Pallas kernels: 7 us -> 7.55 us
    ppermute x15, waiting for transfers between devices: 18.4 us -> 14.8 us  [the longest x14 14.1 us: swap(): lax.ppermute(part, 'row', [(i, i ^ mask) for i in range(devices)])]
    unnamed x10 -> x12, local copies, waits for them, and re-layouts: 0.02 us -> 0.96 us
    ppermute x15, starting transfers between devices: 12.5 us -> 13.4 us  [the longest x14 13.3 us: swap(): lax.ppermute(part, 'row', [(i, i ^ mask) for i in range(devices)])]
    pallas_call x2 -> x3, Pallas kernels: 4.69 us -> 5.17 us  [the longest x1 3.44 us: body(): pl.pallas_call(functools.partial(last_kernel, devices, groups, parts), ou...]
  transfers between devices with their start and end apart: 15 -> 15, of which waited for: 7 -> 7; matrix products, arithmetic and copies ran while one was open for 0% -> 0% of each run, Pallas kernels for 4% -> 6%
where the time goes in v5:
time: 37.7 us; the launch traced here: 37.5 us
  waiting for transfers between devices  14.8 us (39%)
  starting transfers between devices  13.4 us (36%)
  Pallas kernels  7.55 us (20%)
  local copies, waits for them, and re-layouts  0.96 us (3%)
  between operations  0.77 us (2%)
    ppermute x14, waiting for transfers between devices, swap(): lax.ppermute(part, 'row', [(i, i ^ mask) for i in range(devices)])  14.1 us
    ppermute x14, starting transfers between devices, swap(): lax.ppermute(part, 'row', [(i, i ^ mask) for i in range(devices)])  13.3 us
    pallas_call x1, Pallas kernels, body(): pl.pallas_call(functools.partial(last_kernel, devices, groups, parts), ou...  3.44 us
    pallas_call x1, Pallas kernels, body(): pl.pallas_call(pack_kernel, out_shape=jax.ShapeDtypeStruct((piece_rows, B...  1.79 us
    pallas_call x2, Pallas kernels, early(): pl.pallas_call(functools.partial(early_kernel, [len(piece) for piece in u...  1.74 us
    unnamed x12, local copies, waits for them, and re-layouts  0.96 us
    ppermute x1, waiting for transfers between devices, body(): lax.ppermute(jnp.where(middle, got[2 * LAYER][0], got[near][0]), 'row', [...  0.78 us
  transfers between devices with their start and end apart: 15, of which 7 were waited for; matrix products, arithmetic and copies ran while one was open for 0% of the time, Pallas kernels for 6%

profile of v5, /device:TPU:0, one launch (start us, length us, event | category | flops | bytes accessed | tf_op | source)
XLA Modules:
  0.0 37.5 jit_solution(9780779080571853883)
XLA Ops:
  0.6 0.0 copy-start.4
  0.6 0.0 copy-start.3
  0.7 0.0 copy-start.2
  0.7 1.8 %pack.1.refs_0_ = bf16[912,128]{1,0:T(8,128)(2,1)} custom-call(s32[1,6]{1,0:T(1,128)} %mask_ref, s32[1,8]{1,0:T(1,128)} %dest_hbm.3, bf16[128,768]{1,0:T(8,128)(2,1)} %rows_ref, f32[768]{0:T(1024)} %tau_ref, bf16[128,128]{1,0:T(8,128)(2,1)} %metric_hbm.1), custom_call_target="tpu_custom_call" | custom-call | tf_op jit(solution)/shard_map/pack/pallas_call | solution.py:186
  2.5 3.1 %collective-permute-start.3 = (bf16[912,128]{1,0:T(8,128)(2,1)}, bf16[912,128]{1,0:T(8,128)(2,1)S(1)}, u32[]{:S(2)}, u32[]{:S(2)}) collective-permute-start(bf16[912,128]{1,0:T(8,128)(2,1)} %pack.1.refs_0_), channel_id=1, source_target_pairs={{0,4},{1,5},{2,6},{3,7},{4,0},{5,1},{6,2},{7,3},{8,12},{9,13},{10,... | collective-permute-start | bytes 700424 | tf_op jit(solution)/shard_map/ppermute | solution.py:230
  5.5 1.5 %collective-permute-start.1 = (bf16[912,128]{1,0:T(8,128)(2,1)}, bf16[912,128]{1,0:T(8,128)(2,1)S(1)}, u32[]{:S(2)}, u32[]{:S(2)}) collective-permute-start(bf16[912,128]{1,0:T(8,128)(2,1)} %pack.1.refs_0_), channel_id=1, source_target_pairs={{0,2},{1,3},{2,0},{3,1},{4,6},{5,7},{6,4},{7,5},{8,10},{9,11},{10,... | collective-permute-start | bytes 700424 | tf_op jit(solution)/shard_map/ppermute | solution.py:230
  7.1 2.6 %collective-permute-start.6 = (bf16[912,128]{1,0:T(8,128)(2,1)}, bf16[912,128]{1,0:T(8,128)(2,1)S(1)}, u32[]{:S(2)}, u32[]{:S(2)}) collective-permute-start(bf16[912,128]{1,0:T(8,128)(2,1)} %pack.1.refs_0_), channel_id=1, source_target_pairs={{0,8},{1,9},{2,10},{3,11},{4,12},{5,13},{6,14},{7,15},{8,0},{9,1},... | collective-permute-start | bytes 700424 | tf_op jit(solution)/shard_map/ppermute | solution.py:230
  9.7 0.0 collective-permute-start
  9.7 5.4 %collective-permute-done.3.refs_1_.refs_4_ = bf16[912,128]{1,0:T(8,128)(2,1)S(1)} collective-permute-done((bf16[912,128]{1,0:T(8,128)(2,1)}, bf16[912,128]{1,0:T(8,128)(2,1)S(1)}, u32[]{:S(2)}, u32[]{:S(2)}) %collective-permute-start.3) | collective-permute-done | bytes 233504 | tf_op jit(solution)/shard_map/ppermute | solution.py:230
  15.1 2.7 %collective-permute-start.5 = (bf16[912,128]{1,0:T(8,128)(2,1)S(1)}, bf16[912,128]{1,0:T(8,128)(2,1)S(1)}, u32[]{:S(2)}, u32[]{:S(2)}) collective-permute-start(bf16[912,128]{1,0:T(8,128)(2,1)S(1)} %collective-permute-done.3.refs_1_.refs_4_), channel_id=1, source_target_pairs={{0,2},{1,3},{2,0},{3,1},{4,6},{5,7},{6,4},{7,5},{8,10},{9,11},{10,... | collective-permute-start | bytes 700424 | tf_op jit(solution)/shard_map/ppermute | solution.py:230
  17.8 0.0 collective-permute-start.4
  17.8 0.0 collective-permute-done.1.refs_0_.refs_2_
  17.8 0.5 %collective-permute-start.2 = (bf16[912,128]{1,0:T(8,128)(2,1)S(1)}, bf16[912,128]{1,0:T(8,128)(2,1)S(1)}, u32[]{:S(2)}, u32[]{:S(2)}) collective-permute-start(bf16[912,128]{1,0:T(8,128)(2,1)S(1)} %collective-permute-done.1.refs_0_.refs_2_), channel_id=1, source_target_pairs={{0,1},{1,0},{2,3},{3,2},{4,5},{5,4},{6,7},{7,6},{8,9},{9,8},{10,11... | collective-permute-start | bytes 700424 | tf_op jit(solution)/shard_map/ppermute | solution.py:230
  18.3 1.8 %collective-permute-done.6.refs_3_.refs_8_ = bf16[912,128]{1,0:T(8,128)(2,1)S(1)} collective-permute-done((bf16[912,128]{1,0:T(8,128)(2,1)}, bf16[912,128]{1,0:T(8,128)(2,1)S(1)}, u32[]{:S(2)}, u32[]{:S(2)}) %collective-permute-start.6) | collective-permute-done | bytes 233504 | tf_op jit(solution)/shard_map/ppermute | solution.py:230
  20.1 0.0 copy-start.1
  20.1 0.1 collective-permute-start.11
  20.2 0.0 copy-done.4
  20.2 0.0 copy-done.3
  20.2 0.0 copy-done.2
  20.2 0.6 %local.1 = (bf16[128,768]{1,0:T(8,128)(2,1)S(1)}, f32[1,768]{1,0:T(1,128)S(1)}) custom-call(s32[1,6]{1,0:T(1,128)S(1)} %copy-done.4, bf16[128,768]{1,0:T(8,128)(2,1)S(1)} %copy-done.2, f32[768]{0:T(1024)S(1)} %copy-done.3), custom_call_target="tpu_custom_call" | custom-call | tf_op jit(solution)/shard_map/local/pallas_call | solution.py:201
  20.8 0.0 copy-start.5
  20.8 0.0 collective-permute-done.4.refs_5_
  20.9 0.6 %collective-permute-start.9 = (bf16[912,128]{1,0:T(8,128)(2,1)S(1)}, bf16[912,128]{1,0:T(8,128)(2,1)S(1)}, u32[]{:S(2)}, u32[]{:S(2)}) collective-permute-start(bf16[912,128]{1,0:T(8,128)(2,1)S(1)} %collective-permute-done.6.refs_3_.refs_8_), channel_id=1, source_target_pairs={{0,2},{1,3},{2,0},{3,1},{4,6},{5,7},{6,4},{7,5},{8,10},{9,11},{10,... | collective-permute-start | bytes 700424 | tf_op jit(solution)/shard_map/ppermute | solution.py:230
  21.5 0.0 collective-permute-done.refs_1_
  21.5 2.0 %collective-permute-done.5.refs_4_.refs_6_ = bf16[912,128]{1,0:T(8,128)(2,1)S(1)} collective-permute-done((bf16[912,128]{1,0:T(8,128)(2,1)S(1)}, bf16[912,128]{1,0:T(8,128)(2,1)S(1)}, u32[]{:S(2)}, u32[]{:S(2)}) %collective-permute-start.5) | collective-permute-done | bytes 233504 | tf_op jit(solution)/shard_map/ppermute | solution.py:230
  23.4 0.0 collective-permute-done.2.refs_2_.refs_3_
  23.4 0.0 copy-start
  23.4 0.9 %copy-done = bf16[912,128]{1,0:T(8,128)(2,1)S(1)} copy-done((bf16[912,128]{1,0:T(8,128)(2,1)S(1)}, bf16[912,128]{1,0:T(8,128)(2,1)}, u32[]{:S(2)}) %copy-start) | copy-done | bytes 233496
  24.4 1.1 %early.2 = (bf16[6,128,128]{2,1,0:T(8,128)(2,1)S(1)}, f32[6,8,768]{2,1,0:T(8,128)S(1)}, bf16[6,768,128]{2,1,0:T(8,128)(2,1)S(1)}) custom-call(bf16[128,768]{1,0:T(8,128)(2,1)S(1)} %get-tuple-element.25.masked_ref, bf16[912,128]{1,0:T(8,128)(2,1)S(1)} %copy-done, bf16[912,128]{1,0:T(8,128)(2,1)S(1)} %collective-permute-done.refs_1_, ...), custom_call_target="tpu_custom_call" | custom-call | tf_op jit(solution)/shard_map/early/pallas_call | solution.py:216
  25.5 0.8 %collective-permute-done.11.refs_12_ = bf16[912,128]{1,0:T(8,128)(2,1)S(1)} collective-permute-done((bf16[912,128]{1,0:T(8,128)(2,1)S(1)}, bf16[912,128]{1,0:T(8,128)(2,1)S(1)}, u32[]{:S(2)}, u32[]{:S(2)}) %collective-permute-start.11) | collective-permute-done | bytes 233504 | tf_op jit(solution)/shard_map/ppermute | solution.py:253
  26.3 1.8 %collective-permute-start.13 = (bf16[912,128]{1,0:T(8,128)(2,1)S(1)}, bf16[912,128]{1,0:T(8,128)(2,1)S(1)}, u32[]{:S(2)}, u32[]{:S(2)}) collective-permute-start(bf16[912,128]{1,0:T(8,128)(2,1)S(1)} %collective-permute-done.11.refs_12_), channel_id=1, source_target_pairs={{0,2},{1,3},{2,0},{3,1},{4,6},{5,7},{6,4},{7,5},{8,10},{9,11},{10,... | collective-permute-start | bytes 700424 | tf_op jit(solution)/shard_map/ppermute | solution.py:230
  28.0 0.0 collective-permute-start.12
  28.0 0.5 %collective-permute-start.7 = (bf16[912,128]{1,0:T(8,128)(2,1)S(1)}, bf16[912,128]{1,0:T(8,128)(2,1)S(1)}, u32[]{:S(2)}, u32[]{:S(2)}) collective-permute-start(bf16[912,128]{1,0:T(8,128)(2,1)S(1)} %collective-permute-done.5.refs_4_.refs_6_), channel_id=1, source_target_pairs={{0,1},{1,0},{2,3},{3,2},{4,5},{5,4},{6,7},{7,6},{8,9},{9,8},{10,11... | collective-permute-start | bytes 700424 | tf_op jit(solution)/shard_map/ppermute | solution.py:230
  28.6 0.0 collective-permute-start.8
  28.6 0.7 %collective-permute-done.9.refs_10_ = bf16[912,128]{1,0:T(8,128)(2,1)S(1)} collective-permute-done((bf16[912,128]{1,0:T(8,128)(2,1)S(1)}, bf16[912,128]{1,0:T(8,128)(2,1)S(1)}, u32[]{:S(2)}, u32[]{:S(2)}) %collective-permute-start.9) | collective-permute-done | bytes 233504 | tf_op jit(solution)/shard_map/ppermute | solution.py:230
  29.2 0.0 collective-permute-start.10
  29.2 3.4 %collective-permute-done.13.refs_14_ = bf16[912,128]{1,0:T(8,128)(2,1)S(1)} collective-permute-done((bf16[912,128]{1,0:T(8,128)(2,1)S(1)}, bf16[912,128]{1,0:T(8,128)(2,1)S(1)}, u32[]{:S(2)}, u32[]{:S(2)}) %collective-permute-start.13) | collective-permute-done | bytes 233504 | tf_op jit(solution)/shard_map/ppermute | solution.py:230
  32.6 0.0 collective-permute-start.14
  32.6 0.0 collective-permute-done.10.refs_2_.refs_11_
  32.6 0.6 %early.3 = (bf16[3,128,128]{2,1,0:T(8,128)(2,1)S(1)}, f32[3,8,768]{2,1,0:T(8,128)S(1)}, bf16[3,768,128]{2,1,0:T(8,128)(2,1)S(1)}) custom-call(bf16[128,768]{1,0:T(8,128)(2,1)S(1)} %get-tuple-element.25.masked_ref, bf16[912,128]{1,0:T(8,128)(2,1)S(1)} %collective-permute-done.1.refs_0_.refs_2_, bf16[912,128]{1,0:T(8,128)(2,1)S(1)} %collective-permute-done.3.refs_1_.refs_4_, ...), custom_call_target="tpu_custom_call" | custom-call | tf_op jit(solution)/shard_map/early/pallas_call | solution.py:216
  33.3 0.0 collective-permute-done.7.refs_7_
  33.3 0.0 collective-permute-done.8.refs_9_
  33.3 0.0 collective-permute-done.12.refs_13_
  33.3 0.8 %collective-permute-done.14.refs_15_ = bf16[912,128]{1,0:T(8,128)(2,1)S(1)} collective-permute-done((bf16[912,128]{1,0:T(8,128)(2,1)S(1)}, bf16[912,128]{1,0:T(8,128)(2,1)S(1)}, u32[]{:S(2)}, u32[]{:S(2)}) %collective-permute-start.14) | collective-permute-done | bytes 233504 | tf_op jit(solution)/shard_map/ppermute | solution.py:230
  34.1 0.0 copy-done.1
  34.1 0.0 copy-done.5
  34.1 3.4 %last.1 = (bf16[1,8,128,128]{3,2,1,0:T(8,128)(2,1)}, f32[8,128]{1,0:T(8,128)}) custom-call(s32[1,8]{1,0:T(1,128)S(1)} %copy-done.5, bf16[128,768]{1,0:T(8,128)(2,1)S(1)} %get-tuple-element.25.masked_ref, f32[1,768]{1,0:T(1,128)S(1)} %get-tuple-element.24.tau_ref, bf16[912,128]{1,0:T(8,128)(2,1)S(1)} %copy-done.1, ...), custom_call_target="tpu_custom_call" | custom-call | tf_op jit(solution)/shard_map/last/pallas_call | solution.py:269
  (1 shorter events, 0.0 us)
Async XLA Ops:
  0.6 19.6 %copy-start.4 = (s32[1,6]{1,0:T(1,128)S(1)}, s32[1,6]{1,0:T(1,128)}, u32[]{:S(2)}) copy-start(s32[1,6]{1,0:T(1,128)} %mask_ref) | copy-start | bytes 76
  0.6 19.6 %copy-start.3 = (f32[768]{0:T(1024)S(1)}, f32[768]{0:T(1024)}, u32[]{:S(2)}) copy-start(f32[768]{0:T(1024)} %tau_ref) | copy-start | bytes 9220
  0.7 19.6 %copy-start.2 = (bf16[128,768]{1,0:T(8,128)(2,1)S(1)}, bf16[128,768]{1,0:T(8,128)(2,1)}, u32[]{:S(2)}) copy-start(bf16[128,768]{1,0:T(8,128)(2,1)} %rows_ref) | copy-start | bytes 589828
  2.5 12.6 %collective-permute-start.3 = (bf16[912,128]{1,0:T(8,128)(2,1)}, bf16[912,128]{1,0:T(8,128)(2,1)S(1)}, u32[]{:S(2)}, u32[]{:S(2)}) collective-permute-start(bf16[912,128]{1,0:T(8,128)(2,1)} %pack.1.refs_0_), channel_id=1, source_target_pairs={{0,4},{1,5},{2,6},{3,7},{4,0},{5,1},{6,2},{7,3},{8,12},{9,13},{10,... | collective-permute-start | bytes 700424 | tf_op jit(solution)/shard_map/ppermute | solution.py:230
  5.5 12.2 %collective-permute-start.1 = (bf16[912,128]{1,0:T(8,128)(2,1)}, bf16[912,128]{1,0:T(8,128)(2,1)S(1)}, u32[]{:S(2)}, u32[]{:S(2)}) collective-permute-start(bf16[912,128]{1,0:T(8,128)(2,1)} %pack.1.refs_0_), channel_id=1, source_target_pairs={{0,2},{1,3},{2,0},{3,1},{4,6},{5,7},{6,4},{7,5},{8,10},{9,11},{10,... | collective-permute-start | bytes 700424 | tf_op jit(solution)/shard_map/ppermute | solution.py:230
  7.1 13.0 %collective-permute-start.6 = (bf16[912,128]{1,0:T(8,128)(2,1)}, bf16[912,128]{1,0:T(8,128)(2,1)S(1)}, u32[]{:S(2)}, u32[]{:S(2)}) collective-permute-start(bf16[912,128]{1,0:T(8,128)(2,1)} %pack.1.refs_0_), channel_id=1, source_target_pairs={{0,8},{1,9},{2,10},{3,11},{4,12},{5,13},{6,14},{7,15},{8,0},{9,1},... | collective-permute-start | bytes 700424 | tf_op jit(solution)/shard_map/ppermute | solution.py:230
  9.7 11.8 %collective-permute-start = (bf16[912,128]{1,0:T(8,128)(2,1)}, bf16[912,128]{1,0:T(8,128)(2,1)S(1)}, u32[]{:S(2)}, u32[]{:S(2)}) collective-permute-start(bf16[912,128]{1,0:T(8,128)(2,1)} %pack.1.refs_0_), channel_id=1, source_target_pairs={{0,1},{1,0},{2,3},{3,2},{4,5},{5,4},{6,7},{7,6},{8,9},{9,8},{10,11... | collective-permute-start | bytes 700424 | tf_op jit(solution)/shard_map/ppermute | solution.py:230
  15.1 8.4 %collective-permute-start.5 = (bf16[912,128]{1,0:T(8,128)(2,1)S(1)}, bf16[912,128]{1,0:T(8,128)(2,1)S(1)}, u32[]{:S(2)}, u32[]{:S(2)}) collective-permute-start(bf16[912,128]{1,0:T(8,128)(2,1)S(1)} %collective-permute-done.3.refs_1_.refs_4_), channel_id=1, source_target_pairs={{0,2},{1,3},{2,0},{3,1},{4,6},{5,7},{6,4},{7,5},{8,10},{9,11},{10,... | collective-permute-start | bytes 700424 | tf_op jit(solution)/shard_map/ppermute | solution.py:230
  17.8 3.1 %collective-permute-start.4 = (bf16[912,128]{1,0:T(8,128)(2,1)S(1)}, bf16[912,128]{1,0:T(8,128)(2,1)S(1)}, u32[]{:S(2)}, u32[]{:S(2)}) collective-permute-start(bf16[912,128]{1,0:T(8,128)(2,1)S(1)} %collective-permute-done.3.refs_1_.refs_4_), channel_id=1, source_target_pairs={{0,1},{1,0},{2,3},{3,2},{4,5},{5,4},{6,7},{7,6},{8,9},{9,8},{10,11... | collective-permute-start | bytes 700424 | tf_op jit(solution)/shard_map/ppermute | solution.py:230
  17.8 5.7 %collective-permute-start.2 = (bf16[912,128]{1,0:T(8,128)(2,1)S(1)}, bf16[912,128]{1,0:T(8,128)(2,1)S(1)}, u32[]{:S(2)}, u32[]{:S(2)}) collective-permute-start(bf16[912,128]{1,0:T(8,128)(2,1)S(1)} %collective-permute-done.1.refs_0_.refs_2_), channel_id=1, source_target_pairs={{0,1},{1,0},{2,3},{3,2},{4,5},{5,4},{6,7},{7,6},{8,9},{9,8},{10,11... | collective-permute-start | bytes 700424 | tf_op jit(solution)/shard_map/ppermute | solution.py:230
  20.1 14.0 %copy-start.1 = (bf16[912,128]{1,0:T(8,128)(2,1)S(1)}, bf16[912,128]{1,0:T(8,128)(2,1)}, u32[]{:S(2)}) copy-start(bf16[912,128]{1,0:T(8,128)(2,1)} %pack.1.refs_0_) | copy-start | bytes 700420
  20.1 6.1 %collective-permute-start.11 = (bf16[912,128]{1,0:T(8,128)(2,1)S(1)}, bf16[912,128]{1,0:T(8,128)(2,1)S(1)}, u32[]{:S(2)}, u32[]{:S(2)}) collective-permute-start(bf16[912,128]{1,0:T(8,128)(2,1)S(1)} %broadcast_select_fusion), channel_id=1, source_target_pairs={{0,8},{1,9},{2,10},{3,11},{4,0},{5,1},{6,2},{7,3},{8,12},{9,13},{1... | collective-permute-start | bytes 700424 | tf_op jit(solution)/shard_map/ppermute | solution.py:253
  20.8 13.3 %copy-start.5 = (s32[1,8]{1,0:T(1,128)S(1)}, s32[1,8]{1,0:T(1,128)}, u32[]{:S(2)}) copy-start(s32[1,8]{1,0:T(1,128)} %dest_hbm.3) | copy-start | bytes 100
  20.9 8.4 %collective-permute-start.9 = (bf16[912,128]{1,0:T(8,128)(2,1)S(1)}, bf16[912,128]{1,0:T(8,128)(2,1)S(1)}, u32[]{:S(2)}, u32[]{:S(2)}) collective-permute-start(bf16[912,128]{1,0:T(8,128)(2,1)S(1)} %collective-permute-done.6.refs_3_.refs_8_), channel_id=1, source_target_pairs={{0,2},{1,3},{2,0},{3,1},{4,6},{5,7},{6,4},{7,5},{8,10},{9,11},{10,... | collective-permute-start | bytes 700424 | tf_op jit(solution)/shard_map/ppermute | solution.py:230
  23.4 0.9 %copy-start = (bf16[912,128]{1,0:T(8,128)(2,1)S(1)}, bf16[912,128]{1,0:T(8,128)(2,1)}, u32[]{:S(2)}) copy-start(bf16[912,128]{1,0:T(8,128)(2,1)} %pack.1.refs_0_) | copy-start | bytes 700420
  26.3 6.3 %collective-permute-start.13 = (bf16[912,128]{1,0:T(8,128)(2,1)S(1)}, bf16[912,128]{1,0:T(8,128)(2,1)S(1)}, u32[]{:S(2)}, u32[]{:S(2)}) collective-permute-start(bf16[912,128]{1,0:T(8,128)(2,1)S(1)} %collective-permute-done.11.refs_12_), channel_id=1, source_target_pairs={{0,2},{1,3},{2,0},{3,1},{4,6},{5,7},{6,4},{7,5},{8,10},{9,11},{10,... | collective-permute-start | bytes 700424 | tf_op jit(solution)/shard_map/ppermute | solution.py:230
  28.0 5.2 %collective-permute-start.12 = (bf16[912,128]{1,0:T(8,128)(2,1)S(1)}, bf16[912,128]{1,0:T(8,128)(2,1)S(1)}, u32[]{:S(2)}, u32[]{:S(2)}) collective-permute-start(bf16[912,128]{1,0:T(8,128)(2,1)S(1)} %collective-permute-done.11.refs_12_), channel_id=1, source_target_pairs={{0,1},{1,0},{2,3},{3,2},{4,5},{5,4},{6,7},{7,6},{8,9},{9,8},{10,11... | collective-permute-start | bytes 700424 | tf_op jit(solution)/shard_map/ppermute | solution.py:230
  28.0 5.2 %collective-permute-start.7 = (bf16[912,128]{1,0:T(8,128)(2,1)S(1)}, bf16[912,128]{1,0:T(8,128)(2,1)S(1)}, u32[]{:S(2)}, u32[]{:S(2)}) collective-permute-start(bf16[912,128]{1,0:T(8,128)(2,1)S(1)} %collective-permute-done.5.refs_4_.refs_6_), channel_id=1, source_target_pairs={{0,1},{1,0},{2,3},{3,2},{4,5},{5,4},{6,7},{7,6},{8,9},{9,8},{10,11... | collective-permute-start | bytes 700424 | tf_op jit(solution)/shard_map/ppermute | solution.py:230
  28.6 4.7 %collective-permute-start.8 = (bf16[912,128]{1,0:T(8,128)(2,1)S(1)}, bf16[912,128]{1,0:T(8,128)(2,1)S(1)}, u32[]{:S(2)}, u32[]{:S(2)}) collective-permute-start(bf16[912,128]{1,0:T(8,128)(2,1)S(1)} %collective-permute-done.6.refs_3_.refs_8_), channel_id=1, source_target_pairs={{0,1},{1,0},{2,3},{3,2},{4,5},{5,4},{6,7},{7,6},{8,9},{9,8},{10,11... | collective-permute-start | bytes 700424 | tf_op jit(solution)/shard_map/ppermute | solution.py:230
  29.2 3.4 %collective-permute-start.10 = (bf16[912,128]{1,0:T(8,128)(2,1)S(1)}, bf16[912,128]{1,0:T(8,128)(2,1)S(1)}, u32[]{:S(2)}, u32[]{:S(2)}) collective-permute-start(bf16[912,128]{1,0:T(8,128)(2,1)S(1)} %collective-permute-done.9.refs_10_), channel_id=1, source_target_pairs={{0,1},{1,0},{2,3},{3,2},{4,5},{5,4},{6,7},{7,6},{8,9},{9,8},{10,11... | collective-permute-start | bytes 700424 | tf_op jit(solution)/shard_map/ppermute | solution.py:230
  32.6 1.5 %collective-permute-start.14 = (bf16[912,128]{1,0:T(8,128)(2,1)S(1)}, bf16[912,128]{1,0:T(8,128)(2,1)S(1)}, u32[]{:S(2)}, u32[]{:S(2)}) collective-permute-start(bf16[912,128]{1,0:T(8,128)(2,1)S(1)} %collective-permute-done.13.refs_14_), channel_id=1, source_target_pairs={{0,1},{1,0},{2,3},{3,2},{4,5},{5,4},{6,7},{7,6},{8,9},{9,8},{10,11... | collective-permute-start | bytes 700424 | tf_op jit(solution)/shard_map/ppermute | solution.py:230

commit v6 on v5

--- a/solution.py
+++ b/solution.py
@@ -136,13 +136,6 @@
             strips[m] = strip[k]
             window[m * rows : (m + 1) * rows, :] = part[k]
             grams[m] = gram.at[k]
-    fetch.wait()
-    copies = [
-        pltpu.make_async_copy(strips.at[dest_ref[0, j] ^ me], chi_ref.at[0, j], sems.at[j])
-        for j in range(fanout)
-    ]
-    for copy in copies:
-        copy.start()
     window_of(
         me,
         [pieces[m] for m in late],
@@ -160,6 +153,13 @@
     same = row % rows == column % rows
     pair = jnp.where(same, routes + routes.T, 0.0).astype(jnp.bfloat16)
     mixed = dot(jnp.concatenate([pair, pair], axis=1), jnp.concatenate(split(window[...]), axis=0))
+    fetch.wait()
+    copies = [
+        pltpu.make_async_copy(strips.at[dest_ref[0, j] ^ me], chi_ref.at[0, j], sems.at[j])
+        for j in range(fanout)
+    ]
+    for copy in copies:
+        copy.start()
     high, low = split(mixed / tau_ref[...])
     total = jnp.zeros((2 * rows, BLOCK), jnp.float32)
     for m in range(devices):
@@ -241,7 +241,7 @@
     results = [early(first, after(masked, got[2]))]
     got[near + 3] = swap(after(got[near + 2], results[0]), 1)
     for mask in inner:
-        got[mask + 1] = swap(after(got[mask], results[0]), 1)
+        got[mask + 1] = swap(got[mask], 1)
     for mask in inner:
         got[mask + 2] = swap(after(got[mask], got[near], got[2], got[near + 1]), 2)
     for mask in inner:
@@ -261,7 +261,10 @@
     got[last + 1] = swap(after(got[last], results[0]), 1)
     got[last + 2] = swap(after(got[last], results[0]), 2)
     got[last + 3] = swap(after(got[last + 2], [got[mask] for mask in inner]), 1)
-    second = [2, near] + [mask + 3 for mask in inner]
+    second = [2, near]
+    for mask in inner:
+        second += [mask + 1, mask + 3]
+    second += [last + 1, near + 3]
     groups = [first, second]
     results.append(early(second, masked))
     parts = [len(got[m]) for m in range(devices)]

time: 37.7 us -> 37.3 us (0.989)
  waiting for transfers between devices: 14.8 us -> 14.3 us
    ppermute x14, waiting for transfers between devices: 14.1 us -> 13.6 us  [swap(): lax.ppermute(part, 'row', [(i, i ^ mask) for i in range(devices)])]
    pallas_call x2, Pallas kernels: 1.74 us -> 2.19 us  [early(): pl.pallas_call(functools.partial(early_kernel, [len(piece) for piece in u...]
    pallas_call x1, Pallas kernels: 3.44 us -> 3.02 us  [body(): pl.pallas_call(functools.partial(last_kernel, devices, groups, parts), ou...]
  transfers between devices with their start and end apart: 15 -> 15, of which waited for: 7 -> 7; matrix products, arithmetic and copies ran while one was open for 0% -> 0% of each run, Pallas kernels for 6% -> 7%
where the time goes in v6:
time: 37.3 us; the launch traced here: 37.1 us
  waiting for transfers between devices  14.3 us (38%)
  starting transfers between devices  13.4 us (36%)
  Pallas kernels  7.59 us (20%)
  local copies, waits for them, and re-layouts  0.97 us (3%)
  between operations  0.78 us (2%)
    ppermute x14, waiting for transfers between devices, swap(): lax.ppermute(part, 'row', [(i, i ^ mask) for i in range(devices)])  13.6 us
    ppermute x14, starting transfers between devices, swap(): lax.ppermute(part, 'row', [(i, i ^ mask) for i in range(devices)])  13.4 us
    pallas_call x1, Pallas kernels, body(): pl.pallas_call(functools.partial(last_kernel, devices, groups, parts), ou...  3.02 us
    pallas_call x2, Pallas kernels, early(): pl.pallas_call(functools.partial(early_kernel, [len(piece) for piece in u...  2.19 us
    pallas_call x1, Pallas kernels, body(): pl.pallas_call(pack_kernel, out_shape=jax.ShapeDtypeStruct((piece_rows, B...  1.79 us
    unnamed x12, local copies, waits for them, and re-layouts  0.97 us
  transfers between devices with their start and end apart: 15, of which 7 were waited for; matrix products, arithmetic and copies ran while one was open for 0% of the time, Pallas kernels for 7%

profile of v6, /device:TPU:0, one launch (start us, length us, event | category | flops | bytes accessed | tf_op | source)
XLA Modules:
  0.0 37.1 jit_solution(7976300103712884858)
XLA Ops:
  0.6 0.0 copy-start.4
  0.6 0.0 copy-start.3
  0.7 0.0 copy-start.2
  0.7 1.8 %pack.1.refs_0_ = bf16[912,128]{1,0:T(8,128)(2,1)} custom-call(s32[1,6]{1,0:T(1,128)} %mask_ref, s32[1,8]{1,0:T(1,128)} %dest_hbm.3, bf16[128,768]{1,0:T(8,128)(2,1)} %rows_ref, f32[768]{0:T(1024)} %tau_ref, bf16[128,128]{1,0:T(8,128)(2,1)} %metric_hbm.1), custom_call_target="tpu_custom_call" | custom-call | tf_op jit(solution)/shard_map/pack/pallas_call | solution.py:186
  2.5 3.1 %collective-permute-start.3 = (bf16[912,128]{1,0:T(8,128)(2,1)}, bf16[912,128]{1,0:T(8,128)(2,1)S(1)}, u32[]{:S(2)}, u32[]{:S(2)}) collective-permute-start(bf16[912,128]{1,0:T(8,128)(2,1)} %pack.1.refs_0_), channel_id=1, source_target_pairs={{0,4},{1,5},{2,6},{3,7},{4,0},{5,1},{6,2},{7,3},{8,12},{9,13},{10,... | collective-permute-start | bytes 700424 | tf_op jit(solution)/shard_map/ppermute | solution.py:230
  5.5 1.5 %collective-permute-start.1 = (bf16[912,128]{1,0:T(8,128)(2,1)}, bf16[912,128]{1,0:T(8,128)(2,1)S(1)}, u32[]{:S(2)}, u32[]{:S(2)}) collective-permute-start(bf16[912,128]{1,0:T(8,128)(2,1)} %pack.1.refs_0_), channel_id=1, source_target_pairs={{0,2},{1,3},{2,0},{3,1},{4,6},{5,7},{6,4},{7,5},{8,10},{9,11},{10,... | collective-permute-start | bytes 700424 | tf_op jit(solution)/shard_map/ppermute | solution.py:230
  7.1 2.6 %collective-permute-start.6 = (bf16[912,128]{1,0:T(8,128)(2,1)}, bf16[912,128]{1,0:T(8,128)(2,1)S(1)}, u32[]{:S(2)}, u32[]{:S(2)}) collective-permute-start(bf16[912,128]{1,0:T(8,128)(2,1)} %pack.1.refs_0_), channel_id=1, source_target_pairs={{0,8},{1,9},{2,10},{3,11},{4,12},{5,13},{6,14},{7,15},{8,0},{9,1},... | collective-permute-start | bytes 700424 | tf_op jit(solution)/shard_map/ppermute | solution.py:230
  9.7 0.0 collective-permute-start
  9.7 5.4 %collective-permute-done.3.refs_1_.refs_4_ = bf16[912,128]{1,0:T(8,128)(2,1)S(1)} collective-permute-done((bf16[912,128]{1,0:T(8,128)(2,1)}, bf16[912,128]{1,0:T(8,128)(2,1)S(1)}, u32[]{:S(2)}, u32[]{:S(2)}) %collective-permute-start.3) | collective-permute-done | bytes 233504 | tf_op jit(solution)/shard_map/ppermute | solution.py:230
  15.1 2.7 %collective-permute-start.5 = (bf16[912,128]{1,0:T(8,128)(2,1)S(1)}, bf16[912,128]{1,0:T(8,128)(2,1)S(1)}, u32[]{:S(2)}, u32[]{:S(2)}) collective-permute-start(bf16[912,128]{1,0:T(8,128)(2,1)S(1)} %collective-permute-done.3.refs_1_.refs_4_), channel_id=1, source_target_pairs={{0,2},{1,3},{2,0},{3,1},{4,6},{5,7},{6,4},{7,5},{8,10},{9,11},{10,... | collective-permute-start | bytes 700424 | tf_op jit(solution)/shard_map/ppermute | solution.py:230
  17.8 0.0 collective-permute-start.4
  17.8 0.0 collective-permute-done.1.refs_0_.refs_2_
  17.8 0.5 %collective-permute-start.2 = (bf16[912,128]{1,0:T(8,128)(2,1)S(1)}, bf16[912,128]{1,0:T(8,128)(2,1)S(1)}, u32[]{:S(2)}, u32[]{:S(2)}) collective-permute-start(bf16[912,128]{1,0:T(8,128)(2,1)S(1)} %collective-permute-done.1.refs_0_.refs_2_), channel_id=1, source_target_pairs={{0,1},{1,0},{2,3},{3,2},{4,5},{5,4},{6,7},{7,6},{8,9},{9,8},{10,11... | collective-permute-start | bytes 700424 | tf_op jit(solution)/shard_map/ppermute | solution.py:230
  18.3 1.8 %collective-permute-done.6.refs_3_.refs_8_ = bf16[912,128]{1,0:T(8,128)(2,1)S(1)} collective-permute-done((bf16[912,128]{1,0:T(8,128)(2,1)}, bf16[912,128]{1,0:T(8,128)(2,1)S(1)}, u32[]{:S(2)}, u32[]{:S(2)}) %collective-permute-start.6) | collective-permute-done | bytes 233504 | tf_op jit(solution)/shard_map/ppermute | solution.py:230
  20.1 0.1 collective-permute-start.11
  20.2 0.0 copy-done.4
  20.2 0.0 copy-done.3
  20.2 0.0 copy-done.2
  20.2 0.6 %local.1 = (bf16[128,768]{1,0:T(8,128)(2,1)S(1)}, f32[1,768]{1,0:T(1,128)S(1)}) custom-call(s32[1,6]{1,0:T(1,128)S(1)} %copy-done.4, bf16[128,768]{1,0:T(8,128)(2,1)S(1)} %copy-done.2, f32[768]{0:T(1024)S(1)} %copy-done.3), custom_call_target="tpu_custom_call" | custom-call | tf_op jit(solution)/shard_map/local/pallas_call | solution.py:201
  20.8 0.0 collective-permute-done.4.refs_5_
  20.8 0.6 %collective-permute-start.9 = (bf16[912,128]{1,0:T(8,128)(2,1)S(1)}, bf16[912,128]{1,0:T(8,128)(2,1)S(1)}, u32[]{:S(2)}, u32[]{:S(2)}) collective-permute-start(bf16[912,128]{1,0:T(8,128)(2,1)S(1)} %collective-permute-done.6.refs_3_.refs_8_), channel_id=1, source_target_pairs={{0,2},{1,3},{2,0},{3,1},{4,6},{5,7},{6,4},{7,5},{8,10},{9,11},{10,... | collective-permute-start | bytes 700424 | tf_op jit(solution)/shard_map/ppermute | solution.py:230
  21.5 0.0 collective-permute-done.refs_1_
  21.5 2.0 %collective-permute-done.5.refs_4_.refs_6_ = bf16[912,128]{1,0:T(8,128)(2,1)S(1)} collective-permute-done((bf16[912,128]{1,0:T(8,128)(2,1)S(1)}, bf16[912,128]{1,0:T(8,128)(2,1)S(1)}, u32[]{:S(2)}, u32[]{:S(2)}) %collective-permute-start.5) | collective-permute-done | bytes 233504 | tf_op jit(solution)/shard_map/ppermute | solution.py:230
  23.5 0.0 collective-permute-done.2.refs_2_.refs_3_
  23.5 0.0 copy-start
  23.5 0.9 %copy-done = bf16[912,128]{1,0:T(8,128)(2,1)S(1)} copy-done((bf16[912,128]{1,0:T(8,128)(2,1)S(1)}, bf16[912,128]{1,0:T(8,128)(2,1)}, u32[]{:S(2)}) %copy-start) | copy-done | bytes 233496
  24.4 1.1 %early.2 = (bf16[6,128,128]{2,1,0:T(8,128)(2,1)S(1)}, f32[6,8,768]{2,1,0:T(8,128)S(1)}, bf16[6,768,128]{2,1,0:T(8,128)(2,1)S(1)}) custom-call(bf16[128,768]{1,0:T(8,128)(2,1)S(1)} %get-tuple-element.24.masked_ref, bf16[912,128]{1,0:T(8,128)(2,1)S(1)} %copy-done, bf16[912,128]{1,0:T(8,128)(2,1)S(1)} %collective-permute-done.refs_1_, ...), custom_call_target="tpu_custom_call" | custom-call | tf_op jit(solution)/shard_map/early/pallas_call | solution.py:216
  25.5 0.0 copy-start.1
  25.5 0.0 copy-start.5
  25.5 0.7 %collective-permute-done.11.refs_12_ = bf16[912,128]{1,0:T(8,128)(2,1)S(1)} collective-permute-done((bf16[912,128]{1,0:T(8,128)(2,1)S(1)}, bf16[912,128]{1,0:T(8,128)(2,1)S(1)}, u32[]{:S(2)}, u32[]{:S(2)}) %collective-permute-start.11) | collective-permute-done | bytes 233504 | tf_op jit(solution)/shard_map/ppermute | solution.py:253
  26.3 1.8 %collective-permute-start.13 = (bf16[912,128]{1,0:T(8,128)(2,1)S(1)}, bf16[912,128]{1,0:T(8,128)(2,1)S(1)}, u32[]{:S(2)}, u32[]{:S(2)}) collective-permute-start(bf16[912,128]{1,0:T(8,128)(2,1)S(1)} %collective-permute-done.11.refs_12_), channel_id=1, source_target_pairs={{0,2},{1,3},{2,0},{3,1},{4,6},{5,7},{6,4},{7,5},{8,10},{9,11},{10,... | collective-permute-start | bytes 700424 | tf_op jit(solution)/shard_map/ppermute | solution.py:230
  28.1 0.0 collective-permute-start.8
  28.1 0.5 %collective-permute-start.12 = (bf16[912,128]{1,0:T(8,128)(2,1)S(1)}, bf16[912,128]{1,0:T(8,128)(2,1)S(1)}, u32[]{:S(2)}, u32[]{:S(2)}) collective-permute-start(bf16[912,128]{1,0:T(8,128)(2,1)S(1)} %collective-permute-done.11.refs_12_), channel_id=1, source_target_pairs={{0,1},{1,0},{2,3},{3,2},{4,5},{5,4},{6,7},{7,6},{8,9},{9,8},{10,11... | collective-permute-start | bytes 700424 | tf_op jit(solution)/shard_map/ppermute | solution.py:230
  28.6 0.0 collective-permute-start.7
  28.6 0.6 %collective-permute-done.9.refs_10_ = bf16[912,128]{1,0:T(8,128)(2,1)S(1)} collective-permute-done((bf16[912,128]{1,0:T(8,128)(2,1)S(1)}, bf16[912,128]{1,0:T(8,128)(2,1)S(1)}, u32[]{:S(2)}, u32[]{:S(2)}) %collective-permute-start.9) | collective-permute-done | bytes 233504 | tf_op jit(solution)/shard_map/ppermute | solution.py:230
  29.2 0.0 collective-permute-start.10
  29.2 3.4 %collective-permute-done.13.refs_14_ = bf16[912,128]{1,0:T(8,128)(2,1)S(1)} collective-permute-done((bf16[912,128]{1,0:T(8,128)(2,1)S(1)}, bf16[912,128]{1,0:T(8,128)(2,1)S(1)}, u32[]{:S(2)}, u32[]{:S(2)}) %collective-permute-start.13) | collective-permute-done | bytes 233504 | tf_op jit(solution)/shard_map/ppermute | solution.py:230
  32.6 0.0 collective-permute-start.14
  32.6 0.0 collective-permute-done.8.refs_2_.refs_9_
  32.6 0.0 collective-permute-done.7.refs_5_.refs_7_
  32.6 0.0 collective-permute-done.12.refs_4_.refs_13_
  32.6 0.0 collective-permute-done.10.refs_3_.refs_11_
  32.6 1.1 %early.3 = (bf16[6,128,128]{2,1,0:T(8,128)(2,1)S(1)}, f32[6,8,768]{2,1,0:T(8,128)S(1)}, bf16[6,768,128]{2,1,0:T(8,128)(2,1)S(1)}) custom-call(bf16[128,768]{1,0:T(8,128)(2,1)S(1)} %get-tuple-element.24.masked_ref, bf16[912,128]{1,0:T(8,128)(2,1)S(1)} %collective-permute-done.1.refs_0_.refs_2_, bf16[912,128]{1,0:T(8,128)(2,1)S(1)} %collective-permute-done.3.refs_1_.refs_4_, ...), custom_call_target="tpu_custom_call" | custom-call | tf_op jit(solution)/shard_map/early/pallas_call | solution.py:216
  33.7 0.4 collective-permute-done.14.refs_15_
  34.1 0.0 copy-done.1
  34.1 0.0 copy-done.5
  34.1 3.0 %last.1 = (bf16[1,8,128,128]{3,2,1,0:T(8,128)(2,1)}, f32[8,128]{1,0:T(8,128)}) custom-call(s32[1,8]{1,0:T(1,128)S(1)} %copy-done.5, bf16[128,768]{1,0:T(8,128)(2,1)S(1)} %get-tuple-element.24.masked_ref, f32[1,768]{1,0:T(1,128)S(1)} %get-tuple-element.23.tau_ref, bf16[912,128]{1,0:T(8,128)(2,1)S(1)} %copy-done.1, ...), custom_call_target="tpu_custom_call" | custom-call | tf_op jit(solution)/shard_map/last/pallas_call | solution.py:272
  (1 shorter events, 0.0 us)
Async XLA Ops:
  0.6 19.6 %copy-start.4 = (s32[1,6]{1,0:T(1,128)S(1)}, s32[1,6]{1,0:T(1,128)}, u32[]{:S(2)}) copy-start(s32[1,6]{1,0:T(1,128)} %mask_ref) | copy-start | bytes 76
  0.6 19.6 %copy-start.3 = (f32[768]{0:T(1024)S(1)}, f32[768]{0:T(1024)}, u32[]{:S(2)}) copy-start(f32[768]{0:T(1024)} %tau_ref) | copy-start | bytes 9220
  0.7 19.6 %copy-start.2 = (bf16[128,768]{1,0:T(8,128)(2,1)S(1)}, bf16[128,768]{1,0:T(8,128)(2,1)}, u32[]{:S(2)}) copy-start(bf16[128,768]{1,0:T(8,128)(2,1)} %rows_ref) | copy-start | bytes 589828
  2.5 12.6 %collective-permute-start.3 = (bf16[912,128]{1,0:T(8,128)(2,1)}, bf16[912,128]{1,0:T(8,128)(2,1)S(1)}, u32[]{:S(2)}, u32[]{:S(2)}) collective-permute-start(bf16[912,128]{1,0:T(8,128)(2,1)} %pack.1.refs_0_), channel_id=1, source_target_pairs={{0,4},{1,5},{2,6},{3,7},{4,0},{5,1},{6,2},{7,3},{8,12},{9,13},{10,... | collective-permute-start | bytes 700424 | tf_op jit(solution)/shard_map/ppermute | solution.py:230
  5.5 12.2 %collective-permute-start.1 = (bf16[912,128]{1,0:T(8,128)(2,1)}, bf16[912,128]{1,0:T(8,128)(2,1)S(1)}, u32[]{:S(2)}, u32[]{:S(2)}) collective-permute-start(bf16[912,128]{1,0:T(8,128)(2,1)} %pack.1.refs_0_), channel_id=1, source_target_pairs={{0,2},{1,3},{2,0},{3,1},{4,6},{5,7},{6,4},{7,5},{8,10},{9,11},{10,... | collective-permute-start | bytes 700424 | tf_op jit(solution)/shard_map/ppermute | solution.py:230
  7.1 13.0 %collective-permute-start.6 = (bf16[912,128]{1,0:T(8,128)(2,1)}, bf16[912,128]{1,0:T(8,128)(2,1)S(1)}, u32[]{:S(2)}, u32[]{:S(2)}) collective-permute-start(bf16[912,128]{1,0:T(8,128)(2,1)} %pack.1.refs_0_), channel_id=1, source_target_pairs={{0,8},{1,9},{2,10},{3,11},{4,12},{5,13},{6,14},{7,15},{8,0},{9,1},... | collective-permute-start | bytes 700424 | tf_op jit(solution)/shard_map/ppermute | solution.py:230
  9.7 11.8 %collective-permute-start = (bf16[912,128]{1,0:T(8,128)(2,1)}, bf16[912,128]{1,0:T(8,128)(2,1)S(1)}, u32[]{:S(2)}, u32[]{:S(2)}) collective-permute-start(bf16[912,128]{1,0:T(8,128)(2,1)} %pack.1.refs_0_), channel_id=1, source_target_pairs={{0,1},{1,0},{2,3},{3,2},{4,5},{5,4},{6,7},{7,6},{8,9},{9,8},{10,11... | collective-permute-start | bytes 700424 | tf_op jit(solution)/shard_map/ppermute | solution.py:230
  15.1 8.4 %collective-permute-start.5 = (bf16[912,128]{1,0:T(8,128)(2,1)S(1)}, bf16[912,128]{1,0:T(8,128)(2,1)S(1)}, u32[]{:S(2)}, u32[]{:S(2)}) collective-permute-start(bf16[912,128]{1,0:T(8,128)(2,1)S(1)} %collective-permute-done.3.refs_1_.refs_4_), channel_id=1, source_target_pairs={{0,2},{1,3},{2,0},{3,1},{4,6},{5,7},{6,4},{7,5},{8,10},{9,11},{10,... | collective-permute-start | bytes 700424 | tf_op jit(solution)/shard_map/ppermute | solution.py:230
  17.8 3.1 %collective-permute-start.4 = (bf16[912,128]{1,0:T(8,128)(2,1)S(1)}, bf16[912,128]{1,0:T(8,128)(2,1)S(1)}, u32[]{:S(2)}, u32[]{:S(2)}) collective-permute-start(bf16[912,128]{1,0:T(8,128)(2,1)S(1)} %collective-permute-done.3.refs_1_.refs_4_), channel_id=1, source_target_pairs={{0,1},{1,0},{2,3},{3,2},{4,5},{5,4},{6,7},{7,6},{8,9},{9,8},{10,11... | collective-permute-start | bytes 700424 | tf_op jit(solution)/shard_map/ppermute | solution.py:230
  17.8 5.7 %collective-permute-start.2 = (bf16[912,128]{1,0:T(8,128)(2,1)S(1)}, bf16[912,128]{1,0:T(8,128)(2,1)S(1)}, u32[]{:S(2)}, u32[]{:S(2)}) collective-permute-start(bf16[912,128]{1,0:T(8,128)(2,1)S(1)} %collective-permute-done.1.refs_0_.refs_2_), channel_id=1, source_target_pairs={{0,1},{1,0},{2,3},{3,2},{4,5},{5,4},{6,7},{7,6},{8,9},{9,8},{10,11... | collective-permute-start | bytes 700424 | tf_op jit(solution)/shard_map/ppermute | solution.py:230
  20.1 6.1 %collective-permute-start.11 = (bf16[912,128]{1,0:T(8,128)(2,1)S(1)}, bf16[912,128]{1,0:T(8,128)(2,1)S(1)}, u32[]{:S(2)}, u32[]{:S(2)}) collective-permute-start(bf16[912,128]{1,0:T(8,128)(2,1)S(1)} %broadcast_select_fusion), channel_id=1, source_target_pairs={{0,8},{1,9},{2,10},{3,11},{4,0},{5,1},{6,2},{7,3},{8,12},{9,13},{1... | collective-permute-start | bytes 700424 | tf_op jit(solution)/shard_map/ppermute | solution.py:253
  20.8 8.4 %collective-permute-start.9 = (bf16[912,128]{1,0:T(8,128)(2,1)S(1)}, bf16[912,128]{1,0:T(8,128)(2,1)S(1)}, u32[]{:S(2)}, u32[]{:S(2)}) collective-permute-start(bf16[912,128]{1,0:T(8,128)(2,1)S(1)} %collective-permute-done.6.refs_3_.refs_8_), channel_id=1, source_target_pairs={{0,2},{1,3},{2,0},{3,1},{4,6},{5,7},{6,4},{7,5},{8,10},{9,11},{10,... | collective-permute-start | bytes 700424 | tf_op jit(solution)/shard_map/ppermute | solution.py:230
  23.5 0.9 %copy-start = (bf16[912,128]{1,0:T(8,128)(2,1)S(1)}, bf16[912,128]{1,0:T(8,128)(2,1)}, u32[]{:S(2)}) copy-start(bf16[912,128]{1,0:T(8,128)(2,1)} %pack.1.refs_0_) | copy-start | bytes 700420
  25.5 8.6 %copy-start.1 = (bf16[912,128]{1,0:T(8,128)(2,1)S(1)}, bf16[912,128]{1,0:T(8,128)(2,1)}, u32[]{:S(2)}) copy-start(bf16[912,128]{1,0:T(8,128)(2,1)} %pack.1.refs_0_) | copy-start | bytes 700420
  25.5 8.6 %copy-start.5 = (s32[1,8]{1,0:T(1,128)S(1)}, s32[1,8]{1,0:T(1,128)}, u32[]{:S(2)}) copy-start(s32[1,8]{1,0:T(1,128)} %dest_hbm.3) | copy-start | bytes 100
  26.3 6.3 %collective-permute-start.13 = (bf16[912,128]{1,0:T(8,128)(2,1)S(1)}, bf16[912,128]{1,0:T(8,128)(2,1)S(1)}, u32[]{:S(2)}, u32[]{:S(2)}) collective-permute-start(bf16[912,128]{1,0:T(8,128)(2,1)S(1)} %collective-permute-done.11.refs_12_), channel_id=1, source_target_pairs={{0,2},{1,3},{2,0},{3,1},{4,6},{5,7},{6,4},{7,5},{8,10},{9,11},{10,... | collective-permute-start | bytes 700424 | tf_op jit(solution)/shard_map/ppermute | solution.py:230
  28.1 4.5 %collective-permute-start.8 = (bf16[912,128]{1,0:T(8,128)(2,1)S(1)}, bf16[912,128]{1,0:T(8,128)(2,1)S(1)}, u32[]{:S(2)}, u32[]{:S(2)}) collective-permute-start(bf16[912,128]{1,0:T(8,128)(2,1)S(1)} %collective-permute-done.6.refs_3_.refs_8_), channel_id=1, source_target_pairs={{0,1},{1,0},{2,3},{3,2},{4,5},{5,4},{6,7},{7,6},{8,9},{9,8},{10,11... | collective-permute-start | bytes 700424 | tf_op jit(solution)/shard_map/ppermute | solution.py:230
  28.1 4.5 %collective-permute-start.12 = (bf16[912,128]{1,0:T(8,128)(2,1)S(1)}, bf16[912,128]{1,0:T(8,128)(2,1)S(1)}, u32[]{:S(2)}, u32[]{:S(2)}) collective-permute-start(bf16[912,128]{1,0:T(8,128)(2,1)S(1)} %collective-permute-done.11.refs_12_), channel_id=1, source_target_pairs={{0,1},{1,0},{2,3},{3,2},{4,5},{5,4},{6,7},{7,6},{8,9},{9,8},{10,11... | collective-permute-start | bytes 700424 | tf_op jit(solution)/shard_map/ppermute | solution.py:230
  28.6 4.0 %collective-permute-start.7 = (bf16[912,128]{1,0:T(8,128)(2,1)S(1)}, bf16[912,128]{1,0:T(8,128)(2,1)S(1)}, u32[]{:S(2)}, u32[]{:S(2)}) collective-permute-start(bf16[912,128]{1,0:T(8,128)(2,1)S(1)} %collective-permute-done.5.refs_4_.refs_6_), channel_id=1, source_target_pairs={{0,1},{1,0},{2,3},{3,2},{4,5},{5,4},{6,7},{7,6},{8,9},{9,8},{10,11... | collective-permute-start | bytes 700424 | tf_op jit(solution)/shard_map/ppermute | solution.py:230
  29.2 3.4 %collective-permute-start.10 = (bf16[912,128]{1,0:T(8,128)(2,1)S(1)}, bf16[912,128]{1,0:T(8,128)(2,1)S(1)}, u32[]{:S(2)}, u32[]{:S(2)}) collective-permute-start(bf16[912,128]{1,0:T(8,128)(2,1)S(1)} %collective-permute-done.9.refs_10_), channel_id=1, source_target_pairs={{0,1},{1,0},{2,3},{3,2},{4,5},{5,4},{6,7},{7,6},{8,9},{9,8},{10,11... | collective-permute-start | bytes 700424 | tf_op jit(solution)/shard_map/ppermute | solution.py:230
  32.6 1.5 %collective-permute-start.14 = (bf16[912,128]{1,0:T(8,128)(2,1)S(1)}, bf16[912,128]{1,0:T(8,128)(2,1)S(1)}, u32[]{:S(2)}, u32[]{:S(2)}) collective-permute-start(bf16[912,128]{1,0:T(8,128)(2,1)S(1)} %collective-permute-done.13.refs_14_), channel_id=1, source_target_pairs={{0,1},{1,0},{2,3},{3,2},{4,5},{5,4},{6,7},{7,6},{8,9},{9,8},{10,11... | collective-permute-start | bytes 700424 | tf_op jit(solution)/shard_map/ppermute | solution.py:230

commit v7 on v6

--- a/solution.py
+++ b/solution.py
@@ -41,18 +41,21 @@
     copies = [pltpu.make_async_copy(source, target, sems.at[k]) for k, (source, target) in enumerate(moves)]
     for copy in copies:
         copy.start()
-    for copy in copies:
+    rows_copy, tau_copy, mask_copy, dest_copy, metric_copy = copies
+    dest_copy.wait()
+    lane = lax.broadcasted_iota(jnp.int32, (LIST_ROWS, BLOCK), 1)
+    listed = jnp.zeros((LIST_ROWS, BLOCK), jnp.float32)
+    for j in range(dest_ref.shape[1]):
+        listed += (lane == dest_ref[0, j]).astype(jnp.float32)
+    piece_ref[depth + BLOCK :, :] = listed.astype(jnp.bfloat16)
+    for copy in (mask_copy, tau_copy, rows_copy):
         copy.wait()
     tau = tau_ref[...].reshape(1, depth)
     for t in range(tiles):
         cols = slice(t * BLOCK, (t + 1) * BLOCK)
         weight = tau[:, cols] * mask_ref[0, t].astype(jnp.float32)
         piece_ref[cols, :] = (rows_ref[:, cols].astype(jnp.float32) * weight).astype(jnp.bfloat16)
-    lane = lax.broadcasted_iota(jnp.int32, (LIST_ROWS, BLOCK), 1)
-    listed = jnp.zeros((LIST_ROWS, BLOCK), jnp.float32)
-    for j in range(dest_ref.shape[1]):
-        listed += (lane == dest_ref[0, j]).astype(jnp.float32)
-    piece_ref[depth + BLOCK :, :] = listed.astype(jnp.bfloat16)
+    metric_copy.wait()
 
 
 def local_kernel(mask_ref, rows_ref, tau_ref, masked_ref, row_ref):

time: 37.3 us -> 37.3 us (level)
  no operation moved by 1% of the time
where the time goes in v7:
time: 37.3 us; the launch traced here: 37.1 us
  waiting for transfers between devices  14.3 us (38%)
  starting transfers between devices  13.4 us (36%)
  Pallas kernels  7.58 us (20%)
  local copies, waits for them, and re-layouts  0.97 us (3%)
  between operations  0.78 us (2%)
    ppermute x14, waiting for transfers between devices, swap(): lax.ppermute(part, 'row', [(i, i ^ mask) for i in range(devices)])  13.6 us
    ppermute x14, starting transfers between devices, swap(): lax.ppermute(part, 'row', [(i, i ^ mask) for i in range(devices)])  13.4 us
    pallas_call x1, Pallas kernels, body(): pl.pallas_call(functools.partial(last_kernel, devices, groups, parts), ou...  3.03 us
    pallas_call x2, Pallas kernels, early(): pl.pallas_call(functools.partial(early_kernel, [len(piece) for piece in u...  2.2 us
    pallas_call x1, Pallas kernels, body(): pl.pallas_call(pack_kernel, out_shape=jax.ShapeDtypeStruct((piece_rows, B...  1.76 us
    unnamed x12, local copies, waits for them, and re-layouts  0.97 us
  transfers between devices with their start and end apart: 15, of which 7 were waited for; matrix products, arithmetic and copies ran while one was open for 0% of the time, Pallas kernels for 7%

profile of v7, /device:TPU:0, one launch (start us, length us, event | category | flops | bytes accessed | tf_op | source)
XLA Modules:
  0.0 37.1 jit_solution(1829071772460284702)
XLA Ops:
  0.6 0.0 copy-start.4
  0.6 0.0 copy-start.3
  0.7 0.0 copy-start.2
  0.7 1.8 %pack.1.refs_0_ = bf16[912,128]{1,0:T(8,128)(2,1)} custom-call(s32[1,6]{1,0:T(1,128)} %mask_ref, s32[1,8]{1,0:T(1,128)} %dest_hbm.3, bf16[128,768]{1,0:T(8,128)(2,1)} %rows_ref, f32[768]{0:T(1024)} %tau_ref, bf16[128,128]{1,0:T(8,128)(2,1)} %metric_hbm.1), custom_call_target="tpu_custom_call" | custom-call | tf_op jit(solution)/shard_map/pack/pallas_call | solution.py:189
  2.4 3.1 %collective-permute-start.3 = (bf16[912,128]{1,0:T(8,128)(2,1)}, bf16[912,128]{1,0:T(8,128)(2,1)S(1)}, u32[]{:S(2)}, u32[]{:S(2)}) collective-permute-start(bf16[912,128]{1,0:T(8,128)(2,1)} %pack.1.refs_0_), channel_id=1, source_target_pairs={{0,4},{1,5},{2,6},{3,7},{4,0},{5,1},{6,2},{7,3},{8,12},{9,13},{10,... | collective-permute-start | bytes 700424 | tf_op jit(solution)/shard_map/ppermute | solution.py:233
  5.5 1.5 %collective-permute-start.1 = (bf16[912,128]{1,0:T(8,128)(2,1)}, bf16[912,128]{1,0:T(8,128)(2,1)S(1)}, u32[]{:S(2)}, u32[]{:S(2)}) collective-permute-start(bf16[912,128]{1,0:T(8,128)(2,1)} %pack.1.refs_0_), channel_id=1, source_target_pairs={{0,2},{1,3},{2,0},{3,1},{4,6},{5,7},{6,4},{7,5},{8,10},{9,11},{10,... | collective-permute-start | bytes 700424 | tf_op jit(solution)/shard_map/ppermute | solution.py:233
  7.0 2.6 %collective-permute-start.6 = (bf16[912,128]{1,0:T(8,128)(2,1)}, bf16[912,128]{1,0:T(8,128)(2,1)S(1)}, u32[]{:S(2)}, u32[]{:S(2)}) collective-permute-start(bf16[912,128]{1,0:T(8,128)(2,1)} %pack.1.refs_0_), channel_id=1, source_target_pairs={{0,8},{1,9},{2,10},{3,11},{4,12},{5,13},{6,14},{7,15},{8,0},{9,1},... | collective-permute-start | bytes 700424 | tf_op jit(solution)/shard_map/ppermute | solution.py:233
  9.6 0.0 collective-permute-start
  9.6 5.4 %collective-permute-done.3.refs_1_.refs_4_ = bf16[912,128]{1,0:T(8,128)(2,1)S(1)} collective-permute-done((bf16[912,128]{1,0:T(8,128)(2,1)}, bf16[912,128]{1,0:T(8,128)(2,1)S(1)}, u32[]{:S(2)}, u32[]{:S(2)}) %collective-permute-start.3) | collective-permute-done | bytes 233504 | tf_op jit(solution)/shard_map/ppermute | solution.py:233
  15.1 2.7 %collective-permute-start.5 = (bf16[912,128]{1,0:T(8,128)(2,1)S(1)}, bf16[912,128]{1,0:T(8,128)(2,1)S(1)}, u32[]{:S(2)}, u32[]{:S(2)}) collective-permute-start(bf16[912,128]{1,0:T(8,128)(2,1)S(1)} %collective-permute-done.3.refs_1_.refs_4_), channel_id=1, source_target_pairs={{0,2},{1,3},{2,0},{3,1},{4,6},{5,7},{6,4},{7,5},{8,10},{9,11},{10,... | collective-permute-start | bytes 700424 | tf_op jit(solution)/shard_map/ppermute | solution.py:233
  17.8 0.0 collective-permute-start.4
  17.8 0.0 collective-permute-done.1.refs_0_.refs_2_
  17.8 0.5 %collective-permute-start.2 = (bf16[912,128]{1,0:T(8,128)(2,1)S(1)}, bf16[912,128]{1,0:T(8,128)(2,1)S(1)}, u32[]{:S(2)}, u32[]{:S(2)}) collective-permute-start(bf16[912,128]{1,0:T(8,128)(2,1)S(1)} %collective-permute-done.1.refs_0_.refs_2_), channel_id=1, source_target_pairs={{0,1},{1,0},{2,3},{3,2},{4,5},{5,4},{6,7},{7,6},{8,9},{9,8},{10,11... | collective-permute-start | bytes 700424 | tf_op jit(solution)/shard_map/ppermute | solution.py:233
  18.3 1.8 %collective-permute-done.6.refs_3_.refs_8_ = bf16[912,128]{1,0:T(8,128)(2,1)S(1)} collective-permute-done((bf16[912,128]{1,0:T(8,128)(2,1)}, bf16[912,128]{1,0:T(8,128)(2,1)S(1)}, u32[]{:S(2)}, u32[]{:S(2)}) %collective-permute-start.6) | collective-permute-done | bytes 233504 | tf_op jit(solution)/shard_map/ppermute | solution.py:233
  20.1 0.1 collective-permute-start.11
  20.2 0.0 copy-done.4
  20.2 0.0 copy-done.3
  20.2 0.0 copy-done.2
  20.2 0.6 %local.1 = (bf16[128,768]{1,0:T(8,128)(2,1)S(1)}, f32[1,768]{1,0:T(1,128)S(1)}) custom-call(s32[1,6]{1,0:T(1,128)S(1)} %copy-done.4, bf16[128,768]{1,0:T(8,128)(2,1)S(1)} %copy-done.2, f32[768]{0:T(1024)S(1)} %copy-done.3), custom_call_target="tpu_custom_call" | custom-call | tf_op jit(solution)/shard_map/local/pallas_call | solution.py:204
  20.8 0.0 collective-permute-done.4.refs_5_
  20.8 0.6 %collective-permute-start.9 = (bf16[912,128]{1,0:T(8,128)(2,1)S(1)}, bf16[912,128]{1,0:T(8,128)(2,1)S(1)}, u32[]{:S(2)}, u32[]{:S(2)}) collective-permute-start(bf16[912,128]{1,0:T(8,128)(2,1)S(1)} %collective-permute-done.6.refs_3_.refs_8_), channel_id=1, source_target_pairs={{0,2},{1,3},{2,0},{3,1},{4,6},{5,7},{6,4},{7,5},{8,10},{9,11},{10,... | collective-permute-start | bytes 700424 | tf_op jit(solution)/shard_map/ppermute | solution.py:233
  21.4 0.0 collective-permute-done.refs_1_
  21.4 2.0 %collective-permute-done.5.refs_4_.refs_6_ = bf16[912,128]{1,0:T(8,128)(2,1)S(1)} collective-permute-done((bf16[912,128]{1,0:T(8,128)(2,1)S(1)}, bf16[912,128]{1,0:T(8,128)(2,1)S(1)}, u32[]{:S(2)}, u32[]{:S(2)}) %collective-permute-start.5) | collective-permute-done | bytes 233504 | tf_op jit(solution)/shard_map/ppermute | solution.py:233
  23.4 0.0 collective-permute-done.2.refs_2_.refs_3_
  23.4 0.0 copy-start
  23.4 0.9 %copy-done = bf16[912,128]{1,0:T(8,128)(2,1)S(1)} copy-done((bf16[912,128]{1,0:T(8,128)(2,1)S(1)}, bf16[912,128]{1,0:T(8,128)(2,1)}, u32[]{:S(2)}) %copy-start) | copy-done | bytes 233496
  24.4 1.1 %early.2 = (bf16[6,128,128]{2,1,0:T(8,128)(2,1)S(1)}, f32[6,8,768]{2,1,0:T(8,128)S(1)}, bf16[6,768,128]{2,1,0:T(8,128)(2,1)S(1)}) custom-call(bf16[128,768]{1,0:T(8,128)(2,1)S(1)} %get-tuple-element.24.masked_ref, bf16[912,128]{1,0:T(8,128)(2,1)S(1)} %copy-done, bf16[912,128]{1,0:T(8,128)(2,1)S(1)} %collective-permute-done.refs_1_, ...), custom_call_target="tpu_custom_call" | custom-call | tf_op jit(solution)/shard_map/early/pallas_call | solution.py:219
  25.5 0.0 copy-start.1
  25.5 0.0 copy-start.5
  25.5 0.7 %collective-permute-done.11.refs_12_ = bf16[912,128]{1,0:T(8,128)(2,1)S(1)} collective-permute-done((bf16[912,128]{1,0:T(8,128)(2,1)S(1)}, bf16[912,128]{1,0:T(8,128)(2,1)S(1)}, u32[]{:S(2)}, u32[]{:S(2)}) %collective-permute-start.11) | collective-permute-done | bytes 233504 | tf_op jit(solution)/shard_map/ppermute | solution.py:256
  26.2 1.8 %collective-permute-start.13 = (bf16[912,128]{1,0:T(8,128)(2,1)S(1)}, bf16[912,128]{1,0:T(8,128)(2,1)S(1)}, u32[]{:S(2)}, u32[]{:S(2)}) collective-permute-start(bf16[912,128]{1,0:T(8,128)(2,1)S(1)} %collective-permute-done.11.refs_12_), channel_id=1, source_target_pairs={{0,2},{1,3},{2,0},{3,1},{4,6},{5,7},{6,4},{7,5},{8,10},{9,11},{10,... | collective-permute-start | bytes 700424 | tf_op jit(solution)/shard_map/ppermute | solution.py:233
  28.1 0.0 collective-permute-start.8
  28.1 0.5 %collective-permute-start.12 = (bf16[912,128]{1,0:T(8,128)(2,1)S(1)}, bf16[912,128]{1,0:T(8,128)(2,1)S(1)}, u32[]{:S(2)}, u32[]{:S(2)}) collective-permute-start(bf16[912,128]{1,0:T(8,128)(2,1)S(1)} %collective-permute-done.11.refs_12_), channel_id=1, source_target_pairs={{0,1},{1,0},{2,3},{3,2},{4,5},{5,4},{6,7},{7,6},{8,9},{9,8},{10,11... | collective-permute-start | bytes 700424 | tf_op jit(solution)/shard_map/ppermute | solution.py:233
  28.6 0.0 collective-permute-start.7
  28.6 0.6 %collective-permute-done.9.refs_10_ = bf16[912,128]{1,0:T(8,128)(2,1)S(1)} collective-permute-done((bf16[912,128]{1,0:T(8,128)(2,1)S(1)}, bf16[912,128]{1,0:T(8,128)(2,1)S(1)}, u32[]{:S(2)}, u32[]{:S(2)}) %collective-permute-start.9) | collective-permute-done | bytes 233504 | tf_op jit(solution)/shard_map/ppermute | solution.py:233
  29.2 0.0 collective-permute-start.10
  29.2 3.4 %collective-permute-done.13.refs_14_ = bf16[912,128]{1,0:T(8,128)(2,1)S(1)} collective-permute-done((bf16[912,128]{1,0:T(8,128)(2,1)S(1)}, bf16[912,128]{1,0:T(8,128)(2,1)S(1)}, u32[]{:S(2)}, u32[]{:S(2)}) %collective-permute-start.13) | collective-permute-done | bytes 233504 | tf_op jit(solution)/shard_map/ppermute | solution.py:233
  32.6 0.0 collective-permute-start.14
  32.6 0.0 collective-permute-done.8.refs_2_.refs_9_
  32.6 0.0 collective-permute-done.7.refs_5_.refs_7_
  32.6 0.0 collective-permute-done.12.refs_4_.refs_13_
  32.6 0.0 collective-permute-done.10.refs_3_.refs_11_
  32.6 1.1 %early.3 = (bf16[6,128,128]{2,1,0:T(8,128)(2,1)S(1)}, f32[6,8,768]{2,1,0:T(8,128)S(1)}, bf16[6,768,128]{2,1,0:T(8,128)(2,1)S(1)}) custom-call(bf16[128,768]{1,0:T(8,128)(2,1)S(1)} %get-tuple-element.24.masked_ref, bf16[912,128]{1,0:T(8,128)(2,1)S(1)} %collective-permute-done.1.refs_0_.refs_2_, bf16[912,128]{1,0:T(8,128)(2,1)S(1)} %collective-permute-done.3.refs_1_.refs_4_, ...), custom_call_target="tpu_custom_call" | custom-call | tf_op jit(solution)/shard_map/early/pallas_call | solution.py:219
  33.7 0.3 collective-permute-done.14.refs_15_
  34.1 0.0 copy-done.1
  34.1 0.0 copy-done.5
  34.1 3.0 %last.1 = (bf16[1,8,128,128]{3,2,1,0:T(8,128)(2,1)}, f32[8,128]{1,0:T(8,128)}) custom-call(s32[1,8]{1,0:T(1,128)S(1)} %copy-done.5, bf16[128,768]{1,0:T(8,128)(2,1)S(1)} %get-tuple-element.24.masked_ref, f32[1,768]{1,0:T(1,128)S(1)} %get-tuple-element.23.tau_ref, bf16[912,128]{1,0:T(8,128)(2,1)S(1)} %copy-done.1, ...), custom_call_target="tpu_custom_call" | custom-call | tf_op jit(solution)/shard_map/last/pallas_call | solution.py:275
  (1 shorter events, 0.0 us)
Async XLA Ops:
  0.6 19.6 %copy-start.4 = (s32[1,6]{1,0:T(1,128)S(1)}, s32[1,6]{1,0:T(1,128)}, u32[]{:S(2)}) copy-start(s32[1,6]{1,0:T(1,128)} %mask_ref) | copy-start | bytes 76
  0.6 19.6 %copy-start.3 = (f32[768]{0:T(1024)S(1)}, f32[768]{0:T(1024)}, u32[]{:S(2)}) copy-start(f32[768]{0:T(1024)} %tau_ref) | copy-start | bytes 9220
  0.7 19.6 %copy-start.2 = (bf16[128,768]{1,0:T(8,128)(2,1)S(1)}, bf16[128,768]{1,0:T(8,128)(2,1)}, u32[]{:S(2)}) copy-start(bf16[128,768]{1,0:T(8,128)(2,1)} %rows_ref) | copy-start | bytes 589828
  2.4 12.6 %collective-permute-start.3 = (bf16[912,128]{1,0:T(8,128)(2,1)}, bf16[912,128]{1,0:T(8,128)(2,1)S(1)}, u32[]{:S(2)}, u32[]{:S(2)}) collective-permute-start(bf16[912,128]{1,0:T(8,128)(2,1)} %pack.1.refs_0_), channel_id=1, source_target_pairs={{0,4},{1,5},{2,6},{3,7},{4,0},{5,1},{6,2},{7,3},{8,12},{9,13},{10,... | collective-permute-start | bytes 700424 | tf_op jit(solution)/shard_map/ppermute | solution.py:233
  5.5 12.2 %collective-permute-start.1 = (bf16[912,128]{1,0:T(8,128)(2,1)}, bf16[912,128]{1,0:T(8,128)(2,1)S(1)}, u32[]{:S(2)}, u32[]{:S(2)}) collective-permute-start(bf16[912,128]{1,0:T(8,128)(2,1)} %pack.1.refs_0_), channel_id=1, source_target_pairs={{0,2},{1,3},{2,0},{3,1},{4,6},{5,7},{6,4},{7,5},{8,10},{9,11},{10,... | collective-permute-start | bytes 700424 | tf_op jit(solution)/shard_map/ppermute | solution.py:233
  7.0 13.0 %collective-permute-start.6 = (bf16[912,128]{1,0:T(8,128)(2,1)}, bf16[912,128]{1,0:T(8,128)(2,1)S(1)}, u32[]{:S(2)}, u32[]{:S(2)}) collective-permute-start(bf16[912,128]{1,0:T(8,128)(2,1)} %pack.1.refs_0_), channel_id=1, source_target_pairs={{0,8},{1,9},{2,10},{3,11},{4,12},{5,13},{6,14},{7,15},{8,0},{9,1},... | collective-permute-start | bytes 700424 | tf_op jit(solution)/shard_map/ppermute | solution.py:233
  9.6 11.8 %collective-permute-start = (bf16[912,128]{1,0:T(8,128)(2,1)}, bf16[912,128]{1,0:T(8,128)(2,1)S(1)}, u32[]{:S(2)}, u32[]{:S(2)}) collective-permute-start(bf16[912,128]{1,0:T(8,128)(2,1)} %pack.1.refs_0_), channel_id=1, source_target_pairs={{0,1},{1,0},{2,3},{3,2},{4,5},{5,4},{6,7},{7,6},{8,9},{9,8},{10,11... | collective-permute-start | bytes 700424 | tf_op jit(solution)/shard_map/ppermute | solution.py:233
  15.1 8.4 %collective-permute-start.5 = (bf16[912,128]{1,0:T(8,128)(2,1)S(1)}, bf16[912,128]{1,0:T(8,128)(2,1)S(1)}, u32[]{:S(2)}, u32[]{:S(2)}) collective-permute-start(bf16[912,128]{1,0:T(8,128)(2,1)S(1)} %collective-permute-done.3.refs_1_.refs_4_), channel_id=1, source_target_pairs={{0,2},{1,3},{2,0},{3,1},{4,6},{5,7},{6,4},{7,5},{8,10},{9,11},{10,... | collective-permute-start | bytes 700424 | tf_op jit(solution)/shard_map/ppermute | solution.py:233
  17.8 3.1 %collective-permute-start.4 = (bf16[912,128]{1,0:T(8,128)(2,1)S(1)}, bf16[912,128]{1,0:T(8,128)(2,1)S(1)}, u32[]{:S(2)}, u32[]{:S(2)}) collective-permute-start(bf16[912,128]{1,0:T(8,128)(2,1)S(1)} %collective-permute-done.3.refs_1_.refs_4_), channel_id=1, source_target_pairs={{0,1},{1,0},{2,3},{3,2},{4,5},{5,4},{6,7},{7,6},{8,9},{9,8},{10,11... | collective-permute-start | bytes 700424 | tf_op jit(solution)/shard_map/ppermute | solution.py:233
  17.8 5.7 %collective-permute-start.2 = (bf16[912,128]{1,0:T(8,128)(2,1)S(1)}, bf16[912,128]{1,0:T(8,128)(2,1)S(1)}, u32[]{:S(2)}, u32[]{:S(2)}) collective-permute-start(bf16[912,128]{1,0:T(8,128)(2,1)S(1)} %collective-permute-done.1.refs_0_.refs_2_), channel_id=1, source_target_pairs={{0,1},{1,0},{2,3},{3,2},{4,5},{5,4},{6,7},{7,6},{8,9},{9,8},{10,11... | collective-permute-start | bytes 700424 | tf_op jit(solution)/shard_map/ppermute | solution.py:233
  20.1 6.1 %collective-permute-start.11 = (bf16[912,128]{1,0:T(8,128)(2,1)S(1)}, bf16[912,128]{1,0:T(8,128)(2,1)S(1)}, u32[]{:S(2)}, u32[]{:S(2)}) collective-permute-start(bf16[912,128]{1,0:T(8,128)(2,1)S(1)} %broadcast_select_fusion), channel_id=1, source_target_pairs={{0,8},{1,9},{2,10},{3,11},{4,0},{5,1},{6,2},{7,3},{8,12},{9,13},{1... | collective-permute-start | bytes 700424 | tf_op jit(solution)/shard_map/ppermute | solution.py:256
  20.8 8.4 %collective-permute-start.9 = (bf16[912,128]{1,0:T(8,128)(2,1)S(1)}, bf16[912,128]{1,0:T(8,128)(2,1)S(1)}, u32[]{:S(2)}, u32[]{:S(2)}) collective-permute-start(bf16[912,128]{1,0:T(8,128)(2,1)S(1)} %collective-permute-done.6.refs_3_.refs_8_), channel_id=1, source_target_pairs={{0,2},{1,3},{2,0},{3,1},{4,6},{5,7},{6,4},{7,5},{8,10},{9,11},{10,... | collective-permute-start | bytes 700424 | tf_op jit(solution)/shard_map/ppermute | solution.py:233
  23.4 0.9 %copy-start = (bf16[912,128]{1,0:T(8,128)(2,1)S(1)}, bf16[912,128]{1,0:T(8,128)(2,1)}, u32[]{:S(2)}) copy-start(bf16[912,128]{1,0:T(8,128)(2,1)} %pack.1.refs_0_) | copy-start | bytes 700420
  25.5 8.6 %copy-start.1 = (bf16[912,128]{1,0:T(8,128)(2,1)S(1)}, bf16[912,128]{1,0:T(8,128)(2,1)}, u32[]{:S(2)}) copy-start(bf16[912,128]{1,0:T(8,128)(2,1)} %pack.1.refs_0_) | copy-start | bytes 700420
  25.5 8.6 %copy-start.5 = (s32[1,8]{1,0:T(1,128)S(1)}, s32[1,8]{1,0:T(1,128)}, u32[]{:S(2)}) copy-start(s32[1,8]{1,0:T(1,128)} %dest_hbm.3) | copy-start | bytes 100
  26.2 6.3 %collective-permute-start.13 = (bf16[912,128]{1,0:T(8,128)(2,1)S(1)}, bf16[912,128]{1,0:T(8,128)(2,1)S(1)}, u32[]{:S(2)}, u32[]{:S(2)}) collective-permute-start(bf16[912,128]{1,0:T(8,128)(2,1)S(1)} %collective-permute-done.11.refs_12_), channel_id=1, source_target_pairs={{0,2},{1,3},{2,0},{3,1},{4,6},{5,7},{6,4},{7,5},{8,10},{9,11},{10,... | collective-permute-start | bytes 700424 | tf_op jit(solution)/shard_map/ppermute | solution.py:233
  28.1 4.5 %collective-permute-start.8 = (bf16[912,128]{1,0:T(8,128)(2,1)S(1)}, bf16[912,128]{1,0:T(8,128)(2,1)S(1)}, u32[]{:S(2)}, u32[]{:S(2)}) collective-permute-start(bf16[912,128]{1,0:T(8,128)(2,1)S(1)} %collective-permute-done.6.refs_3_.refs_8_), channel_id=1, source_target_pairs={{0,1},{1,0},{2,3},{3,2},{4,5},{5,4},{6,7},{7,6},{8,9},{9,8},{10,11... | collective-permute-start | bytes 700424 | tf_op jit(solution)/shard_map/ppermute | solution.py:233
  28.1 4.5 %collective-permute-start.12 = (bf16[912,128]{1,0:T(8,128)(2,1)S(1)}, bf16[912,128]{1,0:T(8,128)(2,1)S(1)}, u32[]{:S(2)}, u32[]{:S(2)}) collective-permute-start(bf16[912,128]{1,0:T(8,128)(2,1)S(1)} %collective-permute-done.11.refs_12_), channel_id=1, source_target_pairs={{0,1},{1,0},{2,3},{3,2},{4,5},{5,4},{6,7},{7,6},{8,9},{9,8},{10,11... | collective-permute-start | bytes 700424 | tf_op jit(solution)/shard_map/ppermute | solution.py:233
  28.6 4.0 %collective-permute-start.7 = (bf16[912,128]{1,0:T(8,128)(2,1)S(1)}, bf16[912,128]{1,0:T(8,128)(2,1)S(1)}, u32[]{:S(2)}, u32[]{:S(2)}) collective-permute-start(bf16[912,128]{1,0:T(8,128)(2,1)S(1)} %collective-permute-done.5.refs_4_.refs_6_), channel_id=1, source_target_pairs={{0,1},{1,0},{2,3},{3,2},{4,5},{5,4},{6,7},{7,6},{8,9},{9,8},{10,11... | collective-permute-start | bytes 700424 | tf_op jit(solution)/shard_map/ppermute | solution.py:233
  29.2 3.4 %collective-permute-start.10 = (bf16[912,128]{1,0:T(8,128)(2,1)S(1)}, bf16[912,128]{1,0:T(8,128)(2,1)S(1)}, u32[]{:S(2)}, u32[]{:S(2)}) collective-permute-start(bf16[912,128]{1,0:T(8,128)(2,1)S(1)} %collective-permute-done.9.refs_10_), channel_id=1, source_target_pairs={{0,1},{1,0},{2,3},{3,2},{4,5},{5,4},{6,7},{7,6},{8,9},{9,8},{10,11... | collective-permute-start | bytes 700424 | tf_op jit(solution)/shard_map/ppermute | solution.py:233
  32.6 1.5 %collective-permute-start.14 = (bf16[912,128]{1,0:T(8,128)(2,1)S(1)}, bf16[912,128]{1,0:T(8,128)(2,1)S(1)}, u32[]{:S(2)}, u32[]{:S(2)}) collective-permute-start(bf16[912,128]{1,0:T(8,128)(2,1)S(1)} %collective-permute-done.13.refs_14_), channel_id=1, source_target_pairs={{0,1},{1,0},{2,3},{3,2},{4,5},{5,4},{6,7},{7,6},{8,9},{9,8},{10,11... | collective-permute-start | bytes 700424 | tf_op jit(solution)/shard_map/ppermute | solution.py:233
